TPU v7x, 32 devices: a whole 2x2x4 slice. The times are simulated.
32 devices in a mesh: subj: 2 (over y), band: 4 (over z), lon: 2 (over x), pop: 2 (over core).
Axes of the slice: x: 2, y: 2, z: 4, core: 2. Of those that a mesh axis runs over, the one named last changes fastest.
Arguments:
- activity: float32 [16, 640, 1280], P(('subj', 'pop'), 'band', 'lon'), parts along dimension 0, may hold values from -6 to 6
- drive: bfloat16 [16, 640, 1280], P(('subj', 'pop'), 'band', 'lon'), parts along dimension 0, may hold values from -6 to 6
- basis: bfloat16 [1280, 320, 640], P(('subj', 'band', 'lon')), parts along dimension 0, may hold values from -6 to 6
- kernels: float32 [4, 640], replicated, may hold values from 0.2 to 2
- conn_block: int32 [8, 8], replicated, may hold values from 0 to 3
- coupling: float32 [16, 8], P('subj'), parts along dimension 0, may hold values from -2.5 to 2.5
- rate_params: float32 [8, 8], P('subj'), parts along dimension 0, may hold values from 0.5 to 2
Outputs:
- activity_next: float32 [16, 640, 1280], P(('subj', 'pop'), 'band', 'lon'), parts along dimension 0
There are 2 independent parts, one for each index of `subj`. A program takes and returns all parts, laid end to end along the dimension named above; an argument that names none is the same for every part. Nothing has to cross between parts.
All inputs are finite; a program needn't handle non-finite values.
Results may differ from a plain program's by a relative error of at most 0.0095.
Values may be sent and summed in bfloat16 or wider, within the bound.
No kernel may reach another device: no remote copies, remote signals or barrier semaphores. Data moves between devices by JAX's collectives and lax.ppermute only.
A program may use at most 192 MiB of HBM per device.

v0:
```python
import math

import jax
import jax.numpy as jnp
from jax import lax
from jax.sharding import PartitionSpec as P

NLAT = 640
NLON = 1280
DEG = 640
STEPS = 2


time_step = 0.5


def with_halo(shard, sides, width):
    for axis, dim in sides:
        size, length = (lax.axis_size(axis), shard.shape[dim])
        up = [(i, (i + 1) % size) for i in range(size - 1)]
        down = [(j, i) for i, j in up]
        last = lax.slice_in_dim(shard, length - width, length, axis=dim)
        leading = lax.slice_in_dim(shard, 0, width, axis=dim)
        before = lax.ppermute(last, axis, up)
        after = lax.ppermute(leading, axis, down)
        shard = jnp.concatenate([before, shard, after], axis=dim)
    return shard


def fourier_table():
    longitude = jnp.arange(NLON, dtype=jnp.int32)
    wavenumber = jnp.arange(DEG, dtype=jnp.int32)
    phase = longitude[:, None] * wavenumber[None, :] % NLON
    angle = phase.astype(jnp.float32) * (2.0 * math.pi / NLON)
    return jnp.stack([jnp.cos(angle), jnp.sin(angle)], axis=1).astype(jnp.bfloat16)


def lat_weights():
    row_index = jnp.arange(NLAT // 2, dtype=jnp.float32)
    colatitude = math.pi * (4.0 * row_index + 3.0) / (4.0 * NLAT + 2.0)
    return math.pi * jnp.sin(colatitude) / NLAT


def to_owners(fourier):
    return lax.all_to_all(fourier, ("band", "lon"), split_axis=2, concat_axis=3, tiled=True)


def to_latitudes(synthesis):
    return lax.all_to_all(synthesis, ("band", "lon"), split_axis=3, concat_axis=2, tiled=True)


def local(activity, drive, basis, kernels, conn_block, coupling, rate_params):
    pop_here = activity.shape[0]
    owned_count = basis.shape[0]
    half_lat = basis.shape[1]
    quarter = DEG // 2
    owner_index = lax.axis_index("band") * lax.axis_size("lon") + lax.axis_index("lon")
    pop_first = lax.axis_index("pop") * pop_here
    params = lax.dynamic_slice_in_dim(rate_params, pop_first, pop_here, 1)
    gain_row, thresh, decay_row, lateral = (params[0], params[1], params[2], params[3])
    cos_sin = fourier_table()
    weights = lat_weights()
    wavenumber = owner_index * owned_count + jnp.arange(owned_count, dtype=jnp.int32)
    degree = jnp.arange(DEG, dtype=jnp.int32)
    triangle = degree[None, :] >= wavenumber[:, None]
    slots = jnp.arange(2, dtype=jnp.int32)
    parity_pick = (slots[None, :] == (wavenumber % 2)[:, None])[None, None, :, :, None]
    every_wave = jnp.arange(DEG, dtype=jnp.int32)
    amplitude = jnp.where(every_wave == 0, 1.0, 2.0).astype(jnp.bfloat16)
    coup_own = lax.dynamic_slice_in_dim(coupling, pop_first, pop_here, 0)
    block_own = lax.dynamic_slice_in_dim(conn_block, pop_first, pop_here, 0)
    onehot = (block_own[..., None] == jnp.arange(kernels.shape[0], dtype=jnp.int32)).astype(
        jnp.float32
    )
    mixing = coup_own[..., None] * jnp.einsum(
        "ijb,bn->ijn", onehot, kernels, precision=lax.Precision.HIGHEST
    )
    basis_split = basis.reshape(owned_count, half_lat, quarter, 2)
    drive_f32 = drive.astype(jnp.float32)
    activity_now = activity
    for step_index in range(STEPS):
        rates = jax.nn.sigmoid(
            gain_row[:, None, None] * (activity_now - thresh[:, None, None])
        ).astype(jnp.bfloat16)
        lat_rows = lax.all_to_all(rates, "lon", split_axis=1, concat_axis=2, tiled=True)
        fourier = jnp.einsum(
            "ijk,kcm->icmj", lat_rows, cos_sin, preferred_element_type=jnp.float32
        ).astype(jnp.bfloat16)
        spectrum = to_owners(fourier)
        northern = spectrum[..., :half_lat].astype(jnp.float32)
        southern = jnp.flip(spectrum[..., half_lat:], axis=3).astype(jnp.float32)
        even_part = (weights * (northern + southern)).astype(jnp.bfloat16)
        odd_part = (weights * (northern - southern)).astype(jnp.bfloat16)
        operand = jnp.where(parity_pick, even_part[:, :, :, None, :], odd_part[:, :, :, None, :])
        coeffs = jnp.einsum(
            "icmsj,mjqs->icmqs", operand, basis_split, preferred_element_type=jnp.float32
        )
        coeffs = coeffs.reshape(pop_here, 2, owned_count, DEG)
        coeffs = jnp.where(triangle[None, None], coeffs, 0.0)
        gathered = lax.all_gather(coeffs.astype(jnp.bfloat16), "pop", axis=0, tiled=True).astype(
            coeffs.dtype
        )
        mixed_spec = jnp.sum(mixing[:, :, None, None, :] * gathered[None], axis=1).astype(
            jnp.bfloat16
        )
        degree_parts = jnp.einsum(
            "icmqs,mjqs->icmsj",
            mixed_spec.reshape(pop_here, 2, owned_count, quarter, 2),
            basis_split,
            preferred_element_type=jnp.float32,
        )
        same_parity = jnp.sum(jnp.where(parity_pick, degree_parts, 0.0), axis=3)
        other_parity = jnp.sum(jnp.where(parity_pick, 0.0, degree_parts), axis=3)
        synthesis = jnp.concatenate(
            [same_parity + other_parity, jnp.flip(same_parity - other_parity, axis=3)], axis=3
        ).astype(jnp.bfloat16)
        returned = to_latitudes(synthesis)
        scaled = returned * amplitude[None, None, :, None]
        synth_field = jnp.einsum(
            "icmj,kcm->ijk", scaled, cos_sin, preferred_element_type=jnp.float32
        ) * (1.0 / NLON)
        padded = with_halo(lat_rows, ((("band", "lon"), 1),), 1).astype(jnp.float32)
        rates_f32 = lat_rows.astype(jnp.float32)
        lateral_term = (
            jnp.roll(rates_f32, 1, axis=2)
            + jnp.roll(rates_f32, -1, axis=2)
            + padded[:, 2:, :]
            + padded[:, :-2, :]
            - 4.0 * rates_f32
        )
        coupled = synth_field + lateral[:, None, None] * lateral_term
        coupled_grid = lax.all_to_all(
            coupled.astype(jnp.bfloat16), "lon", split_axis=2, concat_axis=1, tiled=True
        ).astype(coupled.dtype)
        forcing = -decay_row[:, None, None] * activity_now + coupled_grid + drive_f32
        activity_now = activity_now + time_step * forcing
    return activity_now


def solution(mesh):
    in_specs = (
        P(("subj", "pop"), "band", "lon"),
        P(("subj", "pop"), "band", "lon"),
        P(("subj", "band", "lon"), None, None),
        P(),
        P(),
        P("subj", None),
        P("subj", None),
    )
    out_specs = P(("subj", "pop"), "band", "lon")
    return jax.shard_map(local, mesh=mesh, in_specs=in_specs, out_specs=out_specs, check_vma=False)
```

profile of v0, /device:TPU:0, one launch (start us, length us, event | category | flops | bytes accessed | tf_op | source)
XLA Modules:
  0.0 531.6 jit_solution(762499637347597196)
XLA Ops:
  8.4 2.0 divide_convert_fusion.1
  10.4 1.3 copy.134
  11.7 4.2 all-to-all-start
  15.9 14.5 %sine_convert_fusion = (bf16[1280,1,640]{2,0,1:T(8,128)(2,1)S(1)}, bf16[1280,1,640]{2,0,1:T(8,128)(2,1)}) fusion(), kind=kLoop, calls=%fused_computation.14 | loop fusion | flops 9011200 | bytes 3276800 | tf_op jit(solution)/shard_map/convert.13
  31.8 3.7 fusion.54
  35.5 3.4 copy.136
  38.9 7.1 %all-to-all-start.1 = ((bf16[4,2,640,80]{3,0,1,2:T(4,128)(2,1)}), bf16[4,2,640,80]{3,0,1,2:T(4,128)(2,1)S(1)}, u32[]{:S(2)}, u32[]{:S(2)}) async-start(bf16[4,2,640,80]{3,0,1,2:T(4,128)(2,1)} %copy.136), calls=%async_computation.1 | async-start | bytes 2621440 | tf_op jit(solution)/shard_map/all_to_all | solution.py:45
  46.3 48.1 %copy.140 = bf16[80,320,640]{1,0,2:T(8,128)(2,1)} copy(bf16[80,320,640]{2,1,0:T(8,128)(2,1)} %param.9) | data formatting | bytes 65536000 | tf_op args[2]
  94.5 53.5 %copy.170 = bf16[80,320,320,2,1]{2,1,4,3,0:T(8,128)(2,1)} copy(bf16[80,320,320,2,1]{1,0,3,2,4:T(8,128)(2,1)} %bitcast.160) | data formatting | bytes 65536000 | tf_op jit(solution)/shard_map/reshape | solution.py:78
  148.2 1.9 copy.197
  150.1 2.2 all_to_all.99
  152.5 2.2 reverse
  155.7 16.3 %convolution_bitcast_fusion.1 = bf16[4,2,80,320,2]{3,0,1,4,2:T(4,128)(2,1)} fusion(bf16[80,320,320,2,1]{2,1,4,3,0:T(8,128)(2,1)} %copy.170, pred[80,2]{1,0:T(8,128)(4,1)S(1)} %iota_compare_fusion.1, bf16[4,2,80,320]{3,0,1,2:T(4,128)(2,1)S(1)} %copy.139, bf16[4,2,80,320]{3,0,1,2:T(4,128)(2,1)S(1)} %copy.138), kind=kOutput, calls=%fused_computation.55 | convolution fusion | flops 262553600 | bytes 34406560 | tf_op jit(solution)/shard_map/icmsj,mjqs->icmqs/dot_general | solution.py:95
  172.0 4.1 copy.142
  179.2 10.1 %all-gather.3.cloned.1.call-done = bf16[8,2,80,640]{3,2,1,0:T(8,128)(2,1)} async-done(((bf16[4,2,80,640]{3,2,1,0:T(8,128)(2,1)}), bf16[8,2,80,640]{3,2,1,0:T(8,128)(2,1)}) %all-gather.3.cloned.1.call-update) | async-done | bytes 1638416 | tf_op jit(solution)/shard_map/all_gather | solution.py:100
  189.3 1.7 convert_element_type.151
  192.7 2.9 copy.145
  195.6 18.7 %select_reduce_fusion.2 = (f32[80,4,2,320]{3,1,2,0:T(4,128)S(1)}, f32[80,4,2,320]{3,1,2,0:T(4,128)S(1)}) fusion(pred[80,2]{1,0:T(8,128)(4,1)S(1)} %iota_compare_fusion.1, bf16[4,2,80,320,2]{3,0,1,4,2:T(4,128)(2,1)} %copy.145, bf16[80,320,320,2,1]{2,1,4,3,0:T(8,128)(2,1)} %copy.170), kind=kOutput, calls=%fused_computation.32 | convolution fusion | flops 263372800 | bytes 35225760 | tf_op jit(solution)/shard_map/icmqs,mjqs->icmsj/dot_general | solution.py:106
  215.7 3.5 reverse.1
  220.2 2.9 copy.147
  223.1 5.8 %all-to-all-start.2 = ((bf16[4,2,80,640]{2,1,0,3:T(2,128)(2,1)}), bf16[4,2,80,640]{2,1,0,3:T(2,128)(2,1)S(1)}, u32[]{:S(2)}, u32[]{:S(2)}) async-start(bf16[4,2,80,640]{2,1,0,3:T(2,128)(2,1)} %copy.147), calls=%async_computation.2 | async-start | bytes 2621440 | tf_op jit(solution)/shard_map/all_to_all | solution.py:49
  229.0 3.9 collective-permute-start
  234.2 2.1 fusion.85
  237.0 3.2 collective-permute-done
  240.6 1.4 maximum_convert_fusion
  242.0 18.9 %all-to-all-done.2 = bf16[4,2,80,640]{2,1,0,3:T(2,128)(2,1)S(1)} async-done(((bf16[4,2,80,640]{2,1,0,3:T(2,128)(2,1)}), bf16[4,2,80,640]{2,1,0,3:T(2,128)(2,1)S(1)}, u32[]{:S(2)}, u32[]{:S(2)}) %all-to-all-start.2) | async-done | bytes 819232 | tf_op jit(solution)/shard_map/all_to_all | solution.py:49
  262.9 5.6 %fusion.31 = bf16[4,80,1280]{2,1,0:T(8,128)(2,1)S(1)} fusion(f32[4,82,1280]{2,1,0:T(8,128)} %maximum_convert_fusion, f32[4,80,1279]{2,1,0:T(8,128)} %get-tuple-element.20, f32[4,80,1]{2,1,0:T(8,128)} %get-tuple-element.22, f32[4,80,1]{2,1,0:T(8,128)} %get-tuple-element.21, f32[4,80,1279]{2,1,0:T(8,128)} %get-tuple-element.19, f32[4]{0:T(128)S(1)} %copy-done.16, ...), kind=kOutput, calls=%fused_computation.26 | convolution fusion | flops 1055539200 | bytes 12289296 | tf_op jit(solution)/shard_map/icmj,kcm->ijk/dot_general | solution.py:119
  268.5 1.6 copy.150
  270.1 19.1 %all_to_all.126 = bf16[4,80,1280]{1,0,2:T(4,128)(2,1)} all-to-all(bf16[4,80,1280]{1,0,2:T(4,128)(2,1)S(1)} %copy.150), channel_id=1, replica_groups=mesh['subj'=2,'band'=4,'lon'=2,'pop'=2] {'lon'}, dimensions={2} | all-to-all | bytes 1638400 | tf_op jit(solution)/shard_map/all_to_all | solution.py:132
  289.2 3.0 copy.151
  292.2 2.5 divide_convert_fusion
  295.1 12.2 %all_to_all.127 = bf16[4,160,640]{2,0,1:T(4,128)(2,1)S(1)} all-to-all(bf16[4,160,640]{2,0,1:T(4,128)(2,1)S(1)} %copy.152), channel_id=1, replica_groups=mesh['subj'=2,'band'=4,'lon'=2,'pop'=2] {'lon'}, dimensions={1} | all-to-all | bytes 1638400 | tf_op jit(solution)/shard_map/all_to_all | solution.py:85
  308.7 4.1 fusion.51
  312.8 3.4 copy.154
  316.2 36.4 %all_to_all.128 = bf16[4,2,640,80]{3,0,1,2:T(4,128)(2,1)S(1)} all-to-all(bf16[4,2,640,80]{3,0,1,2:T(4,128)(2,1)} %copy.154), channel_id=1, replica_groups=mesh['subj'=2,'band'=4,'lon'=2,'pop'=2] {'band','lon'}, dimensions={2} | all-to-all | bytes 1638400 | tf_op jit(solution)/shard_map/all_to_all | solution.py:45
  352.6 1.9 copy.196
  354.5 2.2 all_to_all.112
  357.7 12.1 %reverse.2 = bf16[4,2,80,384]{3,2,1,0:T(8,128)(2,1)} reverse(bf16[4,2,80,384]{3,2,1,0:T(8,128)(2,1)} %bitcast.183), dimensions={3} | reverse | bytes 983040
  369.8 1.4 fusion.62
  371.8 16.3 %convolution_bitcast_fusion = bf16[4,2,80,320,2]{3,0,1,4,2:T(4,128)(2,1)} fusion(bf16[80,320,320,2,1]{2,1,4,3,0:T(8,128)(2,1)} %copy.170, pred[80,2]{1,0:T(8,128)(4,1)S(1)} %iota_compare_fusion.1, bf16[4,2,80,320]{3,0,1,2:T(4,128)(2,1)S(1)} %copy.157, bf16[4,2,80,320]{3,0,1,2:T(4,128)(2,1)S(1)} %copy.156), kind=kOutput, calls=%fused_computation.54 | convolution fusion | flops 262553600 | bytes 34406560 | tf_op jit(solution)/shard_map/icmsj,mjqs->icmqs/dot_general | solution.py:95
  388.2 5.1 copy.159
  393.2 1.6 copy.160
  396.5 8.6 %all-gather.5.cloned.1.call-done = bf16[8,2,80,640]{3,2,1,0:T(8,128)(2,1)} async-done(((bf16[4,2,80,640]{3,2,1,0:T(8,128)(2,1)}), bf16[8,2,80,640]{3,2,1,0:T(8,128)(2,1)}) %all-gather.5.cloned.1.call-update) | async-done | bytes 1638416 | tf_op jit(solution)/shard_map/all_gather | solution.py:100
  405.1 1.7 convert_element_type.171
  407.7 1.4 copy.161
  409.1 4.9 copy.162
  414.0 19.4 %select_reduce_fusion = (f32[80,4,2,320]{3,1,2,0:T(4,128)S(1)}, f32[80,4,2,320]{3,1,2,0:T(4,128)}) fusion(pred[80,2]{1,0:T(8,128)(4,1)S(1)} %iota_compare_fusion.1, bf16[4,2,80,320,2]{3,0,1,4,2:T(4,128)(2,1)} %copy.162, bf16[80,320,320,2,1]{2,1,4,3,0:T(8,128)(2,1)} %copy.170), kind=kOutput, calls=%fused_computation.30 | convolution fusion | flops 263372800 | bytes 35225760 | tf_op jit(solution)/shard_map/icmqs,mjqs->icmsj/dot_general | solution.py:106
  433.4 2.4 fusion.72
  436.9 3.5 reverse.3
  440.8 1.6 pad_maximum_fusion.2
  442.5 2.9 copy.164
  445.4 5.8 %all-to-all-start.6 = ((bf16[4,2,80,640]{2,1,0,3:T(2,128)(2,1)}), bf16[4,2,80,640]{2,1,0,3:T(2,128)(2,1)}, u32[]{:S(2)}, u32[]{:S(2)}) async-start(bf16[4,2,80,640]{2,1,0,3:T(2,128)(2,1)} %copy.164), calls=%async_computation.6 | async-start | bytes 2621440 | tf_op jit(solution)/shard_map/all_to_all | solution.py:49
  451.2 3.9 collective-permute-start.2
  456.4 2.1 fusion.82
  459.3 3.3 collective-permute-done.2
  462.8 1.5 maximum_convert_fusion.1
  464.3 19.0 %all-to-all-done.6 = bf16[4,2,80,640]{2,1,0,3:T(2,128)(2,1)} async-done(((bf16[4,2,80,640]{2,1,0,3:T(2,128)(2,1)}), bf16[4,2,80,640]{2,1,0,3:T(2,128)(2,1)}, u32[]{:S(2)}, u32[]{:S(2)}) %all-to-all-start.6) | async-done | bytes 819232 | tf_op jit(solution)/shard_map/all_to_all | solution.py:49
  483.3 3.3 copy.194
  486.6 2.2 all_to_all.116
  488.8 6.5 %fusion.34 = bf16[4,80,1280]{2,1,0:T(8,128)(2,1)} fusion(f32[4,82,1280]{2,1,0:T(8,128)} %maximum_convert_fusion.1, f32[4,80,1279]{2,1,0:T(8,128)} %get-tuple-element.14, f32[4,80,1]{2,1,0:T(8,128)} %get-tuple-element.16, f32[4,80,1]{2,1,0:T(8,128)S(1)} %get-tuple-element.15, f32[4,80,1279]{2,1,0:T(8,128)} %get-tuple-element.13, ...), kind=kOutput, calls=%fused_computation.27 | convolution fusion | flops 1055539200 | bytes 12289296 | tf_op jit(solution)/shard_map/icmj,kcm->ijk/dot_general | solution.py:119
  495.3 2.8 copy.167
  498.1 19.1 %all_to_all.129 = bf16[4,80,1280]{1,0,2:T(4,128)(2,1)} all-to-all(bf16[4,80,1280]{1,0,2:T(4,128)(2,1)S(1)} %copy.167), channel_id=1, replica_groups=mesh['subj'=2,'band'=4,'lon'=2,'pop'=2] {'lon'}, dimensions={2} | all-to-all | bytes 1638400 | tf_op jit(solution)/shard_map/all_to_all | solution.py:132
  517.1 3.8 copy.168
  520.9 3.6 fusion.40
  (90 shorter events, 26.4 us)
Async XLA Ops:
  6.5 171.9 %copy-start = (f32[4,640]{1,0:T(4,128)S(1)}, f32[4,640]{1,0:T(4,128)}, u32[]{:S(2)}) copy-start(f32[4,640]{1,0:T(4,128)} %param.10) | copy-start | bytes 30724
  7.8 0.6 copy-start.9
  11.7 18.8 %all-to-all-start = ((bf16[4,160,640]{2,0,1:T(4,128)(2,1)}), bf16[4,160,640]{2,0,1:T(4,128)(2,1)S(1)}, u32[]{:S(2)}, u32[]{:S(2)}) async-start(bf16[4,160,640]{2,0,1:T(4,128)(2,1)} %copy.134), calls=%async_computation | async-start | bytes 1638400 | tf_op jit(solution)/shard_map/all_to_all | solution.py:85
  30.5 1.4 copy-start.6
  38.9 109.3 %all-to-all-start.1 = ((bf16[4,2,640,80]{3,0,1,2:T(4,128)(2,1)}), bf16[4,2,640,80]{3,0,1,2:T(4,128)(2,1)S(1)}, u32[]{:S(2)}, u32[]{:S(2)}) async-start(bf16[4,2,640,80]{3,0,1,2:T(4,128)(2,1)} %copy.136), calls=%async_computation.1 | async-start | bytes 2621440 | tf_op jit(solution)/shard_map/all_to_all | solution.py:45
  46.0 143.3 %all-gather.3.cloned.1.call-start = ((), (), s32[]{:S(2)}) async-start(), calls=%async_computation.8 | async-start | bytes 2457600 | tf_op jit(solution)/shard_map/all_gather | solution.py:100
  148.2 28.5 %copy-start.7 = (pred[80,640]{1,0:T(8,128)(4,1)}, pred[80,640]{1,0:T(8,128)(4,1)S(1)}, u32[]{:S(2)}) copy-start(pred[80,640]{1,0:T(8,128)(4,1)S(1)} %iota_compare_fusion) | copy-start | bytes 153604
  176.7 1.7 copy-start.14
  176.8 1.7 copy-start.15
  223.1 37.8 %all-to-all-start.2 = ((bf16[4,2,80,640]{2,1,0,3:T(2,128)(2,1)}), bf16[4,2,80,640]{2,1,0,3:T(2,128)(2,1)S(1)}, u32[]{:S(2)}, u32[]{:S(2)}) async-start(bf16[4,2,80,640]{2,1,0,3:T(2,128)(2,1)} %copy.147), calls=%async_computation.2 | async-start | bytes 2621440 | tf_op jit(solution)/shard_map/all_to_all | solution.py:49
  228.9 176.2 %all-gather.5.cloned.1.call-start = ((), (), s32[]{:S(2)}) async-start(), calls=%async_computation.9 | async-start | bytes 2457600 | tf_op jit(solution)/shard_map/all_gather | solution.py:100
  229.0 11.3 %collective-permute-start = (bf16[4,1,1280]{2,1,0:T(2,128)(2,1)S(1)}, bf16[4,1,1280]{2,1,0:T(2,128)(2,1)S(1)}, u32[]{:S(2)}, u32[]{:S(2)}) collective-permute-start(bf16[4,1,1280]{2,1,0:T(2,128)(2,1)S(1)} %get-tuple-element.23), channel_id=1, source_target_pairs={{0,2},{2,4},{4,6},{6,8},{8,10},{10,12},{12,14},{1,3},{3,5},{5,7},{... | collective-permute-start | bytes 30728 | tf_op jit(solution)/shard_map/ppermute | solution.py:24
  232.9 7.7 %collective-permute-start.1 = (bf16[4,1,1280]{2,1,0:T(2,128)(2,1)S(1)}, bf16[4,1,1280]{2,1,0:T(2,128)(2,1)S(1)}, u32[]{:S(2)}, u32[]{:S(2)}) collective-permute-start(bf16[4,1,1280]{2,1,0:T(2,128)(2,1)S(1)} %get-tuple-element.24), channel_id=1, source_target_pairs={{2,0},{4,2},{6,4},{8,6},{10,8},{12,10},{14,12},{3,1},{5,3},{7,5},{... | collective-permute-start | bytes 30728 | tf_op jit(solution)/shard_map/ppermute | solution.py:25
  261.8 1.0 copy-start.13
  261.8 1.0 copy-start.16
  289.2 3.0 copy-start.2
  289.2 3.0 copy-start.10
  289.2 3.0 copy-start.11
  292.1 2.6 copy-start.3
  393.2 1.6 copy-start.8
  433.4 2.4 copy-start.5
  445.4 37.9 %all-to-all-start.6 = ((bf16[4,2,80,640]{2,1,0,3:T(2,128)(2,1)}), bf16[4,2,80,640]{2,1,0,3:T(2,128)(2,1)}, u32[]{:S(2)}, u32[]{:S(2)}) async-start(bf16[4,2,80,640]{2,1,0,3:T(2,128)(2,1)} %copy.164), calls=%async_computation.6 | async-start | bytes 2621440 | tf_op jit(solution)/shard_map/all_to_all | solution.py:49
  451.2 11.3 %collective-permute-start.2 = (bf16[4,1,1280]{2,1,0:T(2,128)(2,1)S(1)}, bf16[4,1,1280]{2,1,0:T(2,128)(2,1)S(1)}, u32[]{:S(2)}, u32[]{:S(2)}) collective-permute-start(bf16[4,1,1280]{2,1,0:T(2,128)(2,1)S(1)} %get-tuple-element.17), channel_id=1, source_target_pairs={{0,2},{2,4},{4,6},{6,8},{8,10},{10,12},{12,14},{1,3},{3,5},{5,7},{... | collective-permute-start | bytes 30728 | tf_op jit(solution)/shard_map/ppermute | solution.py:24
  455.1 7.7 %collective-permute-start.3 = (bf16[4,1,1280]{2,1,0:T(2,128)(2,1)S(1)}, bf16[4,1,1280]{2,1,0:T(2,128)(2,1)S(1)}, u32[]{:S(2)}, u32[]{:S(2)}) collective-permute-start(bf16[4,1,1280]{2,1,0:T(2,128)(2,1)S(1)} %get-tuple-element.18), channel_id=1, source_target_pairs={{2,0},{4,2},{6,4},{8,6},{10,8},{12,10},{14,12},{3,1},{5,3},{7,5},{... | collective-permute-start | bytes 30728 | tf_op jit(solution)/shard_map/ppermute | solution.py:25
  486.6 2.2 copy-start.17
  517.1 3.8 copy-start.4
  517.1 3.8 copy-start.12
  520.9 3.6 copy-start.1
Sparse Core Ops, SparseCore 0:
  178.0 11.2 all-gather.2
  396.1 8.9 all-gather.4
where the time goes:
time: 541 us; the launch traced here: 532 us
  local copies, waits for them, and re-layouts  199 us (37%)
  matrix products  90.8 us (17%)
  blocking collectives  86.8 us (16%)
  waiting for transfers between devices  63.8 us (12%)
  other arithmetic  43.2 us (8%)
  starting transfers between devices  33.6 us (6%)
  between operations  14.2 us (3%)
    unnamed x43, local copies, waits for them, and re-layouts  70.9 us
    reshape x1, local copies, waits for them, and re-layouts, local(): basis_split = basis.reshape(owned_count, half_lat, quarter, 2)  53.5 us
    all_to_all x2, blocking collectives, local(): lax.all_to_all(coupled.astype(jnp.bfloat16), 'lon', split_axis=2, concat_...  38.2 us
    dot_general x2, matrix products, local(): jnp.einsum('icmqs,mjqs->icmsj', mixed_spec.reshape(pop_here, 2, owned_cou...  38.1 us
    all_to_all x2, waiting for transfers between devices, to_latitudes(): lax.all_to_all(synthesis, ('band', 'lon'), split_axis=3, concat_axis=2, t...  38 us
    all_to_all x1, blocking collectives, to_owners(): lax.all_to_all(fourier, ('band', 'lon'), split_axis=2, concat_axis=3, til...  36.4 us
    dot_general x2, matrix products, local(): jnp.einsum('icmsj,mjqs->icmqs', operand, basis_split, preferred_element_t...  32.6 us
    all_gather x2, waiting for transfers between devices, local(): lax.all_gather(coeffs.astype(jnp.bfloat16), 'pop', axis=0, tiled=True)  18.6 us
  transfers between devices with their start and end apart: 10, of which 8 were waited for; matrix products, arithmetic and copies ran while one was open for 24% of the time, Pallas kernels for 0%

commit v1 on v0

--- a/solution.py
+++ b/solution.py
@@ -1,17 +1,411 @@
+import functools
 import math
 
 import jax
 import jax.numpy as jnp
+import ml_dtypes
+import numpy as np
 from jax import lax
+from jax.experimental import pallas as pl
+from jax.experimental.pallas import tpu as pltpu
 from jax.sharding import PartitionSpec as P
 
-NLAT = 640
-NLON = 1280
-DEG = 640
 STEPS = 2
-
-
 time_step = 0.5
+F32 = jnp.float32
+BF16 = jnp.bfloat16
+OWNERS = ("band", "lon")
+EVERYONE = ("band", "lon", "pop")
+MIB = 1 << 20
+
+
+def call(body, out_shape, vmem_mib, flops=0, nbytes=0, **kw):
+    return pl.pallas_call(
+        body,
+        out_shape=out_shape,
+        compiler_params=pltpu.CompilerParams(vmem_limit_bytes=vmem_mib * MIB),
+        cost_estimate=pl.CostEstimate(flops=flops, bytes_accessed=nbytes, transcendentals=0),
+        **kw,
+    )
+
+
+def whole():
+    return pl.BlockSpec(memory_space=pltpu.VMEM)
+
+
+def scalars():
+    return pl.BlockSpec(memory_space=pltpu.SMEM)
+
+
+def shape(*dims, dtype=BF16):
+    return jax.ShapeDtypeStruct(dims, dtype)
+
+
+def nt_dot(a, b):
+    return lax.dot_general(a, b, (((1,), (1,)), ((), ())), preferred_element_type=F32)
+
+
+def fourier_table(nlon, deg):
+    phase = np.arange(deg, dtype=np.int64)[:, None] * np.arange(nlon, dtype=np.int64)[None, :] % nlon
+    angle = phase.astype(np.float32) * np.float32(2.0 * math.pi / nlon)
+    return np.stack([np.cos(angle), np.sin(angle)]).astype(ml_dtypes.bfloat16)
+
+
+def lat_weights(nlat):
+    row_index = np.arange(nlat // 2, dtype=np.float32)
+    colatitude = np.float32(math.pi) * (4.0 * row_index + 3.0) / np.float32(4.0 * nlat + 2.0)
+    return (np.float32(math.pi) * np.sin(colatitude) / np.float32(nlat)).astype(np.float32)
+
+
+def grid_rates_body(params, flip, act, drive, rates, carried):
+    i = pl.program_id(0)
+    gain, thresh, decay = params[0, i], params[1, i], params[2, i]
+    halves, rows = rates.shape[0], rates.shape[2]
+    for h in range(halves):
+        u = act[0, h * rows : (h + 1) * rows, :]
+        d = drive[0, h * rows : (h + 1) * rows, :].astype(F32)
+        r = jax.nn.sigmoid(gain * (u - thresh)).astype(BF16)
+        c = ((1.0 - time_step * decay) * u + time_step * d).astype(BF16)
+        rates[h, 0] = jnp.dot(flip[...], r, preferred_element_type=F32).astype(BF16)
+        carried[h, 0] = jnp.dot(flip[...], c, preferred_element_type=F32).astype(BF16)
+
+
+def put_fourier(table, rates, fourier, groups_at_once):
+    halves, pops, rows, cols = rates.shape
+    groups, count, lanes = fourier.shape
+    block = groups_at_once * count
+    for b in range(groups // groups_at_once):
+        parts = []
+        for c in range(2):
+            total = None
+            for h in range(halves):
+                t = table[c, b * block : (b + 1) * block, h * cols : (h + 1) * cols]
+                term = nt_dot(t, rates[h].reshape(pops * rows, cols))
+                total = term if total is None else total + term
+            parts.append(total)
+        joined = jnp.concatenate(parts, axis=1)
+        for g in range(groups_at_once):
+            fourier[b * groups_at_once + g] = joined[g * count : (g + 1) * count].astype(BF16)
+
+
+def put_edges(rates, polar, inner_edge):
+    halves, pops, rows, cols = rates.shape
+    for h in range(halves):
+        strips = [rates[h, i].astype(F32) for i in range(pops)]
+        at = slice(h * cols, (h + 1) * cols)
+        polar[:, at] = jnp.concatenate([v[0:1] for v in strips], axis=0).astype(BF16)
+        last = jnp.concatenate([v[rows - 1 : rows] for v in strips], axis=0)
+        inner_edge[:, at] = last.astype(BF16)
+
+
+def first_fourier_body(table, rates, fourier, polar, inner_edge):
+    put_edges(rates, polar, inner_edge)
+    put_fourier(table, rates, fourier, 4)
+
+
+def lateral_body(params, rates, from_pole, from_equator, across, *refs):
+    out = refs[-1]
+    halves, pops, rows, cols = rates.shape
+    nlon = halves * cols
+    before = from_pole[...].astype(F32)
+    after = from_equator[...].astype(F32) + across[...].astype(F32)
+    for i in range(pops):
+        r = jnp.concatenate([rates[h, i].astype(F32) for h in range(halves)], axis=1)
+        east = pltpu.roll(r, 1, 1)
+        west = pltpu.roll(r, nlon - 1, 1)
+        row = lax.broadcasted_iota(jnp.int32, (rows, nlon), 0)
+        up = jnp.where(row == 0, before[i : i + 1], pltpu.roll(r, 1, 0))
+        down = jnp.where(row == rows - 1, after[i : i + 1], pltpu.roll(r, rows - 1, 0))
+        term = (time_step * params[3, i]) * (east + west + up + down - 4.0 * r)
+        if len(refs) == 2:
+            term = term + (1.0 - time_step * params[2, i]) * refs[0][i]
+        out[i] = term
+
+
+def legendre_body(
+    first, spectrum, weight, mixing, basis, out, even_s, odd_s, north_s, south_s
+):
+    groups, count, lanes = spectrum.shape
+    tiles = even_s.shape[0]
+    block, half_lat, deg = basis.shape
+    pops = mixing.shape[0]
+    src = weight.shape[0]
+    cores = groups // (2 * src)
+    piece = half_lat // src
+    slots = lanes // piece
+    pops_here = slots // 2
+    pad = tiles * 128 - half_lat
+    step = pl.program_id(0)
+
+    def rows_of(p, q):
+        b = (q // pops_here) * pops + p * pops_here + q % pops_here
+        return slice(b * count, (b + 1) * count)
+
+    @pl.when(step == 0)
+    def _():
+        for p in range(cores):
+            evens, odds = [], []
+            for s in range(src):
+                north = spectrum[s * cores + p].astype(F32)
+                south = spectrum[(2 * src - 1 - s) * cores + p].astype(F32)
+                w = weight[s : s + 1]
+                evens.append((w * (north + south)).astype(BF16).astype(F32))
+                odds.append((w * (north - south)).astype(BF16).astype(F32))
+            for q in range(slots):
+                for parts, scratch in ((evens, even_s), (odds, odd_s)):
+                    strips = [v[:, q * piece : (q + 1) * piece] for v in parts]
+                    if pad:
+                        strips.append(jnp.zeros((count, pad), F32))
+                    joined = jnp.concatenate(strips, axis=1)
+                    for t in range(tiles):
+                        scratch[t, rows_of(p, q), :] = joined[:, t * 128 : (t + 1) * 128]
+
+    degree = lax.broadcasted_iota(jnp.int32, (2 * pops, deg), 1)
+    for at in range(block):
+        r = step * block + at
+        m = first[0] + r
+        rows = pl.ds(r, 2 * pops, stride=count)
+        lhs = jnp.concatenate(
+            [
+                jnp.concatenate([scratch[t, rows, :] for t in range(tiles)], axis=1)
+                for scratch in (even_s, odd_s)
+            ],
+            axis=0,
+        )[:, :half_lat].astype(BF16)
+        both = jnp.dot(lhs, basis[at], preferred_element_type=F32)
+        odd = ((degree - m) & 1) == 1
+        coeffs = jnp.where(odd, both[2 * pops :], both[: 2 * pops])
+        coeffs = jnp.where(degree >= m, coeffs, 0.0)
+        mixed = []
+        for c in range(2):
+            total = None
+            for j in range(pops):
+                term = mixing[j] * coeffs[c * pops + j : c * pops + j + 1]
+                total = term if total is None else total + term
+            mixed.append(total)
+        mixed = jnp.concatenate(mixed, axis=0)
+        amplitude = jnp.where(m == 0, 1.0, 2.0)
+        lhs2 = jnp.concatenate([mixed, jnp.where(odd, -mixed, mixed)], axis=0).astype(BF16)
+        field = nt_dot(lhs2, basis[at]) * amplitude
+        if pad:
+            field = jnp.concatenate([field, jnp.zeros((4 * pops, pad), F32)], axis=1)
+        for t in range(tiles):
+            north_s[t, rows, :] = field[: 2 * pops, t * 128 : (t + 1) * 128]
+            south_s[t, rows, :] = field[2 * pops :, t * 128 : (t + 1) * 128]
+
+    @pl.when(step == pl.num_programs(0) - 1)
+    def _():
+        for scratch, south in ((north_s, False), (south_s, True)):
+            for p in range(cores):
+                wide = [
+                    jnp.concatenate(
+                        [scratch[t, rows_of(p, q), :] for t in range(tiles)], axis=1
+                    )
+                    for q in range(slots)
+                ]
+                for s in range(src):
+                    to = (2 * src - 1 - s if south else s) * cores + p
+                    strips = [v[:, s * piece : (s + 1) * piece] for v in wide]
+                    out[to] = jnp.concatenate(strips, axis=1).astype(BF16)
+
+
+def synth_of(spectrum, table, cols, h):
+    _, both = spectrum
+    half = both.shape[0] // 2
+    total = None
+    for c in range(2):
+        term = jnp.dot(
+            both[c * half : (c + 1) * half, :],
+            table[c, :, h * cols : (h + 1) * cols],
+            preferred_element_type=F32,
+        )
+        total = term if total is None else total + term
+    return total
+
+
+def turned(spectrum, turned_s):
+    groups = spectrum.shape[0]
+    stacked = jnp.concatenate([spectrum[g].astype(F32) for g in range(groups)], axis=0)
+    turned_s[...] = stacked.T.astype(BF16)
+
+
+def middle_body(
+    params, table, spectrum, lateral, carried, fourier, rates, polar, inner_edge, inner, turned_s
+):
+    halves, pops, rows, cols = rates.shape
+    turned(spectrum, turned_s)
+    for h in range(halves):
+        synth = synth_of((None, turned_s), table, cols, h) * (time_step / (halves * cols))
+        for i in range(pops):
+            v = lateral[i, :, h * cols : (h + 1) * cols] + synth[i * rows : (i + 1) * rows]
+            inner[i, :, h * cols : (h + 1) * cols] = v
+            u = carried[h, i].astype(F32) + v
+            rates[h, i] = jax.nn.sigmoid(params[0, i] * (u - params[1, i])).astype(BF16)
+    put_edges(rates, polar, inner_edge)
+    put_fourier(table, rates, fourier, 4)
+
+
+def last_body(table, spectrum, lateral, out, turned_s):
+    halves, pops, rows, cols = out.shape
+    turned(spectrum, turned_s)
+    for h in range(halves):
+        synth = synth_of((None, turned_s), table, cols, h) * (time_step / (halves * cols))
+        for i in range(pops):
+            v = lateral[i, :, h * cols : (h + 1) * cols] + synth[i * rows : (i + 1) * rows]
+            out[h, i] = v.astype(BF16)
+
+
+def grid_update_body(params, flip, act, drive, inner, out):
+    i = pl.program_id(0)
+    keep = 1.0 - time_step * params[2, i]
+    halves, rows = inner.shape[0], inner.shape[2]
+    for h in range(halves):
+        at = slice(h * rows, (h + 1) * rows)
+        d = time_step * drive[0, at, :].astype(F32)
+        back = jnp.dot(flip[...], inner[h, 0], preferred_element_type=F32)
+        out[0, at, :] = keep * (keep * act[0, at, :] + d) + d + back
+
+
+def by_parts(activity, drive, basis, kernels, conn_block, coupling, rate_params):
+    pops_here, lat_here, cols = activity.shape
+    owned, half_lat, deg = basis.shape
+    bands, lons, cores = (lax.axis_size(a) for a in ("band", "lon", "pop"))
+    owners = bands * lons
+    groups = owners * cores
+    count = owned // cores
+    rows = lat_here // lons
+    nlat, nlon = bands * lat_here, lons * cols
+    pops = pops_here * cores
+    lanes = 2 * pops_here * rows
+    band, lon, core = (lax.axis_index(a) for a in ("band", "lon", "pop"))
+    owner = band * lons + lon
+    southern = band >= bands // 2
+    params = lax.dynamic_slice_in_dim(rate_params, core * pops_here, pops_here, 1)
+    table = jnp.asarray(fourier_table(nlon, deg))
+    weights = lat_weights(nlat).reshape(owners // 2, 1, rows)
+    weights = jnp.asarray(np.tile(weights, (1, 2 * pops_here, 1)).reshape(owners // 2, lanes))
+    onehot = (conn_block[..., None] == jnp.arange(kernels.shape[0], dtype=jnp.int32)).astype(F32)
+    mixing = coupling[..., None] * jnp.einsum(
+        "ijb,bn->ijn", onehot, kernels, precision=lax.Precision.HIGHEST
+    )
+    mixing = jnp.swapaxes(mixing, 0, 1)
+    row = jnp.arange(rows, dtype=jnp.int32)
+    flip = jnp.where(southern, row[::-1], row)[:, None] == row[None, :]
+    flip = flip.astype(BF16)
+    first_wave = (owner * owned + core * count).astype(jnp.int32)
+    first = jnp.stack([first_wave, core * (count // 4)]).astype(jnp.int32)
+    half = owners // 2
+    poleward = [(o, o - 1) for o in range(1, half)] + [(o, o + 1) for o in range(half, owners - 1)]
+    equatorward = [(o, o + 1) for o in range(half - 1)]
+    equatorward += [(o, o - 1) for o in range(half + 1, owners)]
+    over_equator = [(half - 1, half), (half, half - 1)]
+
+    def one(lead, tail):
+        return pl.BlockSpec((lead, 1) + tail, lambda i: (0, i, 0, 0))
+
+    rates, carried = call(
+        grid_rates_body,
+        (shape(lons, pops_here, rows, cols), shape(lons, pops_here, rows, cols)),
+        32,
+        grid=(pops_here,),
+        in_specs=[
+            scalars(),
+            whole(),
+            pl.BlockSpec((1, lat_here, cols), lambda i: (i, 0, 0)),
+            pl.BlockSpec((1, lat_here, cols), lambda i: (i, 0, 0)),
+        ],
+        out_specs=(one(lons, (rows, cols)), one(lons, (rows, cols))),
+    )(params, flip, activity, drive)
+    rates = lax.all_to_all(rates, "lon", 0, 0, tiled=True)
+    carried = lax.all_to_all(carried, "lon", 0, 0, tiled=True)
+
+    edge = shape(pops_here, nlon)
+    fourier, polar, inner_edge = call(
+        first_fourier_body,
+        (shape(groups, count, lanes), edge, edge),
+        32,
+        in_specs=[whole(), whole()],
+        out_specs=(whole(),) * 3,
+    )(table, rates)
+
+    def coupled(fourier):
+        spectrum = lax.all_to_all(fourier, EVERYONE, 0, 0, tiled=True)
+        tiles = -(-half_lat // 128)
+        block = 4
+        scratch = pltpu.VMEM((tiles, 2 * pops * count, 128), F32)
+        synthesis = call(
+            legendre_body,
+            shape(groups, count, lanes),
+            40,
+            grid_spec=pltpu.PrefetchScalarGridSpec(
+                num_scalar_prefetch=1,
+                grid=(count // block,),
+                in_specs=[
+                    whole(),
+                    whole(),
+                    whole(),
+                    pl.BlockSpec((block, half_lat, deg), lambda i, f: (f[1] + i, 0, 0)),
+                ],
+                out_specs=whole(),
+                scratch_shapes=[scratch] * 4,
+            ),
+        )(first, spectrum, weights, mixing, basis)
+        return lax.all_to_all(synthesis, EVERYONE, 0, 0, tiled=True)
+
+    def lateral(rates, polar, inner_edge, *more):
+        from_pole = lax.ppermute(inner_edge, OWNERS, equatorward)
+        from_equator = lax.ppermute(polar, OWNERS, poleward)
+        across = lax.ppermute(inner_edge, OWNERS, over_equator)
+        return call(
+            lateral_body,
+            shape(pops_here, rows, nlon, dtype=F32),
+            32,
+            in_specs=[scalars()] + [whole()] * (4 + len(more)),
+            out_specs=whole(),
+        )(params, rates, from_pole, from_equator, across, *more)
+
+    back = coupled(fourier)
+    beside = lateral(rates, polar, inner_edge)
+    turned_s = pltpu.VMEM((lanes, deg), BF16)
+    fourier, rates, polar, inner_edge, inner = call(
+        middle_body,
+        (
+            shape(groups, count, lanes),
+            shape(lons, pops_here, rows, cols),
+            edge,
+            edge,
+            shape(pops_here, rows, nlon, dtype=F32),
+        ),
+        48,
+        in_specs=[scalars()] + [whole()] * 4,
+        out_specs=(whole(),) * 5,
+        scratch_shapes=[turned_s],
+    )(params, table, back, beside, carried)
+    back = coupled(fourier)
+    beside = lateral(rates, polar, inner_edge, inner)
+    inner = call(
+        last_body,
+        shape(lons, pops_here, rows, cols),
+        48,
+        in_specs=[whole()] * 3,
+        out_specs=whole(),
+        scratch_shapes=[turned_s],
+    )(table, back, beside)
+    inner = lax.all_to_all(inner, "lon", 0, 0, tiled=True)
+    return call(
+        grid_update_body,
+        shape(*activity.shape, dtype=F32),
+        32,
+        grid=(pops_here,),
+        in_specs=[
+            scalars(),
+            whole(),
+            pl.BlockSpec((1, lat_here, cols), lambda i: (i, 0, 0)),
+            pl.BlockSpec((1, lat_here, cols), lambda i: (i, 0, 0)),
+            one(lons, (rows, cols)),
+        ],
+        out_specs=pl.BlockSpec((1, lat_here, cols), lambda i: (i, 0, 0)),
+    )(params, flip, activity, drive, inner)
 
 
 def with_halo(shard, sides, width):
@@ -27,18 +421,12 @@
     return shard
 
 
-def fourier_table():
-    longitude = jnp.arange(NLON, dtype=jnp.int32)
-    wavenumber = jnp.arange(DEG, dtype=jnp.int32)
-    phase = longitude[:, None] * wavenumber[None, :] % NLON
-    angle = phase.astype(jnp.float32) * (2.0 * math.pi / NLON)
+def plain_table(nlon, deg):
+    longitude = jnp.arange(nlon, dtype=jnp.int32)
+    wavenumber = jnp.arange(deg, dtype=jnp.int32)
+    phase = longitude[:, None] * wavenumber[None, :] % nlon
+    angle = phase.astype(jnp.float32) * (2.0 * math.pi / nlon)
     return jnp.stack([jnp.cos(angle), jnp.sin(angle)], axis=1).astype(jnp.bfloat16)
-
-
-def lat_weights():
-    row_index = jnp.arange(NLAT // 2, dtype=jnp.float32)
-    colatitude = math.pi * (4.0 * row_index + 3.0) / (4.0 * NLAT + 2.0)
-    return math.pi * jnp.sin(colatitude) / NLAT
 
 
 def to_owners(fourier):
@@ -49,23 +437,25 @@
     return lax.all_to_all(synthesis, ("band", "lon"), split_axis=3, concat_axis=2, tiled=True)
 
 
-def local(activity, drive, basis, kernels, conn_block, coupling, rate_params):
+def by_arrays(activity, drive, basis, kernels, conn_block, coupling, rate_params):
     pop_here = activity.shape[0]
     owned_count = basis.shape[0]
     half_lat = basis.shape[1]
-    quarter = DEG // 2
+    deg = basis.shape[2]
+    nlon = activity.shape[2] * lax.axis_size("lon")
+    quarter = deg // 2
     owner_index = lax.axis_index("band") * lax.axis_size("lon") + lax.axis_index("lon")
     pop_first = lax.axis_index("pop") * pop_here
     params = lax.dynamic_slice_in_dim(rate_params, pop_first, pop_here, 1)
     gain_row, thresh, decay_row, lateral = (params[0], params[1], params[2], params[3])
-    cos_sin = fourier_table()
-    weights = lat_weights()
+    cos_sin = plain_table(nlon, deg)
+    weights = jnp.asarray(lat_weights(2 * half_lat))
     wavenumber = owner_index * owned_count + jnp.arange(owned_count, dtype=jnp.int32)
-    degree = jnp.arange(DEG, dtype=jnp.int32)
+    degree = jnp.arange(deg, dtype=jnp.int32)
     triangle = degree[None, :] >= wavenumber[:, None]
     slots = jnp.arange(2, dtype=jnp.int32)
     parity_pick = (slots[None, :] == (wavenumber % 2)[:, None])[None, None, :, :, None]
-    every_wave = jnp.arange(DEG, dtype=jnp.int32)
+    every_wave = jnp.arange(deg, dtype=jnp.int32)
     amplitude = jnp.where(every_wave == 0, 1.0, 2.0).astype(jnp.bfloat16)
     coup_own = lax.dynamic_slice_in_dim(coupling, pop_first, pop_here, 0)
     block_own = lax.dynamic_slice_in_dim(conn_block, pop_first, pop_here, 0)
@@ -95,7 +485,7 @@
         coeffs = jnp.einsum(
             "icmsj,mjqs->icmqs", operand, basis_split, preferred_element_type=jnp.float32
         )
-        coeffs = coeffs.reshape(pop_here, 2, owned_count, DEG)
+        coeffs = coeffs.reshape(pop_here, 2, owned_count, deg)
         coeffs = jnp.where(triangle[None, None], coeffs, 0.0)
         gathered = lax.all_gather(coeffs.astype(jnp.bfloat16), "pop", axis=0, tiled=True).astype(
             coeffs.dtype
@@ -118,7 +508,7 @@
         scaled = returned * amplitude[None, None, :, None]
         synth_field = jnp.einsum(
             "icmj,kcm->ijk", scaled, cos_sin, preferred_element_type=jnp.float32
-        ) * (1.0 / NLON)
+        ) * (1.0 / nlon)
         padded = with_halo(lat_rows, ((("band", "lon"), 1),), 1).astype(jnp.float32)
         rates_f32 = lat_rows.astype(jnp.float32)
         lateral_term = (
@@ -138,6 +528,20 @@
 
 
 def solution(mesh):
+    bands, lons, cores = (mesh.shape[a] for a in ("band", "lon", "pop"))
+
+    def local(activity, drive, basis, *rest):
+        rows, owned = activity.shape[1] // lons, basis.shape[0]
+        fits = (
+            bands % 2 == 0
+            and owned % (4 * cores) == 0
+            and (owned // cores) % 8 == 0
+            and rows % 16 == 0
+            and activity.shape[2] % 128 == 0
+            and 2 * activity.shape[0] * rows % 128 == 0
+        )
+        return (by_parts if fits else by_arrays)(activity, drive, basis, *rest)
+
     in_specs = (
         P(("subj", "pop"), "band", "lon"),
         P(("subj", "pop"), "band", "lon"),

time: 541 us -> 198 us (0.37)
  local copies, waits for them, and re-layouts: 199 us -> 7.39 us
  matrix products: 90.8 us -> 0.29 us
  Pallas kernels: 0 us -> 56.3 us
  waiting for transfers between devices: 63.8 us -> 19.5 us
  other arithmetic: 43.2 us -> 0.17 us
  between operations: 14.2 us -> 0.22 us
  starting transfers between devices: 33.6 us -> 25.7 us
    dot_general x9 -> x1, matrix products: 90.8 us -> 0.29 us  [by_parts(): jnp.einsum('ijb,bn->ijn', onehot, kernels, precision=lax.Precision.HIGHEST)]
    unnamed x43 -> x28, local copies, waits for them, and re-layouts: 70.9 us -> 6.37 us
    pallas_call x0 -> x9, Pallas kernels: none -> 56.3 us  [the longest x2 34 us: coupled(): call(legendre_body, shape(groups, count, lanes), 40, grid_spec=pltpu.Pref...]
    reshape x3 -> x0, local copies, waits for them, and re-layouts: 55.8 us -> none  [the longest x1 53.5 us: local(): basis_split = basis.reshape(owned_count, half_lat, quarter, 2)]
    convert_element_type x16 -> x0, local copies, waits for them, and re-layouts: 30.7 us -> none  [the longest x4 10.1 us: local(): jnp.sum(mixing[:, :, None, None, :] * gathered[None], axis=1)]
    all_to_all x4 -> x3, waiting for transfers between devices: 38 us -> 16.8 us  [the longest x2 16.8 us: coupled(): return lax.all_to_all(synthesis, EVERYONE, 0, 0, tiled=True)]
    all_to_all x14 -> x0, local copies, waits for them, and re-layouts: 19.2 us -> none  [the longest x4 8.13 us: to_owners(): lax.all_to_all(fourier, ('band', 'lon'), split_axis=2, concat_axis=3, til...]
    all_gather x2 -> x0, waiting for transfers between devices: 18.6 us -> none  [local(): lax.all_gather(coeffs.astype(jnp.bfloat16), 'pop', axis=0, tiled=True)]
  transfers between devices with their start and end apart: 10 -> 9, of which waited for: 8 -> 6; matrix products, arithmetic and copies ran while one was open for 24% -> 0% of each run, Pallas kernels for 0% -> 10%
where the time goes in v1:
time: 198 us; the launch traced here: 194 us
  blocking collectives  84.3 us (43%)
  Pallas kernels  56.3 us (28%)
  starting transfers between devices  25.7 us (13%)
  waiting for transfers between devices  19.5 us (10%)
  local copies, waits for them, and re-layouts  7.39 us (4%)
    all_to_all x2, blocking collectives, coupled(): spectrum = lax.all_to_all(fourier, EVERYONE, 0, 0, tiled=True)  54.8 us
    pallas_call x2, Pallas kernels, coupled(): call(legendre_body, shape(groups, count, lanes), 40, grid_spec=pltpu.Pref...  34 us
    all_to_all x2, waiting for transfers between devices, coupled(): return lax.all_to_all(synthesis, EVERYONE, 0, 0, tiled=True)  16.8 us
    all_to_all x1, blocking collectives, by_parts(): rates = lax.all_to_all(rates, 'lon', 0, 0, tiled=True)  15.1 us
    all_to_all x1, blocking collectives, by_parts(): inner = lax.all_to_all(inner, 'lon', 0, 0, tiled=True)  14.5 us
    all_to_all x2, starting transfers between devices, coupled(): return lax.all_to_all(synthesis, EVERYONE, 0, 0, tiled=True)  9.19 us
    ppermute x2, starting transfers between devices, lateral(): from_pole = lax.ppermute(inner_edge, OWNERS, equatorward)  9.09 us
    pallas_call x1, Pallas kernels, by_parts(): call(middle_body, (shape(groups, count, lanes), shape(lons, pops_here, ro...  6.94 us
  transfers between devices with their start and end apart: 9, of which 6 were waited for; matrix products, arithmetic and copies ran while one was open for 0% of the time, Pallas kernels for 10%

profile of v1, /device:TPU:0, one launch (start us, length us, event | category | flops | bytes accessed | tf_op | source)
XLA Modules:
  0.0 194.0 jit_solution(6749226470390476389)
XLA Ops:
  0.0 0.0 copy-start
  0.0 0.1 rev.3
  0.1 0.1 fusion.1.flip
  0.2 0.8 constant_dynamic-slice_fusion.params
  1.0 0.0 copy-start.5
  1.0 1.4 copy-done.5
  2.4 0.0 copy-start.7
  2.4 1.1 copy-done.7
  3.5 0.0 copy-start.1
  3.5 2.9 %shard_map.91 = (bf16[2,4,80,640]{3,2,1,0:T(8,128)(2,1)S(1)}, bf16[2,4,80,640]{3,2,1,0:T(8,128)(2,1)}) custom-call(f32[4,4]{1,0:T(4,128)S(1)} %constant_dynamic-slice_fusion.params, bf16[80,80]{1,0:T(8,128)(2,1)S(1)} %fusion.1.flip, f32[4,160,640]{2,1,0:T(8,128)S(1)} %copy-done.5, bf16[4,160,640]{2,1,0:T(8,128)(2,1)S(1)} %copy-done.7), custom_call_target="tpu_custom_call" | custom-call | tf_op jit(solution)/shard_map/pallas_call | solution.py:306
  6.4 15.1 %all_to_all.35.rates = bf16[2,4,80,640]{3,2,1,0:T(8,128)(2,1)S(1)} all-to-all(bf16[2,4,80,640]{3,2,1,0:T(8,128)(2,1)S(1)} %get-tuple-element.15), channel_id=1, replica_groups=mesh['subj'=2,'band'=4,'lon'=2,'pop'=2] {'lon'}, dimensions={0} | all-to-all | bytes 1638400 | tf_op jit(solution)/shard_map/all_to_all | solution.py:319
  21.5 0.0 copy-done.1
  21.5 0.0 copy-start.2
  21.5 2.7 %shard_map.92 = (bf16[16,40,640]{2,1,0:T(8,128)(2,1)S(1)}, bf16[4,1280]{1,0:T(4,128)(2,1)S(1)}, bf16[4,1280]{1,0:T(4,128)(2,1)S(1)}) custom-call(bf16[2,640,1280]{2,1,0:T(8,128)(2,1)S(1)} %copy-done.1, bf16[2,4,80,640]{3,2,1,0:T(8,128)(2,1)S(1)} %all_to_all.35.rates), custom_call_target="tpu_custom_call" | custom-call | tf_op jit(solution)/shard_map/pallas_call | solution.py:323
  24.3 0.0 copy-done.2
  24.3 0.0 copy-start.12
  24.3 0.0 copy-start.13
  24.3 0.0 copy-start.11
  24.3 25.9 %all_to_all.36.spectrum = bf16[16,40,640]{2,1,0:T(8,128)(2,1)S(1)} all-to-all(bf16[16,40,640]{2,1,0:T(8,128)(2,1)S(1)} %get-tuple-element.16), channel_id=1, replica_groups=mesh['subj'=2,'band'=4,'lon'=2,'pop'=2] {'band','lon','pop'}, dimensions={0} | all-to-all | bytes 1638400 | tf_op jit(solution)/shard_map/all_to_all | solution.py:332
  50.2 3.5 %all-to-all-start.3 = ((bf16[2,4,80,640]{3,2,1,0:T(8,128)(2,1)}), bf16[2,4,80,640]{3,2,1,0:T(8,128)(2,1)S(1)}, u32[]{:S(2)}, u32[]{:S(2)}) async-start(bf16[2,4,80,640]{3,2,1,0:T(8,128)(2,1)} %get-tuple-element.19), calls=%async_computation.3 | async-start | bytes 1638400 | tf_op jit(solution)/shard_map/all_to_all | solution.py:320
  53.8 0.0 copy-done.12
  53.8 0.1 copy.12
  53.9 0.0 copy-done.13
  53.9 0.1 copy.10
  54.0 0.1 pad_add_fusion.first
  54.1 0.0 copy-done
  54.1 0.3 fusion.mixing
  54.4 0.0 copy-done.11
  54.4 17.0 %shard_map.93 = bf16[16,40,640]{2,1,0:T(8,128)(2,1)} custom-call(s32[2]{0:T(128)S(1)} %pad_add_fusion.first, bf16[16,40,640]{2,1,0:T(8,128)(2,1)S(1)} %all_to_all.36.spectrum, f32[4,640]{1,0:T(4,128)S(1)} %copy-done.11, f32[8,8,640]{2,1,0:T(8,128)S(1)} %fusion.mixing, bf16[80,320,640]{2,1,0:T(8,128)(2,1)} %basis.3), custom_call_target="tpu_custom_call" | custom-call | tf_op jit(solution)/shard_map/pallas_call | solution.py:336
  71.4 0.0 copy-start.3
  71.4 0.0 all-to-all-done.3.carried
  71.4 5.1 %all-to-all-start.2 = ((bf16[16,40,640]{2,1,0:T(8,128)(2,1)}), bf16[16,40,640]{2,1,0:T(8,128)(2,1)S(1)}, u32[]{:S(2)}, u32[]{:S(2)}) async-start(bf16[16,40,640]{2,1,0:T(8,128)(2,1)} %shard_map.93), calls=%async_computation.2 | async-start | bytes 1638400 | tf_op jit(solution)/shard_map/all_to_all | solution.py:353
  76.5 1.3 collective-permute-start.1
  77.8 0.7 collective-permute-start.2
  78.5 4.5 %collective-permute-start = (bf16[4,1280]{1,0:T(4,128)(2,1)S(1)}, bf16[4,1280]{1,0:T(4,128)(2,1)S(1)}, u32[]{:S(2)}, u32[]{:S(2)}) collective-permute-start(bf16[4,1280]{1,0:T(4,128)(2,1)S(1)} %get-tuple-element.17), channel_id=1, source_target_pairs={{0,2},{2,4},{4,6},{10,8},{12,10},{14,12},{1,3},{3,5},{5,7},{11,9},... | collective-permute-start | bytes 30728 | tf_op jit(solution)/shard_map/ppermute | solution.py:356
  83.1 0.8 collective-permute-done.1.from_equator
  83.9 0.0 collective-permute-done.2.across
  83.9 0.6 collective-permute-done.from_pole
  84.4 0.0 copy-done.3
  84.4 1.6 shard_map.94.lateral
  86.0 0.0 copy-start.4
  86.0 1.2 copy-done.4
  87.2 8.6 %all-to-all-done.2.spectrum = bf16[16,40,640]{2,1,0:T(8,128)(2,1)S(1)} async-done(((bf16[16,40,640]{2,1,0:T(8,128)(2,1)}), bf16[16,40,640]{2,1,0:T(8,128)(2,1)S(1)}, u32[]{:S(2)}, u32[]{:S(2)}) %all-to-all-start.2) | async-done | bytes 819232 | tf_op jit(solution)/shard_map/all_to_all | solution.py:353
  95.8 6.9 %shard_map.95 = (bf16[16,40,640]{2,1,0:T(8,128)(2,1)S(1)}, bf16[2,4,80,640]{3,2,1,0:T(8,128)(2,1)S(1)}, bf16[4,1280]{1,0:T(4,128)(2,1)S(1)}, bf16[4,1280]{1,0:T(4,128)(2,1)S(1)}, f32[4,80,1280]{2,1,0:T(8,128)S(1)}) custom-call(f32[4,4]{1,0:T(4,128)S(1)} %constant_dynamic-slice_fusion.params, bf16[2,640,1280]{2,1,0:T(8,128)(2,1)} %constant.29.clone.table, ...), custom_call_target="tpu_custom_call" | custom-call | tf_op jit(solution)/shard_map/pallas_call | solution.py:370
  102.7 0.0 copy-start.9
  102.7 1.2 copy-done.9
  103.9 28.9 %all_to_all.37.spectrum = bf16[16,40,640]{2,1,0:T(8,128)(2,1)S(1)} all-to-all(bf16[16,40,640]{2,1,0:T(8,128)(2,1)S(1)} %get-tuple-element.20), channel_id=1, replica_groups=mesh['subj'=2,'band'=4,'lon'=2,'pop'=2] {'band','lon','pop'}, dimensions={0} | all-to-all | bytes 1638400 | tf_op jit(solution)/shard_map/all_to_all | solution.py:332
  132.7 17.0 %shard_map.96 = bf16[16,40,640]{2,1,0:T(8,128)(2,1)} custom-call(s32[2]{0:T(128)S(1)} %pad_add_fusion.first, bf16[16,40,640]{2,1,0:T(8,128)(2,1)S(1)} %all_to_all.37.spectrum, f32[4,640]{1,0:T(4,128)S(1)} %copy-done.11, f32[8,8,640]{2,1,0:T(8,128)S(1)} %fusion.mixing, bf16[80,320,640]{2,1,0:T(8,128)(2,1)} %basis.3), custom_call_target="tpu_custom_call" | custom-call | tf_op jit(solution)/shard_map/pallas_call | solution.py:336
  149.7 4.0 %all-to-all-start.5 = ((bf16[16,40,640]{2,1,0:T(8,128)(2,1)}), bf16[16,40,640]{2,1,0:T(8,128)(2,1)S(1)}, u32[]{:S(2)}, u32[]{:S(2)}) async-start(bf16[16,40,640]{2,1,0:T(8,128)(2,1)} %shard_map.96), calls=%async_computation.5 | async-start | bytes 1638400 | tf_op jit(solution)/shard_map/all_to_all | solution.py:353
  153.8 1.3 collective-permute-start.4
  155.1 0.7 collective-permute-start.5
  155.7 4.5 %collective-permute-start.3 = (bf16[4,1280]{1,0:T(4,128)(2,1)S(1)}, bf16[4,1280]{1,0:T(4,128)(2,1)S(1)}, u32[]{:S(2)}, u32[]{:S(2)}) collective-permute-start(bf16[4,1280]{1,0:T(4,128)(2,1)S(1)} %get-tuple-element.22), channel_id=1, source_target_pairs={{0,2},{2,4},{4,6},{10,8},{12,10},{14,12},{1,3},{3,5},{5,7},{11,9},... | collective-permute-start | bytes 30728 | tf_op jit(solution)/shard_map/ppermute | solution.py:356
  160.3 0.8 collective-permute-done.4.from_equator
  161.1 0.0 collective-permute-done.5.across
  161.1 0.6 collective-permute-done.3.from_pole
  161.6 1.4 copy-done.10
  163.1 1.7 shard_map.97.lateral
  164.8 8.2 %all-to-all-done.5.spectrum = bf16[16,40,640]{2,1,0:T(8,128)(2,1)S(1)} async-done(((bf16[16,40,640]{2,1,0:T(8,128)(2,1)}), bf16[16,40,640]{2,1,0:T(8,128)(2,1)S(1)}, u32[]{:S(2)}, u32[]{:S(2)}) %all-to-all-start.5) | async-done | bytes 819232 | tf_op jit(solution)/shard_map/all_to_all | solution.py:353
  173.0 3.7 %shard_map.98 = bf16[2,4,80,640]{3,2,1,0:T(8,128)(2,1)S(1)} custom-call(bf16[2,640,1280]{2,1,0:T(8,128)(2,1)} %constant.29.clone.table, bf16[16,40,640]{2,1,0:T(8,128)(2,1)S(1)} %all-to-all-done.5.spectrum, f32[4,80,1280]{2,1,0:T(8,128)S(1)} %shard_map.97.lateral), custom_call_target="tpu_custom_call" | custom-call | tf_op jit(solution)/shard_map/pallas_call | solution.py:386
  176.7 0.0 copy-start.6
  176.7 14.5 %all_to_all.38.inner = bf16[2,4,80,640]{3,2,1,0:T(8,128)(2,1)S(1)} all-to-all(bf16[2,4,80,640]{3,2,1,0:T(8,128)(2,1)S(1)} %shard_map.98), channel_id=1, replica_groups=mesh['subj'=2,'band'=4,'lon'=2,'pop'=2] {'lon'}, dimensions={0} | all-to-all | bytes 1638400 | tf_op jit(solution)/shard_map/all_to_all | solution.py:394
  191.2 0.0 copy-done.8
  191.2 0.0 copy-done.6
  191.2 2.8 %shard_map.99 = f32[4,160,640]{2,1,0:T(8,128)} custom-call(f32[4,4]{1,0:T(4,128)S(1)} %constant_dynamic-slice_fusion.params, bf16[80,80]{1,0:T(8,128)(2,1)S(1)} %fusion.1.flip, f32[4,160,640]{2,1,0:T(8,128)S(1)} %copy-done.6, bf16[4,160,640]{2,1,0:T(8,128)(2,1)S(1)} %copy-done.8, bf16[2,4,80,640]{3,2,1,0:T(8,128)(2,1)S(1)} %all_to_all.38.inner), custom_call_target="tpu_custom_call" | custom-call | tf_op jit(solution)/shard_map/pallas_call | solution.py:395
  (5 shorter events, 0.0 us)
Async XLA Ops:
  0.0 54.1 %copy-start = (f32[4,640]{1,0:T(4,128)S(1)}, f32[4,640]{1,0:T(4,128)}, u32[]{:S(2)}) copy-start(f32[4,640]{1,0:T(4,128)} %param.12) | copy-start | bytes 30724
  1.0 1.4 copy-start.5
  2.4 1.1 copy-start.7
  3.5 18.0 %copy-start.1 = (bf16[2,640,1280]{2,1,0:T(8,128)(2,1)S(1)}, bf16[2,640,1280]{2,1,0:T(8,128)(2,1)}, u32[]{:S(2)}) copy-start(bf16[2,640,1280]{2,1,0:T(8,128)(2,1)} %constant.29.clone.table) | copy-start | bytes 9830404
  21.5 2.7 %copy-start.2 = (bf16[2,4,80,640]{3,2,1,0:T(8,128)(2,1)}, bf16[2,4,80,640]{3,2,1,0:T(8,128)(2,1)S(1)}, u32[]{:S(2)}) copy-start(bf16[2,4,80,640]{3,2,1,0:T(8,128)(2,1)S(1)} %all_to_all.35.rates) | copy-start | bytes 2457604
  24.3 29.5 %copy-start.12 = (s32[8,8]{1,0:T(8,128)S(1)}, s32[8,8]{1,0:T(8,128)}, u32[]{:S(2)}) copy-start(s32[8,8]{1,0:T(8,128)} %param.13) | copy-start | bytes 772
  24.3 29.6 %copy-start.13 = (f32[8,8]{1,0:T(8,128)S(1)}, f32[8,8]{1,0:T(8,128)}, u32[]{:S(2)}) copy-start(f32[8,8]{1,0:T(8,128)} %param.14) | copy-start | bytes 772
  24.3 30.0 %copy-start.11 = (f32[4,640]{1,0:T(4,128)S(1)}, f32[4,640]{1,0:T(4,128)}, u32[]{:S(2)}) copy-start(f32[4,640]{1,0:T(4,128)} %constant.30.clone.weight) | copy-start | bytes 30724
  50.2 21.1 %all-to-all-start.3 = ((bf16[2,4,80,640]{3,2,1,0:T(8,128)(2,1)}), bf16[2,4,80,640]{3,2,1,0:T(8,128)(2,1)S(1)}, u32[]{:S(2)}, u32[]{:S(2)}) async-start(bf16[2,4,80,640]{3,2,1,0:T(8,128)(2,1)} %get-tuple-element.19), calls=%async_computation.3 | async-start | bytes 1638400 | tf_op jit(solution)/shard_map/all_to_all | solution.py:320
  71.4 13.1 %copy-start.3 = (bf16[2,4,80,640]{3,2,1,0:T(8,128)(2,1)S(1)}, bf16[2,4,80,640]{3,2,1,0:T(8,128)(2,1)}, u32[]{:S(2)}) copy-start(bf16[2,4,80,640]{3,2,1,0:T(8,128)(2,1)} %copy-done.2) | copy-start | bytes 2457604
  71.4 24.4 %all-to-all-start.2 = ((bf16[16,40,640]{2,1,0:T(8,128)(2,1)}), bf16[16,40,640]{2,1,0:T(8,128)(2,1)S(1)}, u32[]{:S(2)}, u32[]{:S(2)}) async-start(bf16[16,40,640]{2,1,0:T(8,128)(2,1)} %shard_map.93), calls=%async_computation.2 | async-start | bytes 1638400 | tf_op jit(solution)/shard_map/all_to_all | solution.py:353
  76.5 7.3 %collective-permute-start.1 = (bf16[4,1280]{1,0:T(4,128)(2,1)S(1)}, bf16[4,1280]{1,0:T(4,128)(2,1)S(1)}, u32[]{:S(2)}, u32[]{:S(2)}) collective-permute-start(bf16[4,1280]{1,0:T(4,128)(2,1)S(1)} %get-tuple-element.18), channel_id=1, source_target_pairs={{2,0},{4,2},{6,4},{8,10},{10,12},{12,14},{3,1},{5,3},{7,5},{9,11},... | collective-permute-start | bytes 30728 | tf_op jit(solution)/shard_map/ppermute | solution.py:357
  77.8 6.0 %collective-permute-start.2 = (bf16[4,1280]{1,0:T(4,128)(2,1)S(1)}, bf16[4,1280]{1,0:T(4,128)(2,1)S(1)}, u32[]{:S(2)}, u32[]{:S(2)}) collective-permute-start(bf16[4,1280]{1,0:T(4,128)(2,1)S(1)} %get-tuple-element.17), channel_id=1, source_target_pairs={{6,8},{8,6},{7,9},{9,7},{22,24},{24,22},{23,25},{25,23}} | collective-permute-start | bytes 30728 | tf_op jit(solution)/shard_map/ppermute | solution.py:358
  78.5 5.9 %collective-permute-start = (bf16[4,1280]{1,0:T(4,128)(2,1)S(1)}, bf16[4,1280]{1,0:T(4,128)(2,1)S(1)}, u32[]{:S(2)}, u32[]{:S(2)}) collective-permute-start(bf16[4,1280]{1,0:T(4,128)(2,1)S(1)} %get-tuple-element.17), channel_id=1, source_target_pairs={{0,2},{2,4},{4,6},{10,8},{12,10},{14,12},{1,3},{3,5},{5,7},{11,9},... | collective-permute-start | bytes 30728 | tf_op jit(solution)/shard_map/ppermute | solution.py:356
  86.0 1.2 copy-start.4
  102.7 1.2 copy-start.9
  149.7 23.3 %all-to-all-start.5 = ((bf16[16,40,640]{2,1,0:T(8,128)(2,1)}), bf16[16,40,640]{2,1,0:T(8,128)(2,1)S(1)}, u32[]{:S(2)}, u32[]{:S(2)}) async-start(bf16[16,40,640]{2,1,0:T(8,128)(2,1)} %shard_map.96), calls=%async_computation.5 | async-start | bytes 1638400 | tf_op jit(solution)/shard_map/all_to_all | solution.py:353
  153.8 7.3 %collective-permute-start.4 = (bf16[4,1280]{1,0:T(4,128)(2,1)S(1)}, bf16[4,1280]{1,0:T(4,128)(2,1)S(1)}, u32[]{:S(2)}, u32[]{:S(2)}) collective-permute-start(bf16[4,1280]{1,0:T(4,128)(2,1)S(1)} %get-tuple-element.23), channel_id=1, source_target_pairs={{2,0},{4,2},{6,4},{8,10},{10,12},{12,14},{3,1},{5,3},{7,5},{9,11},... | collective-permute-start | bytes 30728 | tf_op jit(solution)/shard_map/ppermute | solution.py:357
  155.1 6.0 %collective-permute-start.5 = (bf16[4,1280]{1,0:T(4,128)(2,1)S(1)}, bf16[4,1280]{1,0:T(4,128)(2,1)S(1)}, u32[]{:S(2)}, u32[]{:S(2)}) collective-permute-start(bf16[4,1280]{1,0:T(4,128)(2,1)S(1)} %get-tuple-element.22), channel_id=1, source_target_pairs={{6,8},{8,6},{7,9},{9,7},{22,24},{24,22},{23,25},{25,23}} | collective-permute-start | bytes 30728 | tf_op jit(solution)/shard_map/ppermute | solution.py:358
  155.7 5.9 %collective-permute-start.3 = (bf16[4,1280]{1,0:T(4,128)(2,1)S(1)}, bf16[4,1280]{1,0:T(4,128)(2,1)S(1)}, u32[]{:S(2)}, u32[]{:S(2)}) collective-permute-start(bf16[4,1280]{1,0:T(4,128)(2,1)S(1)} %get-tuple-element.22), channel_id=1, source_target_pairs={{0,2},{2,4},{4,6},{10,8},{12,10},{14,12},{1,3},{3,5},{5,7},{11,9},... | collective-permute-start | bytes 30728 | tf_op jit(solution)/shard_map/ppermute | solution.py:356
  161.6 1.4 copy-start.10
  173.0 18.2 %copy-start.8 = (bf16[4,160,640]{2,1,0:T(8,128)(2,1)S(1)}, bf16[4,160,640]{2,1,0:T(8,128)(2,1)}, u32[]{:S(2)}) copy-start(bf16[4,160,640]{2,1,0:T(8,128)(2,1)} %drive.3) | copy-start | bytes 2457604
  176.7 14.5 %copy-start.6 = (f32[4,160,640]{2,1,0:T(8,128)S(1)}, f32[4,160,640]{2,1,0:T(8,128)}, u32[]{:S(2)}) copy-start(f32[4,160,640]{2,1,0:T(8,128)} %act.3) | copy-start | bytes 4915204

commit v2 on v0

--- a/solution.py
+++ b/solution.py
@@ -1,17 +1,482 @@
+import functools
 import math
 
 import jax
 import jax.numpy as jnp
+import ml_dtypes
+import numpy as np
 from jax import lax
+from jax.experimental import pallas as pl
+from jax.experimental.pallas import tpu as pltpu
 from jax.sharding import PartitionSpec as P
 
-NLAT = 640
-NLON = 1280
-DEG = 640
 STEPS = 2
-
-
 time_step = 0.5
+F32 = jnp.float32
+BF16 = jnp.bfloat16
+OWNERS = ("band", "lon")
+EVERYONE = ("band", "lon", "pop")
+MIB = 1 << 20
+
+
+def call(body, out_shape, vmem_mib, flops=0, nbytes=0, **kw):
+    return pl.pallas_call(
+        body,
+        out_shape=out_shape,
+        compiler_params=pltpu.CompilerParams(vmem_limit_bytes=vmem_mib * MIB),
+        cost_estimate=pl.CostEstimate(flops=flops, bytes_accessed=nbytes, transcendentals=0),
+        **kw,
+    )
+
+
+def whole():
+    return pl.BlockSpec(memory_space=pltpu.VMEM)
+
+
+def scalars():
+    return pl.BlockSpec(memory_space=pltpu.SMEM)
+
+
+def shape(*dims, dtype=BF16):
+    return jax.ShapeDtypeStruct(dims, dtype)
+
+
+def nt_dot(a, b):
+    return lax.dot_general(a, b, (((1,), (1,)), ((), ())), preferred_element_type=F32)
+
+
+def fourier_table(nlon, deg):
+    phase = np.arange(deg, dtype=np.int64)[:, None] * np.arange(nlon, dtype=np.int64)[None, :] % nlon
+    angle = phase.astype(np.float32) * np.float32(2.0 * math.pi / nlon)
+    return np.stack([np.cos(angle), np.sin(angle)]).astype(ml_dtypes.bfloat16)
+
+
+def lat_weights(nlat):
+    row_index = np.arange(nlat // 2, dtype=np.float32)
+    colatitude = np.float32(math.pi) * (4.0 * row_index + 3.0) / np.float32(4.0 * nlat + 2.0)
+    return (np.float32(math.pi) * np.sin(colatitude) / np.float32(nlat)).astype(np.float32)
+
+
+def here():
+    bands, lons = lax.axis_size("band"), lax.axis_size("lon")
+    band, lon = lax.axis_index("band"), lax.axis_index("lon")
+    owner, half = band * lons + lon, bands * lons // 2
+    at_equator = jnp.logical_or(owner == half - 1, owner == half)
+    at_pole = jnp.logical_or(owner == 0, owner == 2 * half - 1)
+    return lon, owner >= half, at_equator, at_pole
+
+
+def in_wire_order(block):
+    rows = block.shape[0]
+    a = lax.broadcasted_iota(jnp.int32, (rows, rows), 0)
+    b = lax.broadcasted_iota(jnp.int32, (rows, rows), 1)
+    move = jnp.where(a == jnp.where(here()[1], rows - 1 - b, b), 1.0, 0.0).astype(BF16)
+    return jnp.dot(move, block, preferred_element_type=F32)
+
+
+def rate_of(params, i, u):
+    return jax.nn.sigmoid(params[0, i] * (u - params[1, i])).astype(BF16)
+
+
+def half_of(ref, lead, half, rows):
+    return ref[lead, pl.ds(pl.multiple_of(half * rows, 16), rows), :]
+
+
+def sent_rates_body(params, act, rates):
+    first = lax.axis_index("pop") * act.shape[0]
+    for i in range(act.shape[0]):
+        rates[i] = in_wire_order(rate_of(params, first + i, act[i])).astype(BF16)
+
+
+def own_half_body(params, table, act, drive, rates, sent, kept, part):
+    pops, rows, cols = rates.shape
+    first = lax.axis_index("pop") * pops
+    lon = here()[0]
+    for i in range(pops):
+        decay = params[2, first + i]
+        for half, out in ((1 - lon, sent), (lon, kept)):
+            u = half_of(act, i, half, rows)
+            d = half_of(drive, i, half, rows).astype(F32)
+            c = ((1.0 - time_step * decay) * u + time_step * d).astype(BF16)
+            out[i] = in_wire_order(c).astype(BF16)
+        r = rate_of(params, first + i, half_of(act, i, lon, rows))
+        rates[i] = in_wire_order(r).astype(BF16)
+    block = part.shape[0] // 4
+    columns = [pl.ds(pl.multiple_of(lon * cols, 128), cols)]
+    flat = [rates[...].reshape(pops * rows, cols)]
+    for b in range(4):
+        part[b * block : (b + 1) * block] = joined_fourier(table, b * block, block, columns, flat)
+
+
+def joined_fourier(table, first, block, columns, rates):
+    parts = []
+    for c in range(2):
+        total = None
+        for at, r in zip(columns, rates):
+            term = nt_dot(table[c, first : first + block, at], r)
+            total = term if total is None else total + term
+        parts.append(total)
+    return jnp.concatenate(parts, axis=1)
+
+
+def put_fourier(table, columns, flat, rates, fourier, part=None):
+    halves, pops, rows, cols = rates.shape
+    groups, total, lanes = fourier.shape
+    extra = halves * pops * cols // lanes
+    count = total - extra
+    pack = 4
+    block = pack * count
+    strips = [rates[h, i].astype(F32) for h in range(halves) for i in range(pops)]
+    polar = jnp.concatenate([v[0:1] for v in strips], axis=0)
+    inner = jnp.concatenate([v[rows - 1 : rows] for v in strips], axis=0)
+    _, southern, _, _ = here()
+    owner = lax.axis_index("band") * lax.axis_size("lon") + lax.axis_index("lon")
+    poleward = jnp.where(southern, owner + 1, owner - 1)
+    cores = lax.axis_size("pop")
+    for b in range(groups // pack):
+        joined = joined_fourier(table, b * block, block, columns, flat)
+        if part is not None:
+            joined = joined + part[b * block : (b + 1) * block]
+        for g in range(pack):
+            to = b * pack + g
+            edge = jnp.where(poleward == to // cores, polar, inner)
+            sums = joined[g * count : (g + 1) * count]
+            fourier[to] = jnp.concatenate([sums, edge], axis=0).astype(BF16)
+
+
+def fourier_of(table, rates, fourier):
+    halves, pops, rows, cols = rates.shape
+    columns = [slice(h * cols, (h + 1) * cols) for h in range(halves)]
+    flat = [rates[h].reshape(pops * rows, cols) for h in range(halves)]
+    put_fourier(table, columns, flat, rates, fourier)
+
+
+def first_fourier_body(table, part, kept, got, fourier, rates):
+    pops, rows, cols = got.shape
+    lon = here()[0]
+    rates[lon] = kept[...]
+    rates[1 - lon] = got[...]
+    columns = [pl.ds(pl.multiple_of((1 - lon) * cols, 128), cols)]
+    put_fourier(table, columns, [got[...].reshape(pops * rows, cols)], rates, fourier, part)
+
+
+def lateral_of(rates, half, halo):
+    _, pops, rows, cols = rates.shape
+    before, after = halo[0, half], halo[1, half]
+    row = lax.broadcasted_iota(jnp.int32, (rows, cols), 0)
+    lane = lax.broadcasted_iota(jnp.int32, (rows, cols), 1)
+    terms = []
+    for i in range(pops):
+        r = rates[half, i].astype(F32)
+        other = rates[1 - half, i].astype(F32)
+        east = jnp.where(lane == 0, other[:, cols - 1 :], pltpu.roll(r, 1, 1))
+        west = jnp.where(lane == cols - 1, other[:, :1], pltpu.roll(r, cols - 1, 1))
+        up = jnp.where(row == 0, before[i : i + 1], pltpu.roll(r, 1, 0))
+        down = jnp.where(row == rows - 1, after[i : i + 1], pltpu.roll(r, rows - 1, 0))
+        terms.append(east + west + up + down - 4.0 * r)
+    return terms
+
+
+def legendre_body(
+    spectrum, weight, mixing, basis, out, halo, held, arrived, even_s, odd_s, north_s, south_s
+):
+    groups, count, lanes = out.shape
+    tiles = even_s.shape[0]
+    _, half_lat, deg = basis.shape
+    pops = mixing.shape[0]
+    src = weight.shape[0]
+    cores = groups // (2 * src)
+    piece = half_lat // src
+    slots = lanes // piece
+    pops_here = slots // 2
+    pad = tiles * 128 - half_lat
+    block = 8
+    owner = lax.axis_index("band") * lax.axis_size("lon") + lax.axis_index("lon")
+    here_first = lax.axis_index("pop") * count
+    first_wave = owner * basis.shape[0] + here_first
+
+    def fetch(r):
+        return pltpu.make_async_copy(basis.at[here_first + r], held.at[r], arrived.at[r])
+
+    @pl.loop(0, count)
+    def _(r):
+        fetch(r).start()
+
+    _, southern, _, at_pole = here()
+    outward = jnp.where(southern, owner + 1, owner - 1)
+    inward = jnp.where(southern, owner - 1, owner + 1)
+    outward = jnp.where(at_pole, owner, outward)
+    for side, neighbour in ((0, outward), (1, inward)):
+        rows = spectrum[neighbour * cores + lax.axis_index("pop")].astype(F32)[count:]
+        if side == 0:
+            rows = jnp.where(at_pole, 0.0, rows)
+        for h in range(halo.shape[1]):
+            halo[side, h] = rows[h * halo.shape[2] : (h + 1) * halo.shape[2]]
+
+    def rows_of(p, q):
+        b = (q // pops_here) * pops + p * pops_here + q % pops_here
+        return slice(b * count, (b + 1) * count)
+
+    for p in range(cores):
+        evens, odds = [], []
+        for s in range(src):
+            north = spectrum[s * cores + p].astype(F32)[:count]
+            south = spectrum[(2 * src - 1 - s) * cores + p].astype(F32)[:count]
+            w = weight[s : s + 1]
+            evens.append((w * (north + south)).astype(BF16).astype(F32))
+            odds.append((w * (north - south)).astype(BF16).astype(F32))
+        for q in range(slots):
+            for parts, scratch in ((evens, even_s), (odds, odd_s)):
+                strips = [v[:, q * piece : (q + 1) * piece] for v in parts]
+                if pad:
+                    strips.append(jnp.zeros((count, pad), F32))
+                joined = jnp.concatenate(strips, axis=1)
+                for t in range(tiles):
+                    scratch[t, rows_of(p, q), :] = joined[:, t * 128 : (t + 1) * 128]
+
+    degree = lax.broadcasted_iota(jnp.int32, (2 * pops, deg), 1)
+
+    @pl.loop(0, count // block)
+    def _(step):
+        for at in range(block):
+            fetch(step * block + at).wait()
+        for at in range(block):
+            r = step * block + at
+            m = first_wave + r
+            rows = pl.ds(r, 2 * pops, stride=count)
+            lhs = jnp.concatenate(
+                [
+                    jnp.concatenate([scratch[t, rows, :] for t in range(tiles)], axis=1)
+                    for scratch in (even_s, odd_s)
+                ],
+                axis=0,
+            )[:, :half_lat].astype(BF16)
+            both = jnp.dot(lhs, held[r], preferred_element_type=F32)
+            odd = ((degree - m) & 1) == 1
+            coeffs = jnp.where(odd, both[2 * pops :], both[: 2 * pops])
+            coeffs = jnp.where(degree >= m, coeffs, 0.0)
+            mixed = []
+            for c in range(2):
+                total = None
+                for j in range(pops):
+                    term = mixing[j] * coeffs[c * pops + j : c * pops + j + 1]
+                    total = term if total is None else total + term
+                mixed.append(total)
+            mixed = jnp.concatenate(mixed, axis=0)
+            amplitude = jnp.where(m == 0, 1.0, 2.0)
+            lhs2 = jnp.concatenate([mixed, jnp.where(odd, -mixed, mixed)], axis=0).astype(BF16)
+            field = nt_dot(lhs2, held[r]) * amplitude
+            if pad:
+                field = jnp.concatenate([field, jnp.zeros((4 * pops, pad), F32)], axis=1)
+            for t in range(tiles):
+                north_s[t, rows, :] = field[: 2 * pops, t * 128 : (t + 1) * 128]
+                south_s[t, rows, :] = field[2 * pops :, t * 128 : (t + 1) * 128]
+
+    for scratch, south in ((north_s, False), (south_s, True)):
+        for p in range(cores):
+            wide = [
+                jnp.concatenate(
+                    [scratch[t, rows_of(p, q), :] for t in range(tiles)], axis=1
+                )
+                for q in range(slots)
+            ]
+            for s in range(src):
+                to = (2 * src - 1 - s if south else s) * cores + p
+                strips = [v[:, s * piece : (s + 1) * piece] for v in wide]
+                out[to] = jnp.concatenate(strips, axis=1).astype(BF16)
+
+
+def turned(spectrum, turned_s):
+    groups = spectrum.shape[0]
+    stacked = jnp.concatenate([spectrum[g].astype(F32) for g in range(groups)], axis=0)
+    turned_s[...] = stacked.T.astype(BF16)
+
+
+def synth_of(both, table, columns):
+    half = both.shape[0] // 2
+    total = None
+    for c in range(2):
+        term = jnp.dot(
+            both[c * half : (c + 1) * half, :], table[c, :, columns], preferred_element_type=F32
+        )
+        total = term if total is None else total + term
+    return total
+
+
+def middle_body(
+    params, table, spectrum, old, halo, kept, got, fourier, rates, inner, turned_s
+):
+    halves, pops, rows, cols = rates.shape
+    first = lax.axis_index("pop") * pops
+    turned(spectrum, turned_s)
+    for h in range(halves):
+        at = slice(h * cols, (h + 1) * cols)
+        synth = synth_of(turned_s, table, at) * (time_step / (halves * cols))
+        lateral = lateral_of(old, h, halo)
+        for i in range(pops):
+            v = synth[i * rows : (i + 1) * rows]
+            v = v + (time_step * params[3, first + i]) * lateral[i]
+            inner[i, :, at] = v
+            u = jnp.where(here()[0] == h, kept[i], got[i]).astype(F32) + v
+            rates[h, i] = rate_of(params, first + i, u)
+    fourier_of(table, rates, fourier)
+
+
+def put_inner(params, table, rates, halo, inner, both, half, out):
+    pops, rows, cols = out.shape
+    first = lax.axis_index("pop") * pops
+    at = pl.ds(pl.multiple_of(half * cols, 128), cols)
+    synth = synth_of(both, table, at) * (time_step / table.shape[2])
+    lateral = lateral_of(rates, half, halo)
+    for i in range(pops):
+        v = synth[i * rows : (i + 1) * rows]
+        v = v + (time_step * params[3, first + i]) * lateral[i]
+        v = v + (1.0 - time_step * params[2, first + i]) * inner[i, :, at]
+        out[i] = v.astype(BF16)
+
+
+def sent_inner_body(params, table, spectrum, rates, halo, inner, out, both):
+    turned(spectrum, both)
+    put_inner(params, table, rates, halo, inner, both, 1 - here()[0], out)
+
+
+def kept_inner_body(params, table, both, rates, halo, inner, out):
+    put_inner(params, table, rates, halo, inner, both, here()[0], out)
+
+
+def grid_update_body(params, act, drive, kept, got, out):
+    i = lax.axis_index("pop") * pl.num_programs(0) + pl.program_id(0)
+    keep = 1.0 - time_step * params[2, i]
+    rows = kept.shape[1]
+    lon = here()[0]
+    for half, inner in ((lon, kept), (1 - lon, got)):
+        d = time_step * half_of(drive, 0, half, rows).astype(F32)
+        at = pl.ds(pl.multiple_of(half * rows, 16), rows)
+        out[0, at, :] = keep * (keep * act[0, at, :] + d) + d + in_wire_order(inner[0])
+
+
+def by_parts(activity, drive, basis, kernels, conn_block, coupling, rate_params):
+    pops_here, lat_here, cols = activity.shape
+    owned, half_lat, deg = basis.shape
+    bands, lons, cores = (lax.axis_size(a) for a in ("band", "lon", "pop"))
+    owners = bands * lons
+    groups = owners * cores
+    count = owned // cores
+    rows = lat_here // lons
+    nlat, nlon = bands * lat_here, lons * cols
+    pops = pops_here * cores
+    lanes = 2 * pops_here * rows
+    band, lon, core = (lax.axis_index(a) for a in ("band", "lon", "pop"))
+    owner = band * lons + lon
+    table = jnp.asarray(fourier_table(nlon, deg))
+    weights = lat_weights(nlat).reshape(owners // 2, 1, rows)
+    weights = jnp.asarray(np.tile(weights, (1, 2 * pops_here, 1)).reshape(owners // 2, lanes))
+    onehot = (conn_block[..., None] == jnp.arange(kernels.shape[0], dtype=jnp.int32)).astype(F32)
+    mixing = coupling[..., None] * jnp.einsum(
+        "ijb,bn->ijn", onehot, kernels, precision=lax.Precision.HIGHEST
+    )
+    mixing = jnp.swapaxes(mixing, 0, 1)
+    swap = [(0, 1), (1, 0)]
+
+    by_pop = pl.BlockSpec((1, rows, cols), lambda i: (i, 0, 0))
+    on_grid = pl.BlockSpec((1, lat_here, cols), lambda i: (i, 0, 0))
+    piece = shape(pops_here, rows, cols)
+    wire = shape(groups, count, lanes)
+    wire_edge = shape(groups, count + pops_here * nlon // lanes, lanes)
+    ends = shape(2, lons, pops_here, cols, dtype=F32)
+    both_halves = shape(lons, pops_here, rows, cols)
+    state = shape(pops_here, rows, nlon, dtype=F32)
+
+    sent = call(
+        sent_rates_body,
+        piece,
+        60,
+        grid=(1,),
+        in_specs=[
+            scalars(),
+            pl.BlockSpec((pops_here, rows, cols), lambda i: (0, 1 - lax.axis_index("lon"), 0)),
+        ],
+        out_specs=pl.BlockSpec((pops_here, rows, cols), lambda i: (0, 0, 0)),
+    )(rate_params, activity)
+    got = lax.ppermute(sent, "lon", swap)
+    kept, carried_sent, carried_kept, part = call(
+        own_half_body,
+        (piece,) * 3 + (shape(deg, lanes, dtype=F32),),
+        24,
+        2 * 10**9,
+        10**7,
+        in_specs=[scalars()] + [whole()] * 3,
+        out_specs=(whole(),) * 4,
+    )(rate_params, table, activity, drive)
+    got, mixing = lax.optimization_barrier((got, mixing))
+    fourier, rates = call(
+        first_fourier_body,
+        (wire_edge, both_halves),
+        16,
+        in_specs=[whole()] * 4,
+        out_specs=(whole(),) * 2,
+    )(table, part, kept, got)
+
+    def coupled(fourier, *more):
+        spectrum = lax.all_to_all(fourier, EVERYONE, 0, 0, tiled=True)
+        spectrum, *more = lax.optimization_barrier((spectrum, *more))
+        more = [lax.ppermute(v, "lon", swap) for v in more]
+        tiles = -(-half_lat // 128)
+        scratch = pltpu.VMEM((tiles, 2 * pops * count, 128), F32)
+        synthesis, halo = call(
+            legendre_body,
+            (wire, ends),
+            40,
+            5 * 10**9,
+            2 * 10**7,
+            in_specs=[whole()] * 3 + [pl.BlockSpec(memory_space=pl.ANY)],
+            out_specs=(whole(),) * 2,
+            scratch_shapes=[
+                pltpu.VMEM((count, half_lat, deg), BF16),
+                pltpu.SemaphoreType.DMA((count,)),
+            ]
+            + [scratch] * 4,
+        )(spectrum, weights, mixing, basis)
+        synthesis, more = lax.optimization_barrier((synthesis, more))
+        back = lax.all_to_all(synthesis, EVERYONE, 0, 0, tiled=True)
+        return back, halo, more
+
+    back, halo, (carried_got,) = coupled(fourier, carried_sent)
+    both = shape(lanes, deg)
+    fourier, rates, inner = call(
+        middle_body,
+        (wire_edge, both_halves, state),
+        32,
+        in_specs=[scalars()] + [whole()] * 6,
+        out_specs=(whole(),) * 3,
+        scratch_shapes=[pltpu.VMEM(both.shape, BF16)],
+    )(rate_params, table, back, rates, halo, carried_kept, carried_got)
+    back, halo, _ = coupled(fourier)
+    sent, both = call(
+        sent_inner_body,
+        (piece, both),
+        24,
+        in_specs=[scalars()] + [whole()] * 5,
+        out_specs=(whole(),) * 2,
+    )(rate_params, table, back, rates, halo, inner)
+    got = lax.ppermute(sent, "lon", swap)
+    kept = call(
+        kept_inner_body,
+        piece,
+        16,
+        10**9,
+        5 * 10**6,
+        in_specs=[scalars()] + [whole()] * 5,
+        out_specs=whole(),
+    )(rate_params, table, both, rates, halo, inner)
+    return call(
+        grid_update_body,
+        shape(*activity.shape, dtype=F32),
+        24,
+        grid=(pops_here,),
+        in_specs=[scalars(), on_grid, on_grid, by_pop, by_pop],
+        out_specs=on_grid,
+    )(rate_params, activity, drive, kept, got)
 
 
 def with_halo(shard, sides, width):
@@ -27,18 +492,12 @@
     return shard
 
 
-def fourier_table():
-    longitude = jnp.arange(NLON, dtype=jnp.int32)
-    wavenumber = jnp.arange(DEG, dtype=jnp.int32)
-    phase = longitude[:, None] * wavenumber[None, :] % NLON
-    angle = phase.astype(jnp.float32) * (2.0 * math.pi / NLON)
+def plain_table(nlon, deg):
+    longitude = jnp.arange(nlon, dtype=jnp.int32)
+    wavenumber = jnp.arange(deg, dtype=jnp.int32)
+    phase = longitude[:, None] * wavenumber[None, :] % nlon
+    angle = phase.astype(jnp.float32) * (2.0 * math.pi / nlon)
     return jnp.stack([jnp.cos(angle), jnp.sin(angle)], axis=1).astype(jnp.bfloat16)
-
-
-def lat_weights():
-    row_index = jnp.arange(NLAT // 2, dtype=jnp.float32)
-    colatitude = math.pi * (4.0 * row_index + 3.0) / (4.0 * NLAT + 2.0)
-    return math.pi * jnp.sin(colatitude) / NLAT
 
 
 def to_owners(fourier):
@@ -49,23 +508,25 @@
     return lax.all_to_all(synthesis, ("band", "lon"), split_axis=3, concat_axis=2, tiled=True)
 
 
-def local(activity, drive, basis, kernels, conn_block, coupling, rate_params):
+def by_arrays(activity, drive, basis, kernels, conn_block, coupling, rate_params):
     pop_here = activity.shape[0]
     owned_count = basis.shape[0]
     half_lat = basis.shape[1]
-    quarter = DEG // 2
+    deg = basis.shape[2]
+    nlon = activity.shape[2] * lax.axis_size("lon")
+    quarter = deg // 2
     owner_index = lax.axis_index("band") * lax.axis_size("lon") + lax.axis_index("lon")
     pop_first = lax.axis_index("pop") * pop_here
     params = lax.dynamic_slice_in_dim(rate_params, pop_first, pop_here, 1)
     gain_row, thresh, decay_row, lateral = (params[0], params[1], params[2], params[3])
-    cos_sin = fourier_table()
-    weights = lat_weights()
+    cos_sin = plain_table(nlon, deg)
+    weights = jnp.asarray(lat_weights(2 * half_lat))
     wavenumber = owner_index * owned_count + jnp.arange(owned_count, dtype=jnp.int32)
-    degree = jnp.arange(DEG, dtype=jnp.int32)
+    degree = jnp.arange(deg, dtype=jnp.int32)
     triangle = degree[None, :] >= wavenumber[:, None]
     slots = jnp.arange(2, dtype=jnp.int32)
     parity_pick = (slots[None, :] == (wavenumber % 2)[:, None])[None, None, :, :, None]
-    every_wave = jnp.arange(DEG, dtype=jnp.int32)
+    every_wave = jnp.arange(deg, dtype=jnp.int32)
     amplitude = jnp.where(every_wave == 0, 1.0, 2.0).astype(jnp.bfloat16)
     coup_own = lax.dynamic_slice_in_dim(coupling, pop_first, pop_here, 0)
     block_own = lax.dynamic_slice_in_dim(conn_block, pop_first, pop_here, 0)
@@ -95,7 +556,7 @@
         coeffs = jnp.einsum(
             "icmsj,mjqs->icmqs", operand, basis_split, preferred_element_type=jnp.float32
         )
-        coeffs = coeffs.reshape(pop_here, 2, owned_count, DEG)
+        coeffs = coeffs.reshape(pop_here, 2, owned_count, deg)
         coeffs = jnp.where(triangle[None, None], coeffs, 0.0)
         gathered = lax.all_gather(coeffs.astype(jnp.bfloat16), "pop", axis=0, tiled=True).astype(
             coeffs.dtype
@@ -118,7 +579,7 @@
         scaled = returned * amplitude[None, None, :, None]
         synth_field = jnp.einsum(
             "icmj,kcm->ijk", scaled, cos_sin, preferred_element_type=jnp.float32
-        ) * (1.0 / NLON)
+        ) * (1.0 / nlon)
         padded = with_halo(lat_rows, ((("band", "lon"), 1),), 1).astype(jnp.float32)
         rates_f32 = lat_rows.astype(jnp.float32)
         lateral_term = (
@@ -138,6 +599,21 @@
 
 
 def solution(mesh):
+    bands, lons, cores = (mesh.shape[a] for a in ("band", "lon", "pop"))
+
+    def local(activity, drive, basis, *rest):
+        rows, owned = activity.shape[1] // lons, basis.shape[0]
+        fits = (
+            bands % 2 == 0
+            and lons == 2
+            and bands * lons * cores % 4 == 0
+            and owned % (8 * cores) == 0
+            and rows % 16 == 0
+            and activity.shape[2] % 128 == 0
+            and 2 * activity.shape[0] * rows % 128 == 0
+        )
+        return (by_parts if fits else by_arrays)(activity, drive, basis, *rest)
+
     in_specs = (
         P(("subj", "pop"), "band", "lon"),
         P(("subj", "pop"), "band", "lon"),

time: 541 us -> 176 us (0.33); the launches traced: 532 us -> 176 us
  local copies, waits for them, and re-layouts: 199 us -> 3.27 us
  matrix products: 90.8 us -> 0.29 us
  waiting for transfers between devices: 63.8 us -> 13 us
  Pallas kernels: 0 us -> 46.1 us
  other arithmetic: 43.2 us -> 0.01 us
  starting transfers between devices: 33.6 us -> 5.16 us
  blocking collectives: 86.8 us -> 108 us
  between operations: 14.2 us -> 0.11 us
    dot_general x9 -> x1, matrix products: 90.8 us -> 0.29 us  [by_parts(): jnp.einsum('ijb,bn->ijn', onehot, kernels, precision=lax.Precision.HIGHEST)]
    unnamed x43 -> x20, local copies, waits for them, and re-layouts: 70.9 us -> 3.11 us
    reshape x3 -> x0, local copies, waits for them, and re-layouts: 55.8 us -> none  [the longest x1 53.5 us: local(): basis_split = basis.reshape(owned_count, half_lat, quarter, 2)]
    pallas_call x0 -> x9, Pallas kernels: none -> 46.1 us  [the longest x2 27.6 us: coupled(): call(legendre_body, (wire, ends), 40, 5 * 10 ** 9, 2 * 10 ** 7, in_specs=...]
    all_to_all x4 -> x0, waiting for transfers between devices: 38 us -> none  [the longest x2 38 us: to_latitudes(): lax.all_to_all(synthesis, ('band', 'lon'), split_axis=3, concat_axis=2, t...]
    convert_element_type x16 -> x0, local copies, waits for them, and re-layouts: 30.7 us -> none  [the longest x4 10.1 us: local(): jnp.sum(mixing[:, :, None, None, :] * gathered[None], axis=1)]
    all_to_all x4 -> x0, starting transfers between devices: 22.9 us -> none  [the longest x2 11.5 us: to_latitudes(): lax.all_to_all(synthesis, ('band', 'lon'), split_axis=3, concat_axis=2, t...]
    all_to_all x4, blocking collectives: 86.8 us -> 108 us  [the longest x2 57.2 us: coupled(): spectrum = lax.all_to_all(fourier, EVERYONE, 0, 0, tiled=True)]
  transfers between devices with their start and end apart: 10 -> 3, of which waited for: 8 -> 2; matrix products, arithmetic and copies ran while one was open for 24% -> 0% of each run, Pallas kernels for 0% -> 10%
where the time goes in v2:
time: 176 us
  blocking collectives  108 us (61%)
  Pallas kernels  46.1 us (26%)
  waiting for transfers between devices  13 us (7%)
  starting transfers between devices  5.16 us (3%)
  local copies, waits for them, and re-layouts  3.27 us (2%)
    all_to_all x2, blocking collectives, coupled(): spectrum = lax.all_to_all(fourier, EVERYONE, 0, 0, tiled=True)  57.2 us
    all_to_all x2, blocking collectives, coupled(): back = lax.all_to_all(synthesis, EVERYONE, 0, 0, tiled=True)  50.5 us
    pallas_call x2, Pallas kernels, coupled(): call(legendre_body, (wire, ends), 40, 5 * 10 ** 9, 2 * 10 ** 7, in_specs=...  27.6 us
    ppermute x2, waiting for transfers between devices, by_parts(): got = lax.ppermute(sent, 'lon', swap)  13 us
    pallas_call x1, Pallas kernels, by_parts(): call(middle_body, (wire_edge, both_halves, state), 32, in_specs=[scalars(...  5.69 us
    ppermute x2, starting transfers between devices, by_parts(): got = lax.ppermute(sent, 'lon', swap)  3.98 us
  transfers between devices with their start and end apart: 3, of which 2 were waited for; matrix products, arithmetic and copies ran while one was open for 0% of the time, Pallas kernels for 10%

profile of v2, /device:TPU:0, one launch (start us, length us, event | category | flops | bytes accessed | tf_op | source)
XLA Modules:
  0.0 175.6 jit_solution(1570048915645577238)
XLA Ops:
  0.0 0.0 copy-start
  0.0 0.0 copy-start.6
  0.0 0.0 copy-start.3
  0.0 0.0 copy-start.8
  0.0 0.0 copy-start.9
  0.0 2.4 %shard_map.92 = bf16[4,80,640]{2,1,0:T(8,128)(2,1)} custom-call(f32[4,8]{1,0:T(4,128)} %params.11, f32[4,160,640]{2,1,0:T(8,128)} %act.5), custom_call_target="tpu_custom_call" | custom-call | tf_op jit(solution)/shard_map/pallas_call | solution.py:390
  2.4 2.9 %collective-permute-start = (bf16[4,80,640]{2,1,0:T(8,128)(2,1)}, bf16[4,80,640]{2,1,0:T(8,128)(2,1)S(1)}, u32[]{:S(2)}, u32[]{:S(2)}) collective-permute-start(bf16[4,80,640]{2,1,0:T(8,128)(2,1)} %shard_map.92), channel_id=1, source_target_pairs={{0,2},{2,0},{1,3},{3,1},{4,6},{6,4},{5,7},{7,5},{8,10},{10,8},{9,1... | collective-permute-start | bytes 1228808 | tf_op jit(solution)/shard_map/ppermute | solution.py:401
  5.3 0.0 copy-done.8
  5.3 0.1 copy.12
  5.4 0.0 copy-done.9
  5.4 0.1 copy.10
  5.5 0.0 copy-done.6
  5.5 0.0 copy-done.3
  5.5 0.0 copy-start.1
  5.5 1.9 %copy-done.1 = bf16[2,640,1280]{2,1,0:T(8,128)(2,1)S(1)} copy-done((bf16[2,640,1280]{2,1,0:T(8,128)(2,1)S(1)}, bf16[2,640,1280]{2,1,0:T(8,128)(2,1)}, u32[]{:S(2)}) %copy-start.1) | copy-done | bytes 3276824
  7.4 0.0 copy-start.4
  7.4 1.1 copy-done.4
  8.6 2.6 %shard_map.91 = (bf16[4,80,640]{2,1,0:T(8,128)(2,1)S(1)}, bf16[4,80,640]{2,1,0:T(8,128)(2,1)S(1)}, bf16[4,80,640]{2,1,0:T(8,128)(2,1)S(1)}, f32[640,640]{1,0:T(8,128)S(1)}) custom-call(f32[4,8]{1,0:T(4,128)S(1)} %copy-done.6, bf16[2,640,1280]{2,1,0:T(8,128)(2,1)S(1)} %copy-done.1, f32[4,160,640]{2,1,0:T(8,128)S(1)} %copy-done.3, ...), custom_call_target="tpu_custom_call" | custom-call | flops 2000000000 | bytes 10000000 | tf_op jit(solution)/shard_map/pallas_call | solution.py:402
  11.2 0.0 copy-done
  11.2 0.3 fusion.mixing
  11.5 3.5 %collective-permute-done.got = bf16[4,80,640]{2,1,0:T(8,128)(2,1)S(1)} collective-permute-done((bf16[4,80,640]{2,1,0:T(8,128)(2,1)}, bf16[4,80,640]{2,1,0:T(8,128)(2,1)S(1)}, u32[]{:S(2)}, u32[]{:S(2)}) %collective-permute-start) | collective-permute-done | bytes 409632 | tf_op jit(solution)/shard_map/ppermute | solution.py:401
  15.0 1.6 shard_map.93
  16.6 0.0 copy-start.7
  16.6 29.7 %all_to_all.20.spectrum = bf16[16,48,640]{2,1,0:T(8,128)(2,1)S(1)} all-to-all(bf16[16,48,640]{2,1,0:T(8,128)(2,1)S(1)} %get-tuple-element.29), channel_id=1, replica_groups=mesh['subj'=2,'band'=4,'lon'=2,'pop'=2] {'band','lon','pop'}, dimensions={0} | all-to-all | bytes 1966080 | tf_op jit(solution)/shard_map/all_to_all | solution.py:421
  46.3 1.2 collective-permute-start.1
  47.4 0.0 copy-done.7
  47.4 0.0 copy-start.2
  47.4 13.9 %shard_map.94 = (bf16[16,40,640]{2,1,0:T(8,128)(2,1)S(1)}, f32[2,2,4,640]{3,2,1,0:T(4,128)S(1)}) custom-call(bf16[16,48,640]{2,1,0:T(8,128)(2,1)S(1)} %all_to_all.20.spectrum, f32[4,640]{1,0:T(4,128)S(1)} %copy-done.7, f32[8,8,640]{2,1,0:T(8,128)S(1)} %fusion.mixing, bf16[80,320,640]{2,1,0:T(8,128)(2,1)} %basis.3), custom_call_target="tpu_custom_call" | custom-call | flops 5000000000 | bytes 20000000 | tf_op jit(solution)/shard_map/pallas_call | solution.py:426
  61.3 0.0 collective-permute-done.1.got
  61.4 25.2 %all_to_all.21.spectrum = bf16[16,40,640]{2,1,0:T(8,128)(2,1)S(1)} all-to-all(bf16[16,40,640]{2,1,0:T(8,128)(2,1)S(1)} %get-tuple-element.35), channel_id=1, replica_groups=mesh['subj'=2,'band'=4,'lon'=2,'pop'=2] {'band','lon','pop'}, dimensions={0} | all-to-all | bytes 1638400 | tf_op jit(solution)/shard_map/all_to_all | solution.py:441
  86.5 0.0 copy-done.2
  86.5 5.7 %shard_map.95 = (bf16[16,48,640]{2,1,0:T(8,128)(2,1)S(1)}, bf16[2,4,80,640]{3,2,1,0:T(8,128)(2,1)S(1)}, f32[4,80,1280]{2,1,0:T(8,128)S(1)}) custom-call(f32[4,8]{1,0:T(4,128)S(1)} %copy-done.6, bf16[2,640,1280]{2,1,0:T(8,128)(2,1)S(1)} %copy-done.2, bf16[16,40,640]{2,1,0:T(8,128)(2,1)S(1)} %all_to_all.21.spectrum, ...), custom_call_target="tpu_custom_call" | custom-call | tf_op jit(solution)/shard_map/pallas_call | solution.py:446
  92.2 27.6 %all_to_all.22.spectrum = bf16[16,48,640]{2,1,0:T(8,128)(2,1)S(1)} all-to-all(bf16[16,48,640]{2,1,0:T(8,128)(2,1)S(1)} %get-tuple-element.40), channel_id=1, replica_groups=mesh['subj'=2,'band'=4,'lon'=2,'pop'=2] {'band','lon','pop'}, dimensions={0} | all-to-all | bytes 1966080 | tf_op jit(solution)/shard_map/all_to_all | solution.py:421
  119.8 13.7 %shard_map.96 = (bf16[16,40,640]{2,1,0:T(8,128)(2,1)S(1)}, f32[2,2,4,640]{3,2,1,0:T(4,128)S(1)}) custom-call(bf16[16,48,640]{2,1,0:T(8,128)(2,1)S(1)} %all_to_all.22.spectrum, f32[4,640]{1,0:T(4,128)S(1)} %copy-done.7, f32[8,8,640]{2,1,0:T(8,128)S(1)} %fusion.mixing, bf16[80,320,640]{2,1,0:T(8,128)(2,1)} %basis.3), custom_call_target="tpu_custom_call" | custom-call | flops 5000000000 | bytes 20000000 | tf_op jit(solution)/shard_map/pallas_call | solution.py:426
  133.5 25.4 %all_to_all.23.spectrum = bf16[16,40,640]{2,1,0:T(8,128)(2,1)S(1)} all-to-all(bf16[16,40,640]{2,1,0:T(8,128)(2,1)S(1)} %get-tuple-element.41), channel_id=1, replica_groups=mesh['subj'=2,'band'=4,'lon'=2,'pop'=2] {'band','lon','pop'}, dimensions={0} | all-to-all | bytes 1638400 | tf_op jit(solution)/shard_map/all_to_all | solution.py:441
  158.9 1.8 %shard_map.97 = (bf16[4,80,640]{2,1,0:T(8,128)(2,1)S(1)}, bf16[640,640]{1,0:T(8,128)(2,1)S(1)}) custom-call(f32[4,8]{1,0:T(4,128)S(1)} %copy-done.6, bf16[2,640,1280]{2,1,0:T(8,128)(2,1)S(1)} %copy-done.2, bf16[16,40,640]{2,1,0:T(8,128)(2,1)S(1)} %all_to_all.23.spectrum, bf16[2,4,80,640]{3,2,1,0:T(8,128)(2,1)S(1)} %get-tuple-element.42.rates, ...), custom_call_target="tpu_custom_call" | custom-call | tf_op jit(solution)/shard_map/pallas_call | solution.py:455
  160.7 1.0 collective-permute-start.2
  161.7 0.0 copy-start.5
  161.7 1.7 shard_map.98.kept
  163.4 9.5 %collective-permute-done.2.got = bf16[4,80,640]{2,1,0:T(8,128)(2,1)S(1)} collective-permute-done((bf16[4,80,640]{2,1,0:T(8,128)(2,1)S(1)}, bf16[4,80,640]{2,1,0:T(8,128)(2,1)S(1)}, u32[]{:S(2)}, u32[]{:S(2)}) %collective-permute-start.2) | collective-permute-done | bytes 409632 | tf_op jit(solution)/shard_map/ppermute | solution.py:462
  172.9 0.0 copy-done.5
  172.9 2.7 %shard_map.99 = f32[4,160,640]{2,1,0:T(8,128)} custom-call(f32[4,8]{1,0:T(4,128)S(1)} %copy-done.6, f32[4,160,640]{2,1,0:T(8,128)S(1)} %copy-done.3, bf16[4,160,640]{2,1,0:T(8,128)(2,1)S(1)} %copy-done.5, bf16[4,80,640]{2,1,0:T(8,128)(2,1)S(1)} %shard_map.98.kept, bf16[4,80,640]{2,1,0:T(8,128)(2,1)S(1)} %collective-permute-done.2.got), custom_call_target="tpu_custom_call" | custom-call | tf_op jit(solution)/shard_map/pallas_call | solution.py:472
  (1 shorter events, 0.0 us)
Async XLA Ops:
  0.0 11.2 %copy-start = (f32[4,640]{1,0:T(4,128)S(1)}, f32[4,640]{1,0:T(4,128)}, u32[]{:S(2)}) copy-start(f32[4,640]{1,0:T(4,128)} %param.12) | copy-start | bytes 30724
  0.0 5.5 %copy-start.6 = (f32[4,8]{1,0:T(4,128)S(1)}, f32[4,8]{1,0:T(4,128)}, u32[]{:S(2)}) copy-start(f32[4,8]{1,0:T(4,128)} %params.11) | copy-start | bytes 388
  0.0 5.5 %copy-start.3 = (f32[4,160,640]{2,1,0:T(8,128)S(1)}, f32[4,160,640]{2,1,0:T(8,128)}, u32[]{:S(2)}) copy-start(f32[4,160,640]{2,1,0:T(8,128)} %act.5) | copy-start | bytes 4915204
  0.0 5.3 %copy-start.8 = (s32[8,8]{1,0:T(8,128)S(1)}, s32[8,8]{1,0:T(8,128)}, u32[]{:S(2)}) copy-start(s32[8,8]{1,0:T(8,128)} %param.13) | copy-start | bytes 772
  0.0 5.4 %copy-start.9 = (f32[8,8]{1,0:T(8,128)S(1)}, f32[8,8]{1,0:T(8,128)}, u32[]{:S(2)}) copy-start(f32[8,8]{1,0:T(8,128)} %param.14) | copy-start | bytes 772
  2.4 12.6 %collective-permute-start = (bf16[4,80,640]{2,1,0:T(8,128)(2,1)}, bf16[4,80,640]{2,1,0:T(8,128)(2,1)S(1)}, u32[]{:S(2)}, u32[]{:S(2)}) collective-permute-start(bf16[4,80,640]{2,1,0:T(8,128)(2,1)} %shard_map.92), channel_id=1, source_target_pairs={{0,2},{2,0},{1,3},{3,1},{4,6},{6,4},{5,7},{7,5},{8,10},{10,8},{9,1... | collective-permute-start | bytes 1228808 | tf_op jit(solution)/shard_map/ppermute | solution.py:401
  5.5 1.9 %copy-start.1 = (bf16[2,640,1280]{2,1,0:T(8,128)(2,1)S(1)}, bf16[2,640,1280]{2,1,0:T(8,128)(2,1)}, u32[]{:S(2)}) copy-start(bf16[2,640,1280]{2,1,0:T(8,128)(2,1)} %constant.4.clone.table) | copy-start | bytes 9830404
  7.4 1.1 copy-start.4
  16.6 30.9 %copy-start.7 = (f32[4,640]{1,0:T(4,128)S(1)}, f32[4,640]{1,0:T(4,128)}, u32[]{:S(2)}) copy-start(f32[4,640]{1,0:T(4,128)} %constant.5.clone.weight) | copy-start | bytes 30724
  46.3 15.1 %collective-permute-start.1 = (bf16[4,80,640]{2,1,0:T(8,128)(2,1)S(1)}, bf16[4,80,640]{2,1,0:T(8,128)(2,1)S(1)}, u32[]{:S(2)}, u32[]{:S(2)}) collective-permute-start(bf16[4,80,640]{2,1,0:T(8,128)(2,1)S(1)} %get-tuple-element.34), channel_id=1, source_target_pairs={{0,2},{2,0},{1,3},{3,1},{4,6},{6,4},{5,7},{7,5},{8,10},{10,8},{9,1... | collective-permute-start | bytes 1228808 | tf_op jit(solution)/shard_map/ppermute | solution.py:423
  47.4 39.1 %copy-start.2 = (bf16[2,640,1280]{2,1,0:T(8,128)(2,1)S(1)}, bf16[2,640,1280]{2,1,0:T(8,128)(2,1)}, u32[]{:S(2)}) copy-start(bf16[2,640,1280]{2,1,0:T(8,128)(2,1)} %constant.4.clone.table) | copy-start | bytes 9830404
  160.7 12.2 %collective-permute-start.2 = (bf16[4,80,640]{2,1,0:T(8,128)(2,1)S(1)}, bf16[4,80,640]{2,1,0:T(8,128)(2,1)S(1)}, u32[]{:S(2)}, u32[]{:S(2)}) collective-permute-start(bf16[4,80,640]{2,1,0:T(8,128)(2,1)S(1)} %get-tuple-element.46), channel_id=1, source_target_pairs={{0,2},{2,0},{1,3},{3,1},{4,6},{6,4},{5,7},{7,5},{8,10},{10,8},{9,1... | collective-permute-start | bytes 1228808 | tf_op jit(solution)/shard_map/ppermute | solution.py:462
  161.7 11.2 %copy-start.5 = (bf16[4,160,640]{2,1,0:T(8,128)(2,1)S(1)}, bf16[4,160,640]{2,1,0:T(8,128)(2,1)}, u32[]{:S(2)}) copy-start(bf16[4,160,640]{2,1,0:T(8,128)(2,1)} %drive.3) | copy-start | bytes 2457604

commit v3 on v2

--- a/solution.py
+++ b/solution.py
@@ -82,9 +82,11 @@
     return ref[lead, pl.ds(pl.multiple_of(half * rows, 16), rows), :]
 
 
-def sent_rates_body(params, act, rates):
-    first = lax.axis_index("pop") * act.shape[0]
-    for i in range(act.shape[0]):
+def sent_rates_body(begin, params, act, rates):
+    count = act.shape[0]
+    pops = params.shape[1] // lax.axis_size("pop")
+    first = lax.axis_index("pop") * pops + begin
+    for i in range(count):
         rates[i] = in_wire_order(rate_of(params, first + i, act[i])).astype(BF16)
 
 
@@ -119,29 +121,55 @@
     return jnp.concatenate(parts, axis=1)
 
 
+def edge_slots(pops, nlon, groups):
+    return -(-pops * (nlon // 128) // groups)
+
+
+def wire_rows(count, lanes, slots):
+    return -(-(count * (lanes // 128) + 2 * slots) // 16) * 16
+
+
+def packed(sums, extra, total):
+    parts = [sums[:, t * 128 : (t + 1) * 128] for t in range(sums.shape[1] // 128)] + extra
+    missing = total - sum(v.shape[0] for v in parts)
+    if missing:
+        parts.append(jnp.zeros((missing, 128), F32))
+    return jnp.concatenate(parts, axis=0).astype(BF16)
+
+
+def unpacked(block, count, lanes):
+    block = block.astype(F32)
+    parts = [block[t * count : (t + 1) * count] for t in range(lanes // 128)]
+    return jnp.concatenate(parts, axis=1)
+
+
 def put_fourier(table, columns, flat, rates, fourier, part=None):
     halves, pops, rows, cols = rates.shape
-    groups, total, lanes = fourier.shape
-    extra = halves * pops * cols // lanes
-    count = total - extra
+    groups, total, _ = fourier.shape
+    lanes = 2 * pops * rows
+    count = table.shape[1] // groups
+    slots = edge_slots(pops, halves * cols, groups)
     pack = 4
     block = pack * count
-    strips = [rates[h, i].astype(F32) for h in range(halves) for i in range(pops)]
-    polar = jnp.concatenate([v[0:1] for v in strips], axis=0)
-    inner = jnp.concatenate([v[rows - 1 : rows] for v in strips], axis=0)
-    _, southern, _, _ = here()
-    owner = lax.axis_index("band") * lax.axis_size("lon") + lax.axis_index("lon")
-    poleward = jnp.where(southern, owner + 1, owner - 1)
-    cores = lax.axis_size("pop")
+    polar, inner = [], []
+    for i in range(pops):
+        for h in range(halves):
+            strip = rates[h, i].astype(F32)
+            for t in range(cols // 128):
+                at = slice(t * 128, (t + 1) * 128)
+                polar.append(strip[:1, at])
+                inner.append(strip[rows - 1 :, at])
+    nothing = [jnp.zeros((1, 128), F32)] * (slots * groups - len(polar))
+    polar, inner = polar + nothing, inner + nothing
     for b in range(groups // pack):
         joined = joined_fourier(table, b * block, block, columns, flat)
         if part is not None:
             joined = joined + part[b * block : (b + 1) * block]
         for g in range(pack):
             to = b * pack + g
-            edge = jnp.where(poleward == to // cores, polar, inner)
+            at = slice(to * slots, (to + 1) * slots)
             sums = joined[g * count : (g + 1) * count]
-            fourier[to] = jnp.concatenate([sums, edge], axis=0).astype(BF16)
+            fourier[to] = packed(sums, polar[at] + inner[at], total)
 
 
 def fourier_of(table, rates, fourier):
@@ -151,22 +179,25 @@
     put_fourier(table, columns, flat, rates, fourier)
 
 
-def first_fourier_body(table, part, kept, got, fourier, rates):
-    pops, rows, cols = got.shape
+def first_fourier_body(table, part, kept, got, got_more, fourier, rates):
+    some, _, cols = got.shape
     lon = here()[0]
     rates[lon] = kept[...]
-    rates[1 - lon] = got[...]
+    rates[1 - lon, :some] = got[...]
+    rates[1 - lon, some:] = got_more[...]
     columns = [pl.ds(pl.multiple_of((1 - lon) * cols, 128), cols)]
-    put_fourier(table, columns, [got[...].reshape(pops * rows, cols)], rates, fourier, part)
-
-
-def lateral_of(rates, half, halo):
+    there = [v[...].reshape(-1, cols) for v in (got, got_more)]
+    flat = [jnp.concatenate(there, axis=0)]
+    put_fourier(table, columns, flat, rates, fourier, part)
+
+
+def lateral_of(rates, half, halo, some=None):
     _, pops, rows, cols = rates.shape
     before, after = halo[0, half], halo[1, half]
     row = lax.broadcasted_iota(jnp.int32, (rows, cols), 0)
     lane = lax.broadcasted_iota(jnp.int32, (rows, cols), 1)
     terms = []
-    for i in range(pops):
+    for i in some or range(pops):
         r = rates[half, i].astype(F32)
         other = rates[1 - half, i].astype(F32)
         east = jnp.where(lane == 0, other[:, cols - 1 :], pltpu.roll(r, 1, 1))
@@ -178,17 +209,20 @@
 
 
 def legendre_body(
-    spectrum, weight, mixing, basis, out, halo, held, arrived, even_s, odd_s, north_s, south_s
+    nlon, spectrum, weight, mixing, basis, out, held, arrived, even_s, odd_s, north_s, south_s
 ):
-    groups, count, lanes = out.shape
+    groups, total, _ = out.shape
+    count = held.shape[0]
+    lanes = weight.shape[1]
     tiles = even_s.shape[0]
     _, half_lat, deg = basis.shape
     pops = mixing.shape[0]
     src = weight.shape[0]
     cores = groups // (2 * src)
     piece = half_lat // src
-    slots = lanes // piece
-    pops_here = slots // 2
+    lots = lanes // piece
+    pops_here = lots // 2
+    slots = edge_slots(pops_here, nlon, groups)
     pad = tiles * 128 - half_lat
     block = 8
     owner = lax.axis_index("band") * lax.axis_size("lon") + lax.axis_index("lon")
@@ -202,16 +236,21 @@
     def _(r):
         fetch(r).start()
 
-    _, southern, _, at_pole = here()
-    outward = jnp.where(southern, owner + 1, owner - 1)
-    inward = jnp.where(southern, owner - 1, owner + 1)
-    outward = jnp.where(at_pole, owner, outward)
-    for side, neighbour in ((0, outward), (1, inward)):
-        rows = spectrum[neighbour * cores + lax.axis_index("pop")].astype(F32)[count:]
-        if side == 0:
-            rows = jnp.where(at_pole, 0.0, rows)
-        for h in range(halo.shape[1]):
-            halo[side, h] = rows[h * halo.shape[2] : (h + 1) * halo.shape[2]]
+    wide = lanes // 128 * count
+    pieces = [spectrum[g].astype(F32)[wide:] for g in range(groups)]
+    passed = []
+    for to in range(2 * src):
+        step = 1 if to < src else -1
+        outward, inward = to - step, to + step
+        crossing = to in (src - 1, src)
+        for p in range(cores):
+            if 0 <= outward < 2 * src:
+                before = pieces[outward * cores + p][slots : 2 * slots]
+            else:
+                before = jnp.zeros((slots, 128), F32)
+            after = pieces[inward * cores + p]
+            after = after[slots : 2 * slots] if crossing else after[:slots]
+            passed.append([before, after])
 
     def rows_of(p, q):
         b = (q // pops_here) * pops + p * pops_here + q % pops_here
@@ -220,12 +259,12 @@
     for p in range(cores):
         evens, odds = [], []
         for s in range(src):
-            north = spectrum[s * cores + p].astype(F32)[:count]
-            south = spectrum[(2 * src - 1 - s) * cores + p].astype(F32)[:count]
+            north = unpacked(spectrum[s * cores + p], count, lanes)
+            south = unpacked(spectrum[(2 * src - 1 - s) * cores + p], count, lanes)
             w = weight[s : s + 1]
             evens.append((w * (north + south)).astype(BF16).astype(F32))
             odds.append((w * (north - south)).astype(BF16).astype(F32))
-        for q in range(slots):
+        for q in range(lots):
             for parts, scratch in ((evens, even_s), (odds, odd_s)):
                 strips = [v[:, q * piece : (q + 1) * piece] for v in parts]
                 if pad:
@@ -278,37 +317,61 @@
                 jnp.concatenate(
                     [scratch[t, rows_of(p, q), :] for t in range(tiles)], axis=1
                 )
-                for q in range(slots)
+                for q in range(lots)
             ]
             for s in range(src):
                 to = (2 * src - 1 - s if south else s) * cores + p
                 strips = [v[:, s * piece : (s + 1) * piece] for v in wide]
-                out[to] = jnp.concatenate(strips, axis=1).astype(BF16)
+                out[to] = packed(jnp.concatenate(strips, axis=1), passed[to], total)
 
 
 def turned(spectrum, turned_s):
     groups = spectrum.shape[0]
-    stacked = jnp.concatenate([spectrum[g].astype(F32) for g in range(groups)], axis=0)
-    turned_s[...] = stacked.T.astype(BF16)
-
-
-def synth_of(both, table, columns):
+    lanes, deg = turned_s.shape
+    blocks = [unpacked(spectrum[g], deg // groups, lanes) for g in range(groups)]
+    turned_s[...] = jnp.concatenate(blocks, axis=0).T.astype(BF16)
+
+
+def put_ends(spectrum, turned_s, halo):
+    groups = spectrum.shape[0]
+    lanes, deg = turned_s.shape
+    _, halves, pops, cols = halo.shape
+    slots = edge_slots(pops, halves * cols, groups)
+    wide = lanes // 128 * (deg // groups)
+    pieces = [spectrum[g].astype(F32)[wide:] for g in range(groups)]
+    per = cols // 128
+    for side in range(2):
+        for i in range(pops):
+            for h in range(halves):
+                for t in range(per):
+                    at = (i * halves + h) * per + t
+                    row = side * slots + at % slots
+                    halo[side, h, i : i + 1, t * 128 : (t + 1) * 128] = pieces[at // slots][
+                        row : row + 1
+                    ]
+
+
+def synth_of(both, table, columns, first=0, count=None):
     half = both.shape[0] // 2
+    count = half if count is None else count
     total = None
     for c in range(2):
         term = jnp.dot(
-            both[c * half : (c + 1) * half, :], table[c, :, columns], preferred_element_type=F32
+            both[c * half + first : c * half + first + count, :],
+            table[c, :, columns],
+            preferred_element_type=F32,
         )
         total = term if total is None else total + term
     return total
 
 
 def middle_body(
-    params, table, spectrum, old, halo, kept, got, fourier, rates, inner, turned_s
+    params, table, spectrum, old, kept, got, fourier, rates, inner, turned_s, halo
 ):
     halves, pops, rows, cols = rates.shape
     first = lax.axis_index("pop") * pops
     turned(spectrum, turned_s)
+    put_ends(spectrum, turned_s, halo)
     for h in range(halves):
         at = slice(h * cols, (h + 1) * cols)
         synth = synth_of(turned_s, table, at) * (time_step / (halves * cols))
@@ -322,30 +385,38 @@
     fourier_of(table, rates, fourier)
 
 
-def put_inner(params, table, rates, halo, inner, both, half, out):
-    pops, rows, cols = out.shape
+def put_inner(params, table, rates, halo, inner, both, half, some, out):
+    _, pops, rows, cols = rates.shape
     first = lax.axis_index("pop") * pops
     at = pl.ds(pl.multiple_of(half * cols, 128), cols)
-    synth = synth_of(both, table, at) * (time_step / table.shape[2])
-    lateral = lateral_of(rates, half, halo)
-    for i in range(pops):
-        v = synth[i * rows : (i + 1) * rows]
-        v = v + (time_step * params[3, first + i]) * lateral[i]
+    synth = synth_of(both, table, at, some[0] * rows, len(some) * rows)
+    synth = synth * (time_step / table.shape[2])
+    lateral = lateral_of(rates, half, halo, some)
+    for k, i in enumerate(some):
+        v = synth[k * rows : (k + 1) * rows]
+        v = v + (time_step * params[3, first + i]) * lateral[k]
         v = v + (1.0 - time_step * params[2, first + i]) * inner[i, :, at]
-        out[i] = v.astype(BF16)
-
-
-def sent_inner_body(params, table, spectrum, rates, halo, inner, out, both):
+        out[k] = v.astype(BF16)
+
+
+def sent_inner_body(some, params, table, spectrum, rates, inner, out, both, halo):
     turned(spectrum, both)
-    put_inner(params, table, rates, halo, inner, both, 1 - here()[0], out)
-
-
-def kept_inner_body(params, table, both, rates, halo, inner, out):
-    put_inner(params, table, rates, halo, inner, both, here()[0], out)
-
-
-def grid_update_body(params, act, drive, kept, got, out):
-    i = lax.axis_index("pop") * pl.num_programs(0) + pl.program_id(0)
+    put_ends(spectrum, both, halo)
+    put_inner(params, table, rates, halo, inner, both, 1 - here()[0], some, out)
+
+
+def more_inner_body(some, params, table, both, rates, halo, inner, out):
+    put_inner(params, table, rates, halo, inner, both, 1 - here()[0], some, out)
+
+
+def kept_inner_body(some, params, table, both, rates, halo, inner, out):
+    put_inner(params, table, rates, halo, inner, both, here()[0], some, out)
+
+
+def grid_update_body(begin, params, act, drive, kept, got, *refs):
+    out = refs[-1]
+    pops = begin + pl.num_programs(0) if begin else 2 * pl.num_programs(0)
+    i = lax.axis_index("pop") * pops + begin + pl.program_id(0)
     keep = 1.0 - time_step * params[2, i]
     rows = kept.shape[1]
     lon = here()[0]
@@ -381,24 +452,27 @@
     by_pop = pl.BlockSpec((1, rows, cols), lambda i: (i, 0, 0))
     on_grid = pl.BlockSpec((1, lat_here, cols), lambda i: (i, 0, 0))
     piece = shape(pops_here, rows, cols)
-    wire = shape(groups, count, lanes)
-    wire_edge = shape(groups, count + pops_here * nlon // lanes, lanes)
+    wire = shape(groups, wire_rows(count, lanes, edge_slots(pops_here, nlon, groups)), 128)
     ends = shape(2, lons, pops_here, cols, dtype=F32)
     both_halves = shape(lons, pops_here, rows, cols)
     state = shape(pops_here, rows, nlon, dtype=F32)
 
-    sent = call(
-        sent_rates_body,
-        piece,
-        60,
-        grid=(1,),
-        in_specs=[
-            scalars(),
-            pl.BlockSpec((pops_here, rows, cols), lambda i: (0, 1 - lax.axis_index("lon"), 0)),
-        ],
-        out_specs=pl.BlockSpec((pops_here, rows, cols), lambda i: (0, 0, 0)),
-    )(rate_params, activity)
-    got = lax.ppermute(sent, "lon", swap)
+    some = pops_here // 2
+    pairs = (list(range(some)), list(range(some, pops_here)))
+    got = []
+    for k, pair in enumerate(pairs):
+        sent = call(
+            functools.partial(sent_rates_body, pair[0]),
+            shape(some, rows, cols),
+            60,
+            grid=(1,),
+            in_specs=[
+                scalars(),
+                pl.BlockSpec((some, rows, cols), lambda i, k=k: (k, 1 - lax.axis_index("lon"), 0)),
+            ],
+            out_specs=pl.BlockSpec((some, rows, cols), lambda i: (0, 0, 0)),
+        )(rate_params, activity)
+        got.append(lax.ppermute(sent, "lon", swap))
     kept, carried_sent, carried_kept, part = call(
         own_half_body,
         (piece,) * 3 + (shape(deg, lanes, dtype=F32),),
@@ -408,14 +482,14 @@
         in_specs=[scalars()] + [whole()] * 3,
         out_specs=(whole(),) * 4,
     )(rate_params, table, activity, drive)
-    got, mixing = lax.optimization_barrier((got, mixing))
+    *got, mixing = lax.optimization_barrier((*got, mixing))
     fourier, rates = call(
         first_fourier_body,
-        (wire_edge, both_halves),
+        (wire, both_halves),
         16,
-        in_specs=[whole()] * 4,
+        in_specs=[whole()] * 5,
         out_specs=(whole(),) * 2,
-    )(table, part, kept, got)
+    )(table, part, kept, *got)
 
     def coupled(fourier, *more):
         spectrum = lax.all_to_all(fourier, EVERYONE, 0, 0, tiled=True)
@@ -423,14 +497,14 @@
         more = [lax.ppermute(v, "lon", swap) for v in more]
         tiles = -(-half_lat // 128)
         scratch = pltpu.VMEM((tiles, 2 * pops * count, 128), F32)
-        synthesis, halo = call(
-            legendre_body,
-            (wire, ends),
+        synthesis = call(
+            functools.partial(legendre_body, nlon),
+            wire,
             40,
             5 * 10**9,
             2 * 10**7,
             in_specs=[whole()] * 3 + [pl.BlockSpec(memory_space=pl.ANY)],
-            out_specs=(whole(),) * 2,
+            out_specs=whole(),
             scratch_shapes=[
                 pltpu.VMEM((count, half_lat, deg), BF16),
                 pltpu.SemaphoreType.DMA((count,)),
@@ -439,44 +513,68 @@
         )(spectrum, weights, mixing, basis)
         synthesis, more = lax.optimization_barrier((synthesis, more))
         back = lax.all_to_all(synthesis, EVERYONE, 0, 0, tiled=True)
-        return back, halo, more
-
-    back, halo, (carried_got,) = coupled(fourier, carried_sent)
+        return back, more
+
+    back, (carried_got,) = coupled(fourier, carried_sent)
     both = shape(lanes, deg)
     fourier, rates, inner = call(
         middle_body,
-        (wire_edge, both_halves, state),
+        (wire, both_halves, state),
         32,
-        in_specs=[scalars()] + [whole()] * 6,
+        in_specs=[scalars()] + [whole()] * 5,
         out_specs=(whole(),) * 3,
-        scratch_shapes=[pltpu.VMEM(both.shape, BF16)],
-    )(rate_params, table, back, rates, halo, carried_kept, carried_got)
-    back, halo, _ = coupled(fourier)
-    sent, both = call(
-        sent_inner_body,
-        (piece, both),
+        scratch_shapes=[pltpu.VMEM(both.shape, BF16), pltpu.VMEM(ends.shape, F32)],
+    )(rate_params, table, back, rates, carried_kept, carried_got)
+    back, _ = coupled(fourier)
+    sent, both, halo = call(
+        functools.partial(sent_inner_body, pairs[0]),
+        (shape(some, rows, cols), both, ends),
         24,
-        in_specs=[scalars()] + [whole()] * 5,
-        out_specs=(whole(),) * 2,
-    )(rate_params, table, back, rates, halo, inner)
-    got = lax.ppermute(sent, "lon", swap)
-    kept = call(
-        kept_inner_body,
-        piece,
-        16,
-        10**9,
-        5 * 10**6,
-        in_specs=[scalars()] + [whole()] * 5,
-        out_specs=whole(),
-    )(rate_params, table, both, rates, halo, inner)
-    return call(
-        grid_update_body,
-        shape(*activity.shape, dtype=F32),
-        24,
-        grid=(pops_here,),
-        in_specs=[scalars(), on_grid, on_grid, by_pop, by_pop],
-        out_specs=on_grid,
-    )(rate_params, activity, drive, kept, got)
+        in_specs=[scalars()] + [whole()] * 4,
+        out_specs=(whole(),) * 3,
+    )(rate_params, table, back, rates, inner)
+
+    def inner_of(body, some, count):
+        return call(
+            functools.partial(body, some),
+            shape(count, rows, cols),
+            16,
+            10**9,
+            5 * 10**6,
+            in_specs=[scalars()] + [whole()] * 5,
+            out_specs=whole(),
+        )(rate_params, table, both, rates, halo, inner)
+
+    got = [lax.ppermute(sent, "lon", swap)]
+    got.append(lax.ppermute(inner_of(more_inner_body, pairs[1], len(pairs[1])), "lon", swap))
+    kept = inner_of(kept_inner_body, pairs[0] + pairs[1], pops_here)
+    out = None
+    for pair, there in zip(pairs, got):
+        begin = pair[0]
+
+        def on(tail, begin=begin):
+            return pl.BlockSpec((1,) + tail, lambda i: (begin + i, 0, 0))
+
+        earlier = [] if out is None else [out]
+        out = call(
+            functools.partial(grid_update_body, begin),
+            shape(*activity.shape, dtype=F32),
+            24,
+            10**7,
+            4 * 10**6,
+            grid=(len(pair),),
+            in_specs=[
+                scalars(),
+                on((lat_here, cols)),
+                on((lat_here, cols)),
+                on((rows, cols)),
+                by_pop,
+            ]
+            + [pl.BlockSpec(memory_space=pl.ANY)] * len(earlier),
+            out_specs=on((lat_here, cols)),
+            input_output_aliases={5: 0} if earlier else {},
+        )(rate_params, activity, drive, kept, there, *earlier)
+    return out
 
 
 def with_halo(shard, sides, width):
@@ -605,6 +703,7 @@
         rows, owned = activity.shape[1] // lons, basis.shape[0]
         fits = (
             bands % 2 == 0
+            and activity.shape[0] % 2 == 0
             and lons == 2
             and bands * lons * cores % 4 == 0
             and owned % (8 * cores) == 0

time: 176 us -> 171 us (0.972)
  waiting for transfers between devices: 13 us -> 7.46 us
  Pallas kernels: 46.1 us -> 50.1 us
  blocking collectives: 108 us -> 104 us
    ppermute x2 -> x4, waiting for transfers between devices: 13 us -> 7.46 us  [the longest x1 2.92 us: by_parts(): got = [lax.ppermute(sent, 'lon', swap)]]
    all_to_all x2, blocking collectives: 57.2 us -> 52.8 us  [coupled(): spectrum = lax.all_to_all(fourier, EVERYONE, 0, 0, tiled=True)]
    pallas_call x8 -> x11, Pallas kernels: 43.5 us -> 47.5 us  [the longest x2 27.5 us: coupled(): call(functools.partial(legendre_body, nlon), wire, 40, 5 * 10 ** 9, 2 * 1...]
    ppermute x2 -> x4, starting transfers between devices: 3.98 us -> 5.08 us  [the longest x2 2.95 us: by_parts(): got.append(lax.ppermute(sent, 'lon', swap))]
  transfers between devices with their start and end apart: 3 -> 5, of which waited for: 2 -> 3; matrix products, arithmetic and copies ran while one was open for 0% -> 0% of each run, Pallas kernels for 10% -> 13%
where the time goes in v3:
time: 171 us
  blocking collectives  104 us (61%)
  Pallas kernels  50.1 us (29%)
  waiting for transfers between devices  7.46 us (4%)
  starting transfers between devices  6.08 us (4%)
  local copies, waits for them, and re-layouts  2.78 us (2%)
    all_to_all x2, blocking collectives, coupled(): spectrum = lax.all_to_all(fourier, EVERYONE, 0, 0, tiled=True)  52.8 us
    all_to_all x2, blocking collectives, coupled(): back = lax.all_to_all(synthesis, EVERYONE, 0, 0, tiled=True)  50.8 us
    pallas_call x2, Pallas kernels, coupled(): call(functools.partial(legendre_body, nlon), wire, 40, 5 * 10 ** 9, 2 * 1...  27.5 us
    pallas_call x1, Pallas kernels, by_parts(): call(middle_body, (wire, both_halves, state), 32, in_specs=[scalars()] +...  5.67 us
    pallas_call x2, Pallas kernels, by_parts(): call(functools.partial(sent_rates_body, pair[0]), shape(some, rows, cols)...  4.05 us
    pallas_call x2, Pallas kernels, by_parts(): call(functools.partial(grid_update_body, begin), shape(*activity.shape, d...  3.54 us
  transfers between devices with their start and end apart: 5, of which 3 were waited for; matrix products, arithmetic and copies ran while one was open for 0% of the time, Pallas kernels for 13%

profile of v3, /device:TPU:0, one launch (start us, length us, event | category | flops | bytes accessed | tf_op | source)
XLA Modules:
  0.0 170.5 jit_solution(7810748447275055444)
XLA Ops:
  0.0 0.0 copy-start
  0.0 0.0 copy-start.1
  0.0 0.0 copy-start.6
  0.0 0.0 copy-start.8
  0.0 0.0 copy-start.9
  0.0 2.1 %shard_map.92 = bf16[2,80,640]{2,1,0:T(8,128)(2,1)} custom-call(f32[4,8]{1,0:T(4,128)} %params.17, f32[4,160,640]{2,1,0:T(8,128)} %act.9), custom_call_target="tpu_custom_call" | custom-call | tf_op jit(solution)/shard_map/pallas_call | solution.py:464
  2.1 3.0 %collective-permute-start = (bf16[2,80,640]{2,1,0:T(8,128)(2,1)}, bf16[2,80,640]{2,1,0:T(8,128)(2,1)S(1)}, u32[]{:S(2)}, u32[]{:S(2)}) collective-permute-start(bf16[2,80,640]{2,1,0:T(8,128)(2,1)} %shard_map.92), channel_id=1, source_target_pairs={{0,2},{2,0},{1,3},{3,1},{4,6},{6,4},{5,7},{7,5},{8,10},{10,8},{9,1... | collective-permute-start | bytes 614408 | tf_op jit(solution)/shard_map/ppermute | solution.py:475
  5.1 1.9 %shard_map.93 = bf16[2,80,640]{2,1,0:T(8,128)(2,1)} custom-call(f32[4,8]{1,0:T(4,128)} %params.17, f32[4,160,640]{2,1,0:T(8,128)} %act.9), custom_call_target="tpu_custom_call" | custom-call | tf_op jit(solution)/shard_map/pallas_call | solution.py:464
  7.0 0.0 collective-permute-start.1
  7.0 0.0 copy-done.8
  7.0 0.1 copy.13
  7.1 0.0 copy-done.9
  7.1 0.1 copy.11
  7.2 0.0 copy-done
  7.2 0.3 fusion.mixing
  7.5 0.0 copy-done.1
  7.5 0.0 copy-done.6
  7.5 0.0 copy-start.2
  7.5 1.4 copy-done.2
  9.0 0.0 copy-start.4
  9.0 1.1 copy-done.4
  10.1 2.6 %shard_map.91 = (bf16[4,80,640]{2,1,0:T(8,128)(2,1)S(1)}, bf16[4,80,640]{2,1,0:T(8,128)(2,1)S(1)}, bf16[4,80,640]{2,1,0:T(8,128)(2,1)S(1)}, f32[640,640]{1,0:T(8,128)S(1)}) custom-call(f32[4,8]{1,0:T(4,128)S(1)} %copy-done.6, bf16[2,640,1280]{2,1,0:T(8,128)(2,1)S(1)} %copy-done.1, f32[4,160,640]{2,1,0:T(8,128)S(1)} %copy-done.2, ...), custom_call_target="tpu_custom_call" | custom-call | flops 2000000000 | bytes 10000000 | tf_op jit(solution)/shard_map/pallas_call | solution.py:476
  12.7 0.0 collective-permute-done.got
  12.7 2.1 %collective-permute-done.1.got_more = bf16[2,80,640]{2,1,0:T(8,128)(2,1)} collective-permute-done((bf16[2,80,640]{2,1,0:T(8,128)(2,1)}, bf16[2,80,640]{2,1,0:T(8,128)(2,1)}, u32[]{:S(2)}, u32[]{:S(2)}) %collective-permute-start.1) | collective-permute-done | bytes 204832 | tf_op jit(solution)/shard_map/ppermute | solution.py:475
  14.8 2.5 %shard_map.94 = (bf16[16,208,128]{2,1,0:T(8,128)(2,1)S(1)}, bf16[2,4,80,640]{3,2,1,0:T(8,128)(2,1)S(1)}) custom-call(bf16[2,640,1280]{2,1,0:T(8,128)(2,1)S(1)} %copy-done.1, f32[640,640]{1,0:T(8,128)S(1)} %get-tuple-element.24.part, bf16[4,80,640]{2,1,0:T(8,128)(2,1)S(1)} %get-tuple-element.25.kept, bf16[2,80,640]{2,1,0:T(8,128)(2,1)S(1)} %collective-permute-done.got, ...), custom_call_target="tpu_custom_call" | custom-call | tf_op jit(solution)/shard_map/pallas_call | solution.py:486
  17.3 0.0 copy-start.7
  17.4 27.4 %all_to_all.20.spectrum = bf16[16,208,128]{2,1,0:T(8,128)(2,1)S(1)} all-to-all(bf16[16,208,128]{2,1,0:T(8,128)(2,1)S(1)} %get-tuple-element.28), channel_id=1, replica_groups=mesh['subj'=2,'band'=4,'lon'=2,'pop'=2] {'band','lon','pop'}, dimensions={0} | all-to-all | bytes 1703936 | tf_op jit(solution)/shard_map/all_to_all | solution.py:495
  44.7 1.0 collective-permute-start.2
  45.7 0.0 copy-done.7
  45.7 13.7 %shard_map.95 = bf16[16,208,128]{2,1,0:T(8,128)(2,1)S(1)} custom-call(bf16[16,208,128]{2,1,0:T(8,128)(2,1)S(1)} %all_to_all.20.spectrum, f32[4,640]{1,0:T(4,128)S(1)} %copy-done.7, f32[8,8,640]{2,1,0:T(8,128)S(1)} %fusion.mixing, bf16[80,320,640]{2,1,0:T(8,128)(2,1)} %basis.3), custom_call_target="tpu_custom_call" | custom-call | flops 5000000000 | bytes 20000000 | tf_op jit(solution)/shard_map/pallas_call | solution.py:500
  59.5 0.0 collective-permute-done.2.got
  59.5 25.4 %all_to_all.21.spectrum = bf16[16,208,128]{2,1,0:T(8,128)(2,1)S(1)} all-to-all(bf16[16,208,128]{2,1,0:T(8,128)(2,1)S(1)} %shard_map.95), channel_id=1, replica_groups=mesh['subj'=2,'band'=4,'lon'=2,'pop'=2] {'band','lon','pop'}, dimensions={0} | all-to-all | bytes 1703936 | tf_op jit(solution)/shard_map/all_to_all | solution.py:515
  84.9 5.7 %shard_map.96 = (bf16[16,208,128]{2,1,0:T(8,128)(2,1)S(1)}, bf16[2,4,80,640]{3,2,1,0:T(8,128)(2,1)S(1)}, f32[4,80,1280]{2,1,0:T(8,128)S(1)}) custom-call(f32[4,8]{1,0:T(4,128)S(1)} %copy-done.6, bf16[2,640,1280]{2,1,0:T(8,128)(2,1)S(1)} %copy-done.1, bf16[16,208,128]{2,1,0:T(8,128)(2,1)S(1)} %all_to_all.21.spectrum, ...), custom_call_target="tpu_custom_call" | custom-call | tf_op jit(solution)/shard_map/pallas_call | solution.py:520
  90.5 25.4 %all_to_all.22.spectrum = bf16[16,208,128]{2,1,0:T(8,128)(2,1)S(1)} all-to-all(bf16[16,208,128]{2,1,0:T(8,128)(2,1)S(1)} %get-tuple-element.37), channel_id=1, replica_groups=mesh['subj'=2,'band'=4,'lon'=2,'pop'=2] {'band','lon','pop'}, dimensions={0} | all-to-all | bytes 1703936 | tf_op jit(solution)/shard_map/all_to_all | solution.py:495
  116.0 13.7 %shard_map.97 = bf16[16,208,128]{2,1,0:T(8,128)(2,1)S(1)} custom-call(bf16[16,208,128]{2,1,0:T(8,128)(2,1)S(1)} %all_to_all.22.spectrum, f32[4,640]{1,0:T(4,128)S(1)} %copy-done.7, f32[8,8,640]{2,1,0:T(8,128)S(1)} %fusion.mixing, bf16[80,320,640]{2,1,0:T(8,128)(2,1)} %basis.3), custom_call_target="tpu_custom_call" | custom-call | flops 5000000000 | bytes 20000000 | tf_op jit(solution)/shard_map/pallas_call | solution.py:500
  129.7 25.4 %all_to_all.23.spectrum = bf16[16,208,128]{2,1,0:T(8,128)(2,1)S(1)} all-to-all(bf16[16,208,128]{2,1,0:T(8,128)(2,1)S(1)} %shard_map.97), channel_id=1, replica_groups=mesh['subj'=2,'band'=4,'lon'=2,'pop'=2] {'band','lon','pop'}, dimensions={0} | all-to-all | bytes 1703936 | tf_op jit(solution)/shard_map/all_to_all | solution.py:515
  155.1 1.4 shard_map.98
  156.5 1.0 collective-permute-start.4
  157.6 1.2 shard_map.100
  158.8 0.0 copy-start.3
  158.8 0.0 copy-start.5
  158.8 1.1 collective-permute-start.3
  159.9 1.7 shard_map.99.kept
  161.6 2.9 %collective-permute-done.4.got = bf16[2,80,640]{2,1,0:T(8,128)(2,1)S(1)} collective-permute-done((bf16[2,80,640]{2,1,0:T(8,128)(2,1)S(1)}, bf16[2,80,640]{2,1,0:T(8,128)(2,1)S(1)}, u32[]{:S(2)}, u32[]{:S(2)}) %collective-permute-start.4) | collective-permute-done | bytes 204832 | tf_op jit(solution)/shard_map/ppermute | solution.py:548
  164.5 0.0 copy-done.3
  164.5 0.0 copy-done.5
  164.6 1.8 %shard_map.101.refs_0_ = f32[4,160,640]{2,1,0:T(8,128)} custom-call(f32[4,8]{1,0:T(4,128)S(1)} %copy-done.6, f32[4,160,640]{2,1,0:T(8,128)S(1)} %copy-done.3, bf16[4,160,640]{2,1,0:T(8,128)(2,1)S(1)} %copy-done.5, bf16[4,80,640]{2,1,0:T(8,128)(2,1)S(1)} %shard_map.99.kept, bf16[2,80,640]{2,1,0:T(8,128)(2,1)S(1)} %collective-permute-done.4.got), custom_call_target="tpu_custom_call" | custom-call | flops 10000000 | bytes 4000000 | tf_op jit(solution)/shard_map/pallas_call | solution.py:559
  166.3 2.4 %collective-permute-done.3.got = bf16[2,80,640]{2,1,0:T(8,128)(2,1)S(1)} collective-permute-done((bf16[2,80,640]{2,1,0:T(8,128)(2,1)S(1)}, bf16[2,80,640]{2,1,0:T(8,128)(2,1)S(1)}, u32[]{:S(2)}, u32[]{:S(2)}) %collective-permute-start.3) | collective-permute-done | bytes 204832 | tf_op jit(solution)/shard_map/ppermute | solution.py:549
  168.7 1.8 %shard_map.102 = f32[4,160,640]{2,1,0:T(8,128)} custom-call(f32[4,8]{1,0:T(4,128)S(1)} %copy-done.6, f32[4,160,640]{2,1,0:T(8,128)S(1)} %copy-done.3, bf16[4,160,640]{2,1,0:T(8,128)(2,1)S(1)} %copy-done.5, bf16[4,80,640]{2,1,0:T(8,128)(2,1)S(1)} %shard_map.99.kept, ...), custom_call_target="tpu_custom_call", output_to_operand_aliasing={{}: (5, {})} | custom-call | flops 10000000 | bytes 4000000 | tf_op jit(solution)/shard_map/pallas_call | solution.py:559
  (1 shorter events, 0.0 us)
Async XLA Ops:
  0.0 7.2 %copy-start = (f32[4,640]{1,0:T(4,128)S(1)}, f32[4,640]{1,0:T(4,128)}, u32[]{:S(2)}) copy-start(f32[4,640]{1,0:T(4,128)} %param.12) | copy-start | bytes 30724
  0.0 7.5 %copy-start.1 = (bf16[2,640,1280]{2,1,0:T(8,128)(2,1)S(1)}, bf16[2,640,1280]{2,1,0:T(8,128)(2,1)}, u32[]{:S(2)}) copy-start(bf16[2,640,1280]{2,1,0:T(8,128)(2,1)} %constant.4.clone.table) | copy-start | bytes 9830404
  0.0 7.5 %copy-start.6 = (f32[4,8]{1,0:T(4,128)S(1)}, f32[4,8]{1,0:T(4,128)}, u32[]{:S(2)}) copy-start(f32[4,8]{1,0:T(4,128)} %params.17) | copy-start | bytes 388
  0.0 7.0 %copy-start.8 = (s32[8,8]{1,0:T(8,128)S(1)}, s32[8,8]{1,0:T(8,128)}, u32[]{:S(2)}) copy-start(s32[8,8]{1,0:T(8,128)} %param.13) | copy-start | bytes 772
  0.0 7.1 %copy-start.9 = (f32[8,8]{1,0:T(8,128)S(1)}, f32[8,8]{1,0:T(8,128)}, u32[]{:S(2)}) copy-start(f32[8,8]{1,0:T(8,128)} %param.14) | copy-start | bytes 772
  2.1 10.6 %collective-permute-start = (bf16[2,80,640]{2,1,0:T(8,128)(2,1)}, bf16[2,80,640]{2,1,0:T(8,128)(2,1)S(1)}, u32[]{:S(2)}, u32[]{:S(2)}) collective-permute-start(bf16[2,80,640]{2,1,0:T(8,128)(2,1)} %shard_map.92), channel_id=1, source_target_pairs={{0,2},{2,0},{1,3},{3,1},{4,6},{6,4},{5,7},{7,5},{8,10},{10,8},{9,1... | collective-permute-start | bytes 614408 | tf_op jit(solution)/shard_map/ppermute | solution.py:475
  7.0 7.8 %collective-permute-start.1 = (bf16[2,80,640]{2,1,0:T(8,128)(2,1)}, bf16[2,80,640]{2,1,0:T(8,128)(2,1)}, u32[]{:S(2)}, u32[]{:S(2)}) collective-permute-start(bf16[2,80,640]{2,1,0:T(8,128)(2,1)} %shard_map.93), channel_id=1, source_target_pairs={{0,2},{2,0},{1,3},{3,1},{4,6},{6,4},{5,7},{7,5},{8,10},{10,8},{9,1... | collective-permute-start | bytes 614408 | tf_op jit(solution)/shard_map/ppermute | solution.py:475
  7.5 1.4 copy-start.2
  9.0 1.1 copy-start.4
  17.3 28.4 %copy-start.7 = (f32[4,640]{1,0:T(4,128)S(1)}, f32[4,640]{1,0:T(4,128)}, u32[]{:S(2)}) copy-start(f32[4,640]{1,0:T(4,128)} %constant.5.clone.weight) | copy-start | bytes 30724
  44.7 14.8 %collective-permute-start.2 = (bf16[4,80,640]{2,1,0:T(8,128)(2,1)S(1)}, bf16[4,80,640]{2,1,0:T(8,128)(2,1)S(1)}, u32[]{:S(2)}, u32[]{:S(2)}) collective-permute-start(bf16[4,80,640]{2,1,0:T(8,128)(2,1)S(1)} %get-tuple-element.32), channel_id=1, source_target_pairs={{0,2},{2,0},{1,3},{3,1},{4,6},{6,4},{5,7},{7,5},{8,10},{10,8},{9,1... | collective-permute-start | bytes 1228808 | tf_op jit(solution)/shard_map/ppermute | solution.py:497
  156.5 8.0 %collective-permute-start.4 = (bf16[2,80,640]{2,1,0:T(8,128)(2,1)S(1)}, bf16[2,80,640]{2,1,0:T(8,128)(2,1)S(1)}, u32[]{:S(2)}, u32[]{:S(2)}) collective-permute-start(bf16[2,80,640]{2,1,0:T(8,128)(2,1)S(1)} %get-tuple-element.42), channel_id=1, source_target_pairs={{0,2},{2,0},{1,3},{3,1},{4,6},{6,4},{5,7},{7,5},{8,10},{10,8},{9,1... | collective-permute-start | bytes 614408 | tf_op jit(solution)/shard_map/ppermute | solution.py:548
  158.8 5.7 %copy-start.3 = (f32[4,160,640]{2,1,0:T(8,128)S(1)}, f32[4,160,640]{2,1,0:T(8,128)}, u32[]{:S(2)}) copy-start(f32[4,160,640]{2,1,0:T(8,128)} %act.9) | copy-start | bytes 4915204
  158.8 5.7 %copy-start.5 = (bf16[4,160,640]{2,1,0:T(8,128)(2,1)S(1)}, bf16[4,160,640]{2,1,0:T(8,128)(2,1)}, u32[]{:S(2)}) copy-start(bf16[4,160,640]{2,1,0:T(8,128)(2,1)} %drive.5) | copy-start | bytes 2457604
  158.8 9.9 %collective-permute-start.3 = (bf16[2,80,640]{2,1,0:T(8,128)(2,1)S(1)}, bf16[2,80,640]{2,1,0:T(8,128)(2,1)S(1)}, u32[]{:S(2)}, u32[]{:S(2)}) collective-permute-start(bf16[2,80,640]{2,1,0:T(8,128)(2,1)S(1)} %shard_map.100), channel_id=1, source_target_pairs={{0,2},{2,0},{1,3},{3,1},{4,6},{6,4},{5,7},{7,5},{8,10},{10,8},{9,1... | collective-permute-start | bytes 614408 | tf_op jit(solution)/shard_map/ppermute | solution.py:549

commit v4 on v3

--- a/solution.py
+++ b/solution.py
@@ -45,10 +45,12 @@
     return lax.dot_general(a, b, (((1,), (1,)), ((), ())), preferred_element_type=F32)
 
 
-def fourier_table(nlon, deg):
-    phase = np.arange(deg, dtype=np.int64)[:, None] * np.arange(nlon, dtype=np.int64)[None, :] % nlon
+def fourier_table(nlon, owners, owned):
+    wave = np.arange(owners * owned, dtype=np.int64).reshape(-1, 2).T.reshape(-1)
+    phase = wave[:, None] * np.arange(nlon // 2, dtype=np.int64)[None, :] % nlon
     angle = phase.astype(np.float32) * np.float32(2.0 * math.pi / nlon)
-    return np.stack([np.cos(angle), np.sin(angle)]).astype(ml_dtypes.bfloat16)
+    table = np.stack([np.cos(angle), np.sin(angle)]).astype(ml_dtypes.bfloat16)
+    return table.reshape(2, 2, -1, nlon // 2)
 
 
 def lat_weights(nlat):
@@ -90,7 +92,7 @@
         rates[i] = in_wire_order(rate_of(params, first + i, act[i])).astype(BF16)
 
 
-def own_half_body(params, table, act, drive, rates, sent, kept, part):
+def own_half_body(params, act, drive, rates, sent, kept):
     pops, rows, cols = rates.shape
     first = lax.axis_index("pop") * pops
     lon = here()[0]
@@ -103,22 +105,6 @@
             out[i] = in_wire_order(c).astype(BF16)
         r = rate_of(params, first + i, half_of(act, i, lon, rows))
         rates[i] = in_wire_order(r).astype(BF16)
-    block = part.shape[0] // 4
-    columns = [pl.ds(pl.multiple_of(lon * cols, 128), cols)]
-    flat = [rates[...].reshape(pops * rows, cols)]
-    for b in range(4):
-        part[b * block : (b + 1) * block] = joined_fourier(table, b * block, block, columns, flat)
-
-
-def joined_fourier(table, first, block, columns, rates):
-    parts = []
-    for c in range(2):
-        total = None
-        for at, r in zip(columns, rates):
-            term = nt_dot(table[c, first : first + block, at], r)
-            total = term if total is None else total + term
-        parts.append(total)
-    return jnp.concatenate(parts, axis=1)
 
 
 def edge_slots(pops, nlon, groups):
@@ -143,14 +129,13 @@
     return jnp.concatenate(parts, axis=1)
 
 
-def put_fourier(table, columns, flat, rates, fourier, part=None):
+def put_fourier(table, rates, fourier):
     halves, pops, rows, cols = rates.shape
     groups, total, _ = fourier.shape
     lanes = 2 * pops * rows
-    count = table.shape[1] // groups
+    waves = table.shape[2]
+    count = 2 * waves // groups
     slots = edge_slots(pops, halves * cols, groups)
-    pack = 4
-    block = pack * count
     polar, inner = [], []
     for i in range(pops):
         for h in range(halves):
@@ -161,34 +146,34 @@
                 inner.append(strip[rows - 1 :, at])
     nothing = [jnp.zeros((1, 128), F32)] * (slots * groups - len(polar))
     polar, inner = polar + nothing, inner + nothing
-    for b in range(groups // pack):
-        joined = joined_fourier(table, b * block, block, columns, flat)
-        if part is not None:
-            joined = joined + part[b * block : (b + 1) * block]
-        for g in range(pack):
-            to = b * pack + g
-            at = slice(to * slots, (to + 1) * slots)
-            sums = joined[g * count : (g + 1) * count]
-            fourier[to] = packed(sums, polar[at] + inner[at], total)
-
-
-def fourier_of(table, rates, fourier):
-    halves, pops, rows, cols = rates.shape
-    columns = [slice(h * cols, (h + 1) * cols) for h in range(halves)]
-    flat = [rates[h].reshape(pops * rows, cols) for h in range(halves)]
-    put_fourier(table, columns, flat, rates, fourier)
-
-
-def first_fourier_body(table, part, kept, got, got_more, fourier, rates):
-    some, _, cols = got.shape
+    one, two = rates[0].astype(F32), rates[1].astype(F32)
+    pack = groups // 4
+    block = pack * count
+    for p, mix in enumerate((one + two - 1.0, one - two)):
+        flat = mix.astype(BF16).reshape(pops * rows, cols)
+        for b in range(waves // block):
+            parts = []
+            for c in range(2):
+                t = table[c, p, b * block : (b + 1) * block]
+                sums = nt_dot(t, flat)
+                if p == 0:
+                    sums = sums + jnp.sum(t.astype(F32), axis=1, keepdims=True)
+                parts.append(sums)
+            joined = jnp.concatenate(parts, axis=1)
+            for k in range(pack):
+                to = (b * pack + k) * 2 + p
+                at = slice(to * slots, (to + 1) * slots)
+                sums = joined[k * count : (k + 1) * count]
+                fourier[to] = packed(sums, polar[at] + inner[at], total)
+
+
+def first_fourier_body(table, kept, got, got_more, fourier, rates):
+    some = got.shape[0]
     lon = here()[0]
     rates[lon] = kept[...]
     rates[1 - lon, :some] = got[...]
     rates[1 - lon, some:] = got_more[...]
-    columns = [pl.ds(pl.multiple_of((1 - lon) * cols, 128), cols)]
-    there = [v[...].reshape(-1, cols) for v in (got, got_more)]
-    flat = [jnp.concatenate(there, axis=0)]
-    put_fourier(table, columns, flat, rates, fourier, part)
+    put_fourier(table, rates, fourier)
 
 
 def lateral_of(rates, half, halo, some=None):
@@ -226,11 +211,11 @@
     pad = tiles * 128 - half_lat
     block = 8
     owner = lax.axis_index("band") * lax.axis_size("lon") + lax.axis_index("lon")
-    here_first = lax.axis_index("pop") * count
-    first_wave = owner * basis.shape[0] + here_first
+    core = lax.axis_index("pop")
+    first_wave = owner * basis.shape[0] + core
 
     def fetch(r):
-        return pltpu.make_async_copy(basis.at[here_first + r], held.at[r], arrived.at[r])
+        return pltpu.make_async_copy(basis.at[cores * r + core], held.at[r], arrived.at[r])
 
     @pl.loop(0, count)
     def _(r):
@@ -281,7 +266,7 @@
             fetch(step * block + at).wait()
         for at in range(block):
             r = step * block + at
-            m = first_wave + r
+            m = first_wave + cores * r
             rows = pl.ds(r, 2 * pops, stride=count)
             lhs = jnp.concatenate(
                 [
@@ -328,7 +313,8 @@
 def turned(spectrum, turned_s):
     groups = spectrum.shape[0]
     lanes, deg = turned_s.shape
-    blocks = [unpacked(spectrum[g], deg // groups, lanes) for g in range(groups)]
+    order = list(range(0, groups, 2)) + list(range(1, groups, 2))
+    blocks = [unpacked(spectrum[g], deg // groups, lanes) for g in order]
     turned_s[...] = jnp.concatenate(blocks, axis=0).T.astype(BF16)
 
 
@@ -351,18 +337,20 @@
                     ]
 
 
-def synth_of(both, table, columns, first=0, count=None):
+def synth_of(both, table, first=0, count=None):
     half = both.shape[0] // 2
     count = half if count is None else count
-    total = None
-    for c in range(2):
-        term = jnp.dot(
-            both[c * half + first : c * half + first + count, :],
-            table[c, :, columns],
-            preferred_element_type=F32,
-        )
-        total = term if total is None else total + term
-    return total
+    waves, cols = table.shape[2:]
+    sums = []
+    for p in range(2):
+        total = None
+        for c in range(2):
+            at = c * half + first
+            some = both[at : at + count, p * waves : (p + 1) * waves]
+            term = jnp.dot(some, table[c, p], preferred_element_type=F32)
+            total = term if total is None else total + term
+        sums.append(total * (time_step / (2 * cols)))
+    return sums
 
 
 def middle_body(
@@ -372,25 +360,26 @@
     first = lax.axis_index("pop") * pops
     turned(spectrum, turned_s)
     put_ends(spectrum, turned_s, halo)
+    even, odd = synth_of(turned_s, table)
     for h in range(halves):
         at = slice(h * cols, (h + 1) * cols)
-        synth = synth_of(turned_s, table, at) * (time_step / (halves * cols))
         lateral = lateral_of(old, h, halo)
         for i in range(pops):
-            v = synth[i * rows : (i + 1) * rows]
+            here_rows = slice(i * rows, (i + 1) * rows)
+            v = even[here_rows] + odd[here_rows] if h == 0 else even[here_rows] - odd[here_rows]
             v = v + (time_step * params[3, first + i]) * lateral[i]
             inner[i, :, at] = v
             u = jnp.where(here()[0] == h, kept[i], got[i]).astype(F32) + v
             rates[h, i] = rate_of(params, first + i, u)
-    fourier_of(table, rates, fourier)
+    put_fourier(table, rates, fourier)
 
 
 def put_inner(params, table, rates, halo, inner, both, half, some, out):
     _, pops, rows, cols = rates.shape
     first = lax.axis_index("pop") * pops
     at = pl.ds(pl.multiple_of(half * cols, 128), cols)
-    synth = synth_of(both, table, at, some[0] * rows, len(some) * rows)
-    synth = synth * (time_step / table.shape[2])
+    even, odd = synth_of(both, table, some[0] * rows, len(some) * rows)
+    synth = even + jnp.where(half == 1, -1.0, 1.0) * odd
     lateral = lateral_of(rates, half, halo, some)
     for k, i in enumerate(some):
         v = synth[k * rows : (k + 1) * rows]
@@ -439,7 +428,7 @@
     lanes = 2 * pops_here * rows
     band, lon, core = (lax.axis_index(a) for a in ("band", "lon", "pop"))
     owner = band * lons + lon
-    table = jnp.asarray(fourier_table(nlon, deg))
+    table = jnp.asarray(fourier_table(nlon, owners, owned))
     weights = lat_weights(nlat).reshape(owners // 2, 1, rows)
     weights = jnp.asarray(np.tile(weights, (1, 2 * pops_here, 1)).reshape(owners // 2, lanes))
     onehot = (conn_block[..., None] == jnp.arange(kernels.shape[0], dtype=jnp.int32)).astype(F32)
@@ -473,23 +462,23 @@
             out_specs=pl.BlockSpec((some, rows, cols), lambda i: (0, 0, 0)),
         )(rate_params, activity)
         got.append(lax.ppermute(sent, "lon", swap))
-    kept, carried_sent, carried_kept, part = call(
+    kept, carried_sent, carried_kept = call(
         own_half_body,
-        (piece,) * 3 + (shape(deg, lanes, dtype=F32),),
+        (piece,) * 3,
         24,
         2 * 10**9,
         10**7,
-        in_specs=[scalars()] + [whole()] * 3,
-        out_specs=(whole(),) * 4,
-    )(rate_params, table, activity, drive)
+        in_specs=[scalars()] + [whole()] * 2,
+        out_specs=(whole(),) * 3,
+    )(rate_params, activity, drive)
     *got, mixing = lax.optimization_barrier((*got, mixing))
     fourier, rates = call(
         first_fourier_body,
         (wire, both_halves),
-        16,
-        in_specs=[whole()] * 5,
+        24,
+        in_specs=[whole()] * 4,
         out_specs=(whole(),) * 2,
-    )(table, part, kept, *got)
+    )(table, kept, *got)
 
     def coupled(fourier, *more):
         spectrum = lax.all_to_all(fourier, EVERYONE, 0, 0, tiled=True)
@@ -705,6 +694,7 @@
             bands % 2 == 0
             and activity.shape[0] % 2 == 0
             and lons == 2
+            and cores == 2
             and bands * lons * cores % 4 == 0
             and owned % (8 * cores) == 0
             and rows % 16 == 0

time: 171 us -> 169 us (0.988)
  waiting for transfers between devices: 7.46 us -> 11 us
  Pallas kernels: 50.1 us -> 47.2 us
  local copies, waits for them, and re-layouts: 2.78 us -> 0.2 us
    ppermute x2, waiting for transfers between devices: 2.13 us -> 6.04 us  [by_parts(): got.append(lax.ppermute(sent, 'lon', swap))]
    unnamed x20 -> x16, local copies, waits for them, and re-layouts: 2.61 us -> 0.03 us
    pallas_call x2, Pallas kernels: 5.08 us -> 2.81 us  [the longest x1 1.65 us: by_parts(): call(first_fourier_body, (wire, both_halves), 24, in_specs=[whole()] * 4,...]
  transfers between devices with their start and end apart: 5 -> 5, of which waited for: 3 -> 4; matrix products, arithmetic and copies ran while one was open for 0% -> 0% of each run, Pallas kernels for 13% -> 13%
where the time goes in v4:
time: 169 us
  blocking collectives  104 us (62%)
  Pallas kernels  47.2 us (28%)
  waiting for transfers between devices  11 us (7%)
  starting transfers between devices  6.1 us (4%)
    all_to_all x2, blocking collectives, coupled(): spectrum = lax.all_to_all(fourier, EVERYONE, 0, 0, tiled=True)  52.8 us
    all_to_all x2, blocking collectives, coupled(): back = lax.all_to_all(synthesis, EVERYONE, 0, 0, tiled=True)  50.8 us
    pallas_call x2, Pallas kernels, coupled(): call(functools.partial(legendre_body, nlon), wire, 40, 5 * 10 ** 9, 2 * 1...  27.5 us
    ppermute x2, waiting for transfers between devices, by_parts(): got.append(lax.ppermute(sent, 'lon', swap))  6.04 us
    pallas_call x1, Pallas kernels, by_parts(): call(middle_body, (wire, both_halves, state), 32, in_specs=[scalars()] +...  4.48 us
    pallas_call x2, Pallas kernels, by_parts(): call(functools.partial(sent_rates_body, pair[0]), shape(some, rows, cols)...  4.03 us
    pallas_call x2, Pallas kernels, by_parts(): call(functools.partial(grid_update_body, begin), shape(*activity.shape, d...  3.54 us
  transfers between devices with their start and end apart: 5, of which 4 were waited for; matrix products, arithmetic and copies ran while one was open for 0% of the time, Pallas kernels for 13%

profile of v4, /device:TPU:0, one launch (start us, length us, event | category | flops | bytes accessed | tf_op | source)
XLA Modules:
  0.0 168.6 jit_solution(14878163956317537985)
XLA Ops:
  0.0 0.0 copy-start
  0.0 0.0 copy-start.4
  0.0 0.0 copy-start.2
  0.0 0.0 copy-start.6
  0.0 0.0 copy-start.7
  0.0 0.0 copy-start.3
  0.0 2.1 %shard_map.92 = bf16[2,80,640]{2,1,0:T(8,128)(2,1)} custom-call(f32[4,8]{1,0:T(4,128)} %params.17, f32[4,160,640]{2,1,0:T(8,128)} %act.9), custom_call_target="tpu_custom_call" | custom-call | tf_op jit(solution)/shard_map/pallas_call | solution.py:453
  2.1 3.0 %collective-permute-start = (bf16[2,80,640]{2,1,0:T(8,128)(2,1)}, bf16[2,80,640]{2,1,0:T(8,128)(2,1)S(1)}, u32[]{:S(2)}, u32[]{:S(2)}) collective-permute-start(bf16[2,80,640]{2,1,0:T(8,128)(2,1)} %shard_map.92), channel_id=1, source_target_pairs={{0,2},{2,0},{1,3},{3,1},{4,6},{6,4},{5,7},{7,5},{8,10},{10,8},{9,1... | collective-permute-start | bytes 614408 | tf_op jit(solution)/shard_map/ppermute | solution.py:464
  5.1 1.9 %shard_map.93 = bf16[2,80,640]{2,1,0:T(8,128)(2,1)} custom-call(f32[4,8]{1,0:T(4,128)} %params.17, f32[4,160,640]{2,1,0:T(8,128)} %act.9), custom_call_target="tpu_custom_call" | custom-call | tf_op jit(solution)/shard_map/pallas_call | solution.py:453
  7.0 0.0 collective-permute-start.1
  7.0 0.0 copy-done.6
  7.0 0.1 copy.13
  7.1 0.0 copy-done.7
  7.1 0.1 copy.11
  7.2 0.0 copy-done
  7.2 0.3 fusion.mixing
  7.5 0.0 copy-done.4
  7.5 0.0 copy-done.2
  7.5 0.0 copy-done.3
  7.5 0.0 copy-start.1
  7.5 1.2 shard_map.91
  8.7 2.5 %collective-permute-done.got = bf16[2,80,640]{2,1,0:T(8,128)(2,1)S(1)} collective-permute-done((bf16[2,80,640]{2,1,0:T(8,128)(2,1)}, bf16[2,80,640]{2,1,0:T(8,128)(2,1)S(1)}, u32[]{:S(2)}, u32[]{:S(2)}) %collective-permute-start) | collective-permute-done | bytes 204832 | tf_op jit(solution)/shard_map/ppermute | solution.py:464
  11.2 3.6 %collective-permute-done.1.got_more = bf16[2,80,640]{2,1,0:T(8,128)(2,1)S(1)} collective-permute-done((bf16[2,80,640]{2,1,0:T(8,128)(2,1)}, bf16[2,80,640]{2,1,0:T(8,128)(2,1)S(1)}, u32[]{:S(2)}, u32[]{:S(2)}) %collective-permute-start.1) | collective-permute-done | bytes 204832 | tf_op jit(solution)/shard_map/ppermute | solution.py:464
  14.8 0.0 copy-done.1
  14.8 0.0 copy-start.5
  14.8 1.7 shard_map.94
  16.4 27.4 %all_to_all.20.spectrum = bf16[16,208,128]{2,1,0:T(8,128)(2,1)S(1)} all-to-all(bf16[16,208,128]{2,1,0:T(8,128)(2,1)S(1)} %get-tuple-element.26), channel_id=1, replica_groups=mesh['subj'=2,'band'=4,'lon'=2,'pop'=2] {'band','lon','pop'}, dimensions={0} | all-to-all | bytes 1703936 | tf_op jit(solution)/shard_map/all_to_all | solution.py:484
  43.8 1.0 collective-permute-start.2
  44.8 0.0 copy-done.5
  44.8 13.7 %shard_map.95 = bf16[16,208,128]{2,1,0:T(8,128)(2,1)S(1)} custom-call(bf16[16,208,128]{2,1,0:T(8,128)(2,1)S(1)} %all_to_all.20.spectrum, f32[4,640]{1,0:T(4,128)S(1)} %copy-done.5, f32[8,8,640]{2,1,0:T(8,128)S(1)} %fusion.mixing, bf16[80,320,640]{2,1,0:T(8,128)(2,1)} %basis.3), custom_call_target="tpu_custom_call" | custom-call | flops 5000000000 | bytes 20000000 | tf_op jit(solution)/shard_map/pallas_call | solution.py:489
  58.5 0.0 collective-permute-done.2.got
  58.5 25.4 %all_to_all.21.spectrum = bf16[16,208,128]{2,1,0:T(8,128)(2,1)S(1)} all-to-all(bf16[16,208,128]{2,1,0:T(8,128)(2,1)S(1)} %shard_map.95), channel_id=1, replica_groups=mesh['subj'=2,'band'=4,'lon'=2,'pop'=2] {'band','lon','pop'}, dimensions={0} | all-to-all | bytes 1703936 | tf_op jit(solution)/shard_map/all_to_all | solution.py:504
  83.9 4.5 %shard_map.96 = (bf16[16,208,128]{2,1,0:T(8,128)(2,1)S(1)}, bf16[2,4,80,640]{3,2,1,0:T(8,128)(2,1)S(1)}, f32[4,80,1280]{2,1,0:T(8,128)S(1)}) custom-call(f32[4,8]{1,0:T(4,128)S(1)} %copy-done.4, bf16[2,2,320,640]{3,2,1,0:T(8,128)(2,1)S(1)} %copy-done.1, bf16[16,208,128]{2,1,0:T(8,128)(2,1)S(1)} %all_to_all.21.spectrum, ...), custom_call_target="tpu_custom_call" | custom-call | tf_op jit(solution)/shard_map/pallas_call | solution.py:509
  88.4 25.4 %all_to_all.22.spectrum = bf16[16,208,128]{2,1,0:T(8,128)(2,1)S(1)} all-to-all(bf16[16,208,128]{2,1,0:T(8,128)(2,1)S(1)} %get-tuple-element.35), channel_id=1, replica_groups=mesh['subj'=2,'band'=4,'lon'=2,'pop'=2] {'band','lon','pop'}, dimensions={0} | all-to-all | bytes 1703936 | tf_op jit(solution)/shard_map/all_to_all | solution.py:484
  113.9 13.7 %shard_map.97 = bf16[16,208,128]{2,1,0:T(8,128)(2,1)S(1)} custom-call(bf16[16,208,128]{2,1,0:T(8,128)(2,1)S(1)} %all_to_all.22.spectrum, f32[4,640]{1,0:T(4,128)S(1)} %copy-done.5, f32[8,8,640]{2,1,0:T(8,128)S(1)} %fusion.mixing, bf16[80,320,640]{2,1,0:T(8,128)(2,1)} %basis.3), custom_call_target="tpu_custom_call" | custom-call | flops 5000000000 | bytes 20000000 | tf_op jit(solution)/shard_map/pallas_call | solution.py:489
  127.6 25.4 %all_to_all.23.spectrum = bf16[16,208,128]{2,1,0:T(8,128)(2,1)S(1)} all-to-all(bf16[16,208,128]{2,1,0:T(8,128)(2,1)S(1)} %shard_map.97), channel_id=1, replica_groups=mesh['subj'=2,'band'=4,'lon'=2,'pop'=2] {'band','lon','pop'}, dimensions={0} | all-to-all | bytes 1703936 | tf_op jit(solution)/shard_map/all_to_all | solution.py:504
  153.0 1.6 shard_map.98
  154.6 1.1 collective-permute-start.4
  155.6 1.4 shard_map.100
  157.0 1.1 collective-permute-start.3
  158.1 2.0 %shard_map.99.kept = bf16[4,80,640]{2,1,0:T(8,128)(2,1)S(1)} custom-call(f32[4,8]{1,0:T(4,128)S(1)} %copy-done.4, bf16[2,2,320,640]{3,2,1,0:T(8,128)(2,1)S(1)} %copy-done.1, bf16[640,640]{1,0:T(8,128)(2,1)S(1)} %get-tuple-element.38.both, bf16[2,4,80,640]{3,2,1,0:T(8,128)(2,1)S(1)} %get-tuple-element.36.rates, f32[2,2,4,640]{3,2,1,0:T(4,128)S(1)} %get-tuple-element.39.halo, ...), custom_call_target="tpu_custom_call" | custom-call | flops 1000000000 | bytes 5000000 | tf_op jit(solution)/shard_map/pallas_call | solution.py:527
  160.1 2.5 %collective-permute-done.4.got = bf16[2,80,640]{2,1,0:T(8,128)(2,1)S(1)} collective-permute-done((bf16[2,80,640]{2,1,0:T(8,128)(2,1)S(1)}, bf16[2,80,640]{2,1,0:T(8,128)(2,1)S(1)}, u32[]{:S(2)}, u32[]{:S(2)}) %collective-permute-start.4) | collective-permute-done | bytes 204832 | tf_op jit(solution)/shard_map/ppermute | solution.py:537
  162.6 1.8 %shard_map.101.refs_0_ = f32[4,160,640]{2,1,0:T(8,128)} custom-call(f32[4,8]{1,0:T(4,128)S(1)} %copy-done.4, f32[4,160,640]{2,1,0:T(8,128)S(1)} %copy-done.2, bf16[4,160,640]{2,1,0:T(8,128)(2,1)S(1)} %copy-done.3, bf16[4,80,640]{2,1,0:T(8,128)(2,1)S(1)} %shard_map.99.kept, bf16[2,80,640]{2,1,0:T(8,128)(2,1)S(1)} %collective-permute-done.4.got), custom_call_target="tpu_custom_call" | custom-call | flops 10000000 | bytes 4000000 | tf_op jit(solution)/shard_map/pallas_call | solution.py:548
  164.4 2.4 %collective-permute-done.3.got = bf16[2,80,640]{2,1,0:T(8,128)(2,1)S(1)} collective-permute-done((bf16[2,80,640]{2,1,0:T(8,128)(2,1)S(1)}, bf16[2,80,640]{2,1,0:T(8,128)(2,1)S(1)}, u32[]{:S(2)}, u32[]{:S(2)}) %collective-permute-start.3) | collective-permute-done | bytes 204832 | tf_op jit(solution)/shard_map/ppermute | solution.py:538
  166.8 1.8 %shard_map.102 = f32[4,160,640]{2,1,0:T(8,128)} custom-call(f32[4,8]{1,0:T(4,128)S(1)} %copy-done.4, f32[4,160,640]{2,1,0:T(8,128)S(1)} %copy-done.2, bf16[4,160,640]{2,1,0:T(8,128)(2,1)S(1)} %copy-done.3, bf16[4,80,640]{2,1,0:T(8,128)(2,1)S(1)} %shard_map.99.kept, ...), custom_call_target="tpu_custom_call", output_to_operand_aliasing={{}: (5, {})} | custom-call | flops 10000000 | bytes 4000000 | tf_op jit(solution)/shard_map/pallas_call | solution.py:548
  (1 shorter events, 0.0 us)
Async XLA Ops:
  0.0 7.2 %copy-start = (f32[4,640]{1,0:T(4,128)S(1)}, f32[4,640]{1,0:T(4,128)}, u32[]{:S(2)}) copy-start(f32[4,640]{1,0:T(4,128)} %param.12) | copy-start | bytes 30724
  0.0 7.5 %copy-start.4 = (f32[4,8]{1,0:T(4,128)S(1)}, f32[4,8]{1,0:T(4,128)}, u32[]{:S(2)}) copy-start(f32[4,8]{1,0:T(4,128)} %params.17) | copy-start | bytes 388
  0.0 7.5 %copy-start.2 = (f32[4,160,640]{2,1,0:T(8,128)S(1)}, f32[4,160,640]{2,1,0:T(8,128)}, u32[]{:S(2)}) copy-start(f32[4,160,640]{2,1,0:T(8,128)} %act.9) | copy-start | bytes 4915204
  0.0 7.0 %copy-start.6 = (s32[8,8]{1,0:T(8,128)S(1)}, s32[8,8]{1,0:T(8,128)}, u32[]{:S(2)}) copy-start(s32[8,8]{1,0:T(8,128)} %param.13) | copy-start | bytes 772
  0.0 7.1 %copy-start.7 = (f32[8,8]{1,0:T(8,128)S(1)}, f32[8,8]{1,0:T(8,128)}, u32[]{:S(2)}) copy-start(f32[8,8]{1,0:T(8,128)} %param.14) | copy-start | bytes 772
  0.0 7.5 %copy-start.3 = (bf16[4,160,640]{2,1,0:T(8,128)(2,1)S(1)}, bf16[4,160,640]{2,1,0:T(8,128)(2,1)}, u32[]{:S(2)}) copy-start(bf16[4,160,640]{2,1,0:T(8,128)(2,1)} %drive.5) | copy-start | bytes 2457604
  2.1 9.1 %collective-permute-start = (bf16[2,80,640]{2,1,0:T(8,128)(2,1)}, bf16[2,80,640]{2,1,0:T(8,128)(2,1)S(1)}, u32[]{:S(2)}, u32[]{:S(2)}) collective-permute-start(bf16[2,80,640]{2,1,0:T(8,128)(2,1)} %shard_map.92), channel_id=1, source_target_pairs={{0,2},{2,0},{1,3},{3,1},{4,6},{6,4},{5,7},{7,5},{8,10},{10,8},{9,1... | collective-permute-start | bytes 614408 | tf_op jit(solution)/shard_map/ppermute | solution.py:464
  7.0 7.7 %collective-permute-start.1 = (bf16[2,80,640]{2,1,0:T(8,128)(2,1)}, bf16[2,80,640]{2,1,0:T(8,128)(2,1)S(1)}, u32[]{:S(2)}, u32[]{:S(2)}) collective-permute-start(bf16[2,80,640]{2,1,0:T(8,128)(2,1)} %shard_map.93), channel_id=1, source_target_pairs={{0,2},{2,0},{1,3},{3,1},{4,6},{6,4},{5,7},{7,5},{8,10},{10,8},{9,1... | collective-permute-start | bytes 614408 | tf_op jit(solution)/shard_map/ppermute | solution.py:464
  7.5 7.2 %copy-start.1 = (bf16[2,2,320,640]{3,2,1,0:T(8,128)(2,1)S(1)}, bf16[2,2,320,640]{3,2,1,0:T(8,128)(2,1)}, u32[]{:S(2)}) copy-start(bf16[2,2,320,640]{3,2,1,0:T(8,128)(2,1)} %constant.4.clone.table) | copy-start | bytes 4915204
  14.8 30.0 %copy-start.5 = (f32[4,640]{1,0:T(4,128)S(1)}, f32[4,640]{1,0:T(4,128)}, u32[]{:S(2)}) copy-start(f32[4,640]{1,0:T(4,128)} %constant.5.clone.weight) | copy-start | bytes 30724
  43.8 14.7 %collective-permute-start.2 = (bf16[4,80,640]{2,1,0:T(8,128)(2,1)S(1)}, bf16[4,80,640]{2,1,0:T(8,128)(2,1)S(1)}, u32[]{:S(2)}, u32[]{:S(2)}) collective-permute-start(bf16[4,80,640]{2,1,0:T(8,128)(2,1)S(1)} %get-tuple-element.30), channel_id=1, source_target_pairs={{0,2},{2,0},{1,3},{3,1},{4,6},{6,4},{5,7},{7,5},{8,10},{10,8},{9,1... | collective-permute-start | bytes 1228808 | tf_op jit(solution)/shard_map/ppermute | solution.py:486
  154.6 8.0 %collective-permute-start.4 = (bf16[2,80,640]{2,1,0:T(8,128)(2,1)S(1)}, bf16[2,80,640]{2,1,0:T(8,128)(2,1)S(1)}, u32[]{:S(2)}, u32[]{:S(2)}) collective-permute-start(bf16[2,80,640]{2,1,0:T(8,128)(2,1)S(1)} %get-tuple-element.40), channel_id=1, source_target_pairs={{0,2},{2,0},{1,3},{3,1},{4,6},{6,4},{5,7},{7,5},{8,10},{10,8},{9,1... | collective-permute-start | bytes 614408 | tf_op jit(solution)/shard_map/ppermute | solution.py:537
  157.0 9.8 %collective-permute-start.3 = (bf16[2,80,640]{2,1,0:T(8,128)(2,1)S(1)}, bf16[2,80,640]{2,1,0:T(8,128)(2,1)S(1)}, u32[]{:S(2)}, u32[]{:S(2)}) collective-permute-start(bf16[2,80,640]{2,1,0:T(8,128)(2,1)S(1)} %shard_map.100), channel_id=1, source_target_pairs={{0,2},{2,0},{1,3},{3,1},{4,6},{6,4},{5,7},{7,5},{8,10},{10,8},{9,1... | collective-permute-start | bytes 614408 | tf_op jit(solution)/shard_map/ppermute | solution.py:538

commit v5 on v4

--- a/solution.py
+++ b/solution.py
@@ -264,6 +264,7 @@
     def _(step):
         for at in range(block):
             fetch(step * block + at).wait()
+        todo = []
         for at in range(block):
             r = step * block + at
             m = first_wave + cores * r
@@ -287,8 +288,10 @@
                     total = term if total is None else total + term
                 mixed.append(total)
             mixed = jnp.concatenate(mixed, axis=0)
+            lhs2 = jnp.concatenate([mixed, jnp.where(odd, -mixed, mixed)], axis=0).astype(BF16)
+            todo.append((r, m, rows, lhs2))
+        for r, m, rows, lhs2 in todo:
             amplitude = jnp.where(m == 0, 1.0, 2.0)
-            lhs2 = jnp.concatenate([mixed, jnp.where(odd, -mixed, mixed)], axis=0).astype(BF16)
             field = nt_dot(lhs2, held[r]) * amplitude
             if pad:
                 field = jnp.concatenate([field, jnp.zeros((4 * pops, pad), F32)], axis=1)

time: 169 us -> 163 us (0.964)
  Pallas kernels: 47.2 us -> 41.1 us
    pallas_call x2, Pallas kernels: 27.5 us -> 21.3 us  [coupled(): call(functools.partial(legendre_body, nlon), wire, 40, 5 * 10 ** 9, 2 * 1...]
  transfers between devices with their start and end apart: 5 -> 5, of which waited for: 4 -> 5; matrix products, arithmetic and copies ran while one was open for 0% -> 0% of each run, Pallas kernels for 13% -> 12%
where the time goes in v5:
time: 163 us; the launch traced here: 162 us
  blocking collectives  103 us (63%)
  Pallas kernels  41.1 us (25%)
  waiting for transfers between devices  11.4 us (7%)
  starting transfers between devices  6.1 us (4%)
    all_to_all x2, blocking collectives, coupled(): spectrum = lax.all_to_all(fourier, EVERYONE, 0, 0, tiled=True)  52.8 us
    all_to_all x2, blocking collectives, coupled(): back = lax.all_to_all(synthesis, EVERYONE, 0, 0, tiled=True)  50.4 us
    pallas_call x2, Pallas kernels, coupled(): call(functools.partial(legendre_body, nlon), wire, 40, 5 * 10 ** 9, 2 * 1...  21.3 us
    ppermute x2, waiting for transfers between devices, by_parts(): got.append(lax.ppermute(sent, 'lon', swap))  6.04 us
    pallas_call x1, Pallas kernels, by_parts(): call(middle_body, (wire, both_halves, state), 32, in_specs=[scalars()] +...  4.48 us
    pallas_call x2, Pallas kernels, by_parts(): call(functools.partial(sent_rates_body, pair[0]), shape(some, rows, cols)...  4.03 us
    pallas_call x2, Pallas kernels, by_parts(): call(functools.partial(grid_update_body, begin), shape(*activity.shape, d...  3.53 us
    pallas_call x2, Pallas kernels, inner_of(): call(functools.partial(body, some), shape(count, rows, cols), 16, 10 ** 9...  3.33 us
  transfers between devices with their start and end apart: 5, of which 5 were waited for; matrix products, arithmetic and copies ran while one was open for 0% of the time, Pallas kernels for 12%

profile of v5, /device:TPU:0, one launch (start us, length us, event | category | flops | bytes accessed | tf_op | source)
XLA Modules:
  0.0 162.4 jit_solution(7385633983756645691)
XLA Ops:
  0.0 0.0 copy-start
  0.0 0.0 copy-start.4
  0.0 0.0 copy-start.2
  0.0 0.0 copy-start.6
  0.0 0.0 copy-start.7
  0.0 0.0 copy-start.3
  0.0 2.1 %shard_map.92 = bf16[2,80,640]{2,1,0:T(8,128)(2,1)} custom-call(f32[4,8]{1,0:T(4,128)} %params.17, f32[4,160,640]{2,1,0:T(8,128)} %act.9), custom_call_target="tpu_custom_call" | custom-call | tf_op jit(solution)/shard_map/pallas_call | solution.py:456
  2.1 3.0 %collective-permute-start = (bf16[2,80,640]{2,1,0:T(8,128)(2,1)}, bf16[2,80,640]{2,1,0:T(8,128)(2,1)S(1)}, u32[]{:S(2)}, u32[]{:S(2)}) collective-permute-start(bf16[2,80,640]{2,1,0:T(8,128)(2,1)} %shard_map.92), channel_id=1, source_target_pairs={{0,2},{2,0},{1,3},{3,1},{4,6},{6,4},{5,7},{7,5},{8,10},{10,8},{9,1... | collective-permute-start | bytes 614408 | tf_op jit(solution)/shard_map/ppermute | solution.py:467
  5.1 1.9 %shard_map.93 = bf16[2,80,640]{2,1,0:T(8,128)(2,1)} custom-call(f32[4,8]{1,0:T(4,128)} %params.17, f32[4,160,640]{2,1,0:T(8,128)} %act.9), custom_call_target="tpu_custom_call" | custom-call | tf_op jit(solution)/shard_map/pallas_call | solution.py:456
  7.0 0.0 collective-permute-start.1
  7.0 0.0 copy-done.6
  7.0 0.1 copy.13
  7.1 0.0 copy-done.7
  7.1 0.1 copy.11
  7.2 0.0 copy-done
  7.2 0.3 fusion.mixing
  7.5 0.0 copy-done.4
  7.5 0.0 copy-done.2
  7.5 0.0 copy-done.3
  7.5 0.0 copy-start.1
  7.5 1.2 shard_map.91
  8.7 2.5 %collective-permute-done.got = bf16[2,80,640]{2,1,0:T(8,128)(2,1)S(1)} collective-permute-done((bf16[2,80,640]{2,1,0:T(8,128)(2,1)}, bf16[2,80,640]{2,1,0:T(8,128)(2,1)S(1)}, u32[]{:S(2)}, u32[]{:S(2)}) %collective-permute-start) | collective-permute-done | bytes 204832 | tf_op jit(solution)/shard_map/ppermute | solution.py:467
  11.2 3.6 %collective-permute-done.1.got_more = bf16[2,80,640]{2,1,0:T(8,128)(2,1)S(1)} collective-permute-done((bf16[2,80,640]{2,1,0:T(8,128)(2,1)}, bf16[2,80,640]{2,1,0:T(8,128)(2,1)S(1)}, u32[]{:S(2)}, u32[]{:S(2)}) %collective-permute-start.1) | collective-permute-done | bytes 204832 | tf_op jit(solution)/shard_map/ppermute | solution.py:467
  14.8 0.0 copy-done.1
  14.8 0.0 copy-start.5
  14.8 1.7 %shard_map.94 = (bf16[16,208,128]{2,1,0:T(8,128)(2,1)S(1)}, bf16[2,4,80,640]{3,2,1,0:T(8,128)(2,1)S(1)}) custom-call(bf16[2,2,320,640]{3,2,1,0:T(8,128)(2,1)S(1)} %copy-done.1, bf16[4,80,640]{2,1,0:T(8,128)(2,1)S(1)} %get-tuple-element.23.kept, bf16[2,80,640]{2,1,0:T(8,128)(2,1)S(1)} %collective-permute-done.got, ...), custom_call_target="tpu_custom_call" | custom-call | tf_op jit(solution)/shard_map/pallas_call | solution.py:478
  16.4 27.4 %all_to_all.20.spectrum = bf16[16,208,128]{2,1,0:T(8,128)(2,1)S(1)} all-to-all(bf16[16,208,128]{2,1,0:T(8,128)(2,1)S(1)} %get-tuple-element.26), channel_id=1, replica_groups=mesh['subj'=2,'band'=4,'lon'=2,'pop'=2] {'band','lon','pop'}, dimensions={0} | all-to-all | bytes 1703936 | tf_op jit(solution)/shard_map/all_to_all | solution.py:487
  43.8 1.0 collective-permute-start.2
  44.8 0.0 copy-done.5
  44.8 10.7 %shard_map.95 = bf16[16,208,128]{2,1,0:T(8,128)(2,1)S(1)} custom-call(bf16[16,208,128]{2,1,0:T(8,128)(2,1)S(1)} %all_to_all.20.spectrum, f32[4,640]{1,0:T(4,128)S(1)} %copy-done.5, f32[8,8,640]{2,1,0:T(8,128)S(1)} %fusion.mixing, bf16[80,320,640]{2,1,0:T(8,128)(2,1)} %basis.3), custom_call_target="tpu_custom_call" | custom-call | flops 5000000000 | bytes 20000000 | tf_op jit(solution)/shard_map/pallas_call | solution.py:492
  55.5 0.5 collective-permute-done.2.got
  55.9 24.9 %all_to_all.21.spectrum = bf16[16,208,128]{2,1,0:T(8,128)(2,1)S(1)} all-to-all(bf16[16,208,128]{2,1,0:T(8,128)(2,1)S(1)} %shard_map.95), channel_id=1, replica_groups=mesh['subj'=2,'band'=4,'lon'=2,'pop'=2] {'band','lon','pop'}, dimensions={0} | all-to-all | bytes 1703936 | tf_op jit(solution)/shard_map/all_to_all | solution.py:507
  80.9 4.5 %shard_map.96 = (bf16[16,208,128]{2,1,0:T(8,128)(2,1)S(1)}, bf16[2,4,80,640]{3,2,1,0:T(8,128)(2,1)S(1)}, f32[4,80,1280]{2,1,0:T(8,128)S(1)}) custom-call(f32[4,8]{1,0:T(4,128)S(1)} %copy-done.4, bf16[2,2,320,640]{3,2,1,0:T(8,128)(2,1)S(1)} %copy-done.1, bf16[16,208,128]{2,1,0:T(8,128)(2,1)S(1)} %all_to_all.21.spectrum, ...), custom_call_target="tpu_custom_call" | custom-call | tf_op jit(solution)/shard_map/pallas_call | solution.py:512
  85.4 25.4 %all_to_all.22.spectrum = bf16[16,208,128]{2,1,0:T(8,128)(2,1)S(1)} all-to-all(bf16[16,208,128]{2,1,0:T(8,128)(2,1)S(1)} %get-tuple-element.35), channel_id=1, replica_groups=mesh['subj'=2,'band'=4,'lon'=2,'pop'=2] {'band','lon','pop'}, dimensions={0} | all-to-all | bytes 1703936 | tf_op jit(solution)/shard_map/all_to_all | solution.py:487
  110.8 10.7 %shard_map.97 = bf16[16,208,128]{2,1,0:T(8,128)(2,1)S(1)} custom-call(bf16[16,208,128]{2,1,0:T(8,128)(2,1)S(1)} %all_to_all.22.spectrum, f32[4,640]{1,0:T(4,128)S(1)} %copy-done.5, f32[8,8,640]{2,1,0:T(8,128)S(1)} %fusion.mixing, bf16[80,320,640]{2,1,0:T(8,128)(2,1)} %basis.3), custom_call_target="tpu_custom_call" | custom-call | flops 5000000000 | bytes 20000000 | tf_op jit(solution)/shard_map/pallas_call | solution.py:492
  121.5 25.4 %all_to_all.23.spectrum = bf16[16,208,128]{2,1,0:T(8,128)(2,1)S(1)} all-to-all(bf16[16,208,128]{2,1,0:T(8,128)(2,1)S(1)} %shard_map.97), channel_id=1, replica_groups=mesh['subj'=2,'band'=4,'lon'=2,'pop'=2] {'band','lon','pop'}, dimensions={0} | all-to-all | bytes 1703936 | tf_op jit(solution)/shard_map/all_to_all | solution.py:507
  146.9 1.6 shard_map.98
  148.5 1.0 collective-permute-start.4
  149.5 1.4 shard_map.100
  150.9 1.1 collective-permute-start.3
  152.0 2.0 %shard_map.99.kept = bf16[4,80,640]{2,1,0:T(8,128)(2,1)S(1)} custom-call(f32[4,8]{1,0:T(4,128)S(1)} %copy-done.4, bf16[2,2,320,640]{3,2,1,0:T(8,128)(2,1)S(1)} %copy-done.1, bf16[640,640]{1,0:T(8,128)(2,1)S(1)} %get-tuple-element.38.both, bf16[2,4,80,640]{3,2,1,0:T(8,128)(2,1)S(1)} %get-tuple-element.36.rates, f32[2,2,4,640]{3,2,1,0:T(4,128)S(1)} %get-tuple-element.39.halo, ...), custom_call_target="tpu_custom_call" | custom-call | flops 1000000000 | bytes 5000000 | tf_op jit(solution)/shard_map/pallas_call | solution.py:530
  154.0 2.5 %collective-permute-done.4.got = bf16[2,80,640]{2,1,0:T(8,128)(2,1)S(1)} collective-permute-done((bf16[2,80,640]{2,1,0:T(8,128)(2,1)S(1)}, bf16[2,80,640]{2,1,0:T(8,128)(2,1)S(1)}, u32[]{:S(2)}, u32[]{:S(2)}) %collective-permute-start.4) | collective-permute-done | bytes 204832 | tf_op jit(solution)/shard_map/ppermute | solution.py:540
  156.5 1.8 %shard_map.101.refs_0_ = f32[4,160,640]{2,1,0:T(8,128)} custom-call(f32[4,8]{1,0:T(4,128)S(1)} %copy-done.4, f32[4,160,640]{2,1,0:T(8,128)S(1)} %copy-done.2, bf16[4,160,640]{2,1,0:T(8,128)(2,1)S(1)} %copy-done.3, bf16[4,80,640]{2,1,0:T(8,128)(2,1)S(1)} %shard_map.99.kept, bf16[2,80,640]{2,1,0:T(8,128)(2,1)S(1)} %collective-permute-done.4.got), custom_call_target="tpu_custom_call" | custom-call | flops 10000000 | bytes 4000000 | tf_op jit(solution)/shard_map/pallas_call | solution.py:551
  158.3 2.4 %collective-permute-done.3.got = bf16[2,80,640]{2,1,0:T(8,128)(2,1)S(1)} collective-permute-done((bf16[2,80,640]{2,1,0:T(8,128)(2,1)S(1)}, bf16[2,80,640]{2,1,0:T(8,128)(2,1)S(1)}, u32[]{:S(2)}, u32[]{:S(2)}) %collective-permute-start.3) | collective-permute-done | bytes 204832 | tf_op jit(solution)/shard_map/ppermute | solution.py:541
  160.7 1.8 %shard_map.102 = f32[4,160,640]{2,1,0:T(8,128)} custom-call(f32[4,8]{1,0:T(4,128)S(1)} %copy-done.4, f32[4,160,640]{2,1,0:T(8,128)S(1)} %copy-done.2, bf16[4,160,640]{2,1,0:T(8,128)(2,1)S(1)} %copy-done.3, bf16[4,80,640]{2,1,0:T(8,128)(2,1)S(1)} %shard_map.99.kept, ...), custom_call_target="tpu_custom_call", output_to_operand_aliasing={{}: (5, {})} | custom-call | flops 10000000 | bytes 4000000 | tf_op jit(solution)/shard_map/pallas_call | solution.py:551
  (1 shorter events, 0.0 us)
Async XLA Ops:
  0.0 7.2 %copy-start = (f32[4,640]{1,0:T(4,128)S(1)}, f32[4,640]{1,0:T(4,128)}, u32[]{:S(2)}) copy-start(f32[4,640]{1,0:T(4,128)} %param.12) | copy-start | bytes 30724
  0.0 7.5 %copy-start.4 = (f32[4,8]{1,0:T(4,128)S(1)}, f32[4,8]{1,0:T(4,128)}, u32[]{:S(2)}) copy-start(f32[4,8]{1,0:T(4,128)} %params.17) | copy-start | bytes 388
  0.0 7.5 %copy-start.2 = (f32[4,160,640]{2,1,0:T(8,128)S(1)}, f32[4,160,640]{2,1,0:T(8,128)}, u32[]{:S(2)}) copy-start(f32[4,160,640]{2,1,0:T(8,128)} %act.9) | copy-start | bytes 4915204
  0.0 7.0 %copy-start.6 = (s32[8,8]{1,0:T(8,128)S(1)}, s32[8,8]{1,0:T(8,128)}, u32[]{:S(2)}) copy-start(s32[8,8]{1,0:T(8,128)} %param.13) | copy-start | bytes 772
  0.0 7.1 %copy-start.7 = (f32[8,8]{1,0:T(8,128)S(1)}, f32[8,8]{1,0:T(8,128)}, u32[]{:S(2)}) copy-start(f32[8,8]{1,0:T(8,128)} %param.14) | copy-start | bytes 772
  0.0 7.5 %copy-start.3 = (bf16[4,160,640]{2,1,0:T(8,128)(2,1)S(1)}, bf16[4,160,640]{2,1,0:T(8,128)(2,1)}, u32[]{:S(2)}) copy-start(bf16[4,160,640]{2,1,0:T(8,128)(2,1)} %drive.5) | copy-start | bytes 2457604
  2.1 9.1 %collective-permute-start = (bf16[2,80,640]{2,1,0:T(8,128)(2,1)}, bf16[2,80,640]{2,1,0:T(8,128)(2,1)S(1)}, u32[]{:S(2)}, u32[]{:S(2)}) collective-permute-start(bf16[2,80,640]{2,1,0:T(8,128)(2,1)} %shard_map.92), channel_id=1, source_target_pairs={{0,2},{2,0},{1,3},{3,1},{4,6},{6,4},{5,7},{7,5},{8,10},{10,8},{9,1... | collective-permute-start | bytes 614408 | tf_op jit(solution)/shard_map/ppermute | solution.py:467
  7.0 7.7 %collective-permute-start.1 = (bf16[2,80,640]{2,1,0:T(8,128)(2,1)}, bf16[2,80,640]{2,1,0:T(8,128)(2,1)S(1)}, u32[]{:S(2)}, u32[]{:S(2)}) collective-permute-start(bf16[2,80,640]{2,1,0:T(8,128)(2,1)} %shard_map.93), channel_id=1, source_target_pairs={{0,2},{2,0},{1,3},{3,1},{4,6},{6,4},{5,7},{7,5},{8,10},{10,8},{9,1... | collective-permute-start | bytes 614408 | tf_op jit(solution)/shard_map/ppermute | solution.py:467
  7.5 7.2 %copy-start.1 = (bf16[2,2,320,640]{3,2,1,0:T(8,128)(2,1)S(1)}, bf16[2,2,320,640]{3,2,1,0:T(8,128)(2,1)}, u32[]{:S(2)}) copy-start(bf16[2,2,320,640]{3,2,1,0:T(8,128)(2,1)} %constant.4.clone.table) | copy-start | bytes 4915204
  14.8 30.0 %copy-start.5 = (f32[4,640]{1,0:T(4,128)S(1)}, f32[4,640]{1,0:T(4,128)}, u32[]{:S(2)}) copy-start(f32[4,640]{1,0:T(4,128)} %constant.5.clone.weight) | copy-start | bytes 30724
  43.8 12.1 %collective-permute-start.2 = (bf16[4,80,640]{2,1,0:T(8,128)(2,1)S(1)}, bf16[4,80,640]{2,1,0:T(8,128)(2,1)S(1)}, u32[]{:S(2)}, u32[]{:S(2)}) collective-permute-start(bf16[4,80,640]{2,1,0:T(8,128)(2,1)S(1)} %get-tuple-element.30), channel_id=1, source_target_pairs={{0,2},{2,0},{1,3},{3,1},{4,6},{6,4},{5,7},{7,5},{8,10},{10,8},{9,1... | collective-permute-start | bytes 1228808 | tf_op jit(solution)/shard_map/ppermute | solution.py:489
  148.5 8.0 %collective-permute-start.4 = (bf16[2,80,640]{2,1,0:T(8,128)(2,1)S(1)}, bf16[2,80,640]{2,1,0:T(8,128)(2,1)S(1)}, u32[]{:S(2)}, u32[]{:S(2)}) collective-permute-start(bf16[2,80,640]{2,1,0:T(8,128)(2,1)S(1)} %get-tuple-element.40), channel_id=1, source_target_pairs={{0,2},{2,0},{1,3},{3,1},{4,6},{6,4},{5,7},{7,5},{8,10},{10,8},{9,1... | collective-permute-start | bytes 614408 | tf_op jit(solution)/shard_map/ppermute | solution.py:540
  150.9 9.8 %collective-permute-start.3 = (bf16[2,80,640]{2,1,0:T(8,128)(2,1)S(1)}, bf16[2,80,640]{2,1,0:T(8,128)(2,1)S(1)}, u32[]{:S(2)}, u32[]{:S(2)}) collective-permute-start(bf16[2,80,640]{2,1,0:T(8,128)(2,1)S(1)} %shard_map.100), channel_id=1, source_target_pairs={{0,2},{2,0},{1,3},{3,1},{4,6},{6,4},{5,7},{7,5},{8,10},{10,8},{9,1... | collective-permute-start | bytes 614408 | tf_op jit(solution)/shard_map/ppermute | solution.py:541

commit v6 on v5

--- a/solution.py
+++ b/solution.py
@@ -251,22 +251,21 @@
             odds.append((w * (north - south)).astype(BF16).astype(F32))
         for q in range(lots):
             for parts, scratch in ((evens, even_s), (odds, odd_s)):
-                strips = [v[:, q * piece : (q + 1) * piece] for v in parts]
+                spairs = [v[:, q * piece : (q + 1) * piece] for v in parts]
                 if pad:
-                    strips.append(jnp.zeros((count, pad), F32))
-                joined = jnp.concatenate(strips, axis=1)
+                    spairs.append(jnp.zeros((count, pad), F32))
+                joined = jnp.concatenate(spairs, axis=1)
                 for t in range(tiles):
                     scratch[t, rows_of(p, q), :] = joined[:, t * 128 : (t + 1) * 128]
 
     degree = lax.broadcasted_iota(jnp.int32, (2 * pops, deg), 1)
 
-    @pl.loop(0, count // block)
-    def _(step):
-        for at in range(block):
-            fetch(step * block + at).wait()
+    def several(start, size):
+        for at in range(size):
+            fetch(start + at).wait()
         todo = []
-        for at in range(block):
-            r = step * block + at
+        for at in range(size):
+            r = start + at
             m = first_wave + cores * r
             rows = pl.ds(r, 2 * pops, stride=count)
             lhs = jnp.concatenate(
@@ -299,6 +298,13 @@
                 north_s[t, rows, :] = field[: 2 * pops, t * 128 : (t + 1) * 128]
                 south_s[t, rows, :] = field[2 * pops :, t * 128 : (t + 1) * 128]
 
+    several(0, block // 2)
+    several(block // 2, block // 2)
+
+    @pl.loop(1, count // block)
+    def _(step):
+        several(step * block, block)
+
     for scratch, south in ((north_s, False), (south_s, True)):
         for p in range(cores):
             wide = [
@@ -309,8 +315,8 @@
             ]
             for s in range(src):
                 to = (2 * src - 1 - s if south else s) * cores + p
-                strips = [v[:, s * piece : (s + 1) * piece] for v in wide]
-                out[to] = packed(jnp.concatenate(strips, axis=1), passed[to], total)
+                spairs = [v[:, s * piece : (s + 1) * piece] for v in wide]
+                out[to] = packed(jnp.concatenate(spairs, axis=1), passed[to], total)
 
 
 def turned(spectrum, turned_s):
@@ -318,7 +324,7 @@
     lanes, deg = turned_s.shape
     order = list(range(0, groups, 2)) + list(range(1, groups, 2))
     blocks = [unpacked(spectrum[g], deg // groups, lanes) for g in order]
-    turned_s[...] = jnp.concatenate(blocks, axis=0).T.astype(BF16)
+    turned_s[...] = jnp.concatenate(blocks, axis=0).astype(BF16).T
 
 
 def put_ends(spectrum, turned_s, halo):
@@ -405,17 +411,12 @@
     put_inner(params, table, rates, halo, inner, both, here()[0], some, out)
 
 
-def grid_update_body(begin, params, act, drive, kept, got, *refs):
+def grid_update_body(begin, pops, params, act, drive, inner, *refs):
     out = refs[-1]
-    pops = begin + pl.num_programs(0) if begin else 2 * pl.num_programs(0)
     i = lax.axis_index("pop") * pops + begin + pl.program_id(0)
     keep = 1.0 - time_step * params[2, i]
-    rows = kept.shape[1]
-    lon = here()[0]
-    for half, inner in ((lon, kept), (1 - lon, got)):
-        d = time_step * half_of(drive, 0, half, rows).astype(F32)
-        at = pl.ds(pl.multiple_of(half * rows, 16), rows)
-        out[0, at, :] = keep * (keep * act[0, at, :] + d) + d + in_wire_order(inner[0])
+    d = time_step * drive[0].astype(F32)
+    out[0] = keep * (keep * act[0] + d) + d + in_wire_order(inner[0])
 
 
 def by_parts(activity, drive, basis, kernels, conn_block, coupling, rate_params):
@@ -462,7 +463,7 @@
                 scalars(),
                 pl.BlockSpec((some, rows, cols), lambda i, k=k: (k, 1 - lax.axis_index("lon"), 0)),
             ],
-            out_specs=pl.BlockSpec((some, rows, cols), lambda i: (0, 0, 0)),
+            out_specs=whole(),
         )(rate_params, activity)
         got.append(lax.ppermute(sent, "lon", swap))
     kept, carried_sent, carried_kept = call(
@@ -526,10 +527,10 @@
         out_specs=(whole(),) * 3,
     )(rate_params, table, back, rates, inner)
 
-    def inner_of(body, some, count):
+    def inner_of(body, which):
         return call(
-            functools.partial(body, some),
-            shape(count, rows, cols),
+            functools.partial(body, which),
+            shape(len(which), rows, cols),
             16,
             10**9,
             5 * 10**6,
@@ -537,35 +538,31 @@
             out_specs=whole(),
         )(rate_params, table, both, rates, halo, inner)
 
-    got = [lax.ppermute(sent, "lon", swap)]
-    got.append(lax.ppermute(inner_of(more_inner_body, pairs[1], len(pairs[1])), "lon", swap))
-    kept = inner_of(kept_inner_body, pairs[0] + pairs[1], pops_here)
-    out = None
-    for pair, there in zip(pairs, got):
-        begin = pair[0]
-
-        def on(tail, begin=begin):
-            return pl.BlockSpec((1,) + tail, lambda i: (begin + i, 0, 0))
-
-        earlier = [] if out is None else [out]
-        out = call(
-            functools.partial(grid_update_body, begin),
+    def update(which, half, inner, *earlier):
+        begin = which[0]
+        block = pl.BlockSpec(
+            (1, rows, cols),
+            lambda i: (begin + i, jnp.abs(half - lax.axis_index("lon")), 0),
+        )
+        return call(
+            functools.partial(grid_update_body, begin, pops_here),
             shape(*activity.shape, dtype=F32),
             24,
             10**7,
             4 * 10**6,
-            grid=(len(pair),),
-            in_specs=[
-                scalars(),
-                on((lat_here, cols)),
-                on((lat_here, cols)),
-                on((rows, cols)),
-                by_pop,
-            ]
+            grid=(len(which),),
+            in_specs=[scalars(), block, block, by_pop]
             + [pl.BlockSpec(memory_space=pl.ANY)] * len(earlier),
-            out_specs=on((lat_here, cols)),
-            input_output_aliases={5: 0} if earlier else {},
-        )(rate_params, activity, drive, kept, there, *earlier)
+            out_specs=block,
+            input_output_aliases={4: 0} if earlier else {},
+        )(rate_params, activity, drive, inner, *earlier)
+
+    got = [lax.ppermute(sent, "lon", swap)]
+    got.append(lax.ppermute(inner_of(more_inner_body, pairs[1]), "lon", swap))
+    everyone = pairs[0] + pairs[1]
+    out = update(everyone, 0, inner_of(kept_inner_body, everyone))
+    for pair, there in zip(pairs, got):
+        out = update(pair, 1, there, out)
     return out
 
 

time: 163 us -> 162 us (level)
  waiting for transfers between devices: 11.4 us -> 9.29 us
  Pallas kernels: 41.1 us -> 42.8 us
    ppermute x1, waiting for transfers between devices: 2.53 us -> 0.01 us  [by_parts(): got = [lax.ppermute(sent, 'lon', swap)]]
    pallas_call x4 -> x5, Pallas kernels: 6.86 us -> 9.14 us  [the longest x3 5.76 us: update(): call(functools.partial(grid_update_body, begin, pops_here), shape(*activi...]
  transfers between devices with their start and end apart: 5 -> 5, of which waited for: 5 -> 4; matrix products, arithmetic and copies ran while one was open for 0% -> 0% of each run, Pallas kernels for 12% -> 13%
where the time goes in v6:
time: 162 us
  blocking collectives  103 us (64%)
  Pallas kernels  42.8 us (26%)
  waiting for transfers between devices  9.29 us (6%)
  starting transfers between devices  6.13 us (4%)
    all_to_all x2, blocking collectives, coupled(): spectrum = lax.all_to_all(fourier, EVERYONE, 0, 0, tiled=True)  52.8 us
    all_to_all x2, blocking collectives, coupled(): back = lax.all_to_all(synthesis, EVERYONE, 0, 0, tiled=True)  50.4 us
    pallas_call x2, Pallas kernels, coupled(): call(functools.partial(legendre_body, nlon), wire, 40, 5 * 10 ** 9, 2 * 1...  20.8 us
    ppermute x2, waiting for transfers between devices, by_parts(): got.append(lax.ppermute(sent, 'lon', swap))  6.04 us
    pallas_call x3, Pallas kernels, update(): call(functools.partial(grid_update_body, begin, pops_here), shape(*activi...  5.76 us
    pallas_call x1, Pallas kernels, by_parts(): call(middle_body, (wire, both_halves, state), 32, in_specs=[scalars()] +...  4.56 us
    pallas_call x2, Pallas kernels, by_parts(): call(functools.partial(sent_rates_body, pair[0]), shape(some, rows, cols)...  4.03 us
    pallas_call x2, Pallas kernels, inner_of(): call(functools.partial(body, which), shape(len(which), rows, cols), 16, 1...  3.38 us
  transfers between devices with their start and end apart: 5, of which 4 were waited for; matrix products, arithmetic and copies ran while one was open for 0% of the time, Pallas kernels for 13%

profile of v6, /device:TPU:0, one launch (start us, length us, event | category | flops | bytes accessed | tf_op | source)
XLA Modules:
  0.0 162.0 jit_solution(4655606499687488143)
XLA Ops:
  0.0 0.0 copy-start
  0.0 0.0 copy-start.4
  0.0 0.0 copy-start.2
  0.0 0.0 copy-start.6
  0.0 0.0 copy-start.7
  0.0 0.0 copy-start.3
  0.0 2.1 %shard_map.92 = bf16[2,80,640]{2,1,0:T(8,128)(2,1)} custom-call(f32[4,8]{1,0:T(4,128)} %params.19, f32[4,160,640]{2,1,0:T(8,128)} %act.11), custom_call_target="tpu_custom_call" | custom-call | tf_op jit(solution)/shard_map/pallas_call | solution.py:457
  2.1 3.0 %collective-permute-start = (bf16[2,80,640]{2,1,0:T(8,128)(2,1)}, bf16[2,80,640]{2,1,0:T(8,128)(2,1)S(1)}, u32[]{:S(2)}, u32[]{:S(2)}) collective-permute-start(bf16[2,80,640]{2,1,0:T(8,128)(2,1)} %shard_map.92), channel_id=1, source_target_pairs={{0,2},{2,0},{1,3},{3,1},{4,6},{6,4},{5,7},{7,5},{8,10},{10,8},{9,1... | collective-permute-start | bytes 614408 | tf_op jit(solution)/shard_map/ppermute | solution.py:468
  5.1 1.9 %shard_map.93 = bf16[2,80,640]{2,1,0:T(8,128)(2,1)} custom-call(f32[4,8]{1,0:T(4,128)} %params.19, f32[4,160,640]{2,1,0:T(8,128)} %act.11), custom_call_target="tpu_custom_call" | custom-call | tf_op jit(solution)/shard_map/pallas_call | solution.py:457
  7.0 0.0 collective-permute-start.1
  7.0 0.0 copy-done.6
  7.0 0.1 copy.14
  7.1 0.0 copy-done.7
  7.1 0.1 copy.12
  7.2 0.0 copy-done
  7.2 0.3 fusion.mixing
  7.5 0.0 copy-done.4
  7.5 0.0 copy-done.2
  7.5 0.0 copy-done.3
  7.5 0.0 copy-start.1
  7.5 1.2 shard_map.91
  8.7 2.5 %collective-permute-done.got = bf16[2,80,640]{2,1,0:T(8,128)(2,1)S(1)} collective-permute-done((bf16[2,80,640]{2,1,0:T(8,128)(2,1)}, bf16[2,80,640]{2,1,0:T(8,128)(2,1)S(1)}, u32[]{:S(2)}, u32[]{:S(2)}) %collective-permute-start) | collective-permute-done | bytes 204832 | tf_op jit(solution)/shard_map/ppermute | solution.py:468
  11.2 3.6 %collective-permute-done.1.got_more = bf16[2,80,640]{2,1,0:T(8,128)(2,1)S(1)} collective-permute-done((bf16[2,80,640]{2,1,0:T(8,128)(2,1)}, bf16[2,80,640]{2,1,0:T(8,128)(2,1)S(1)}, u32[]{:S(2)}, u32[]{:S(2)}) %collective-permute-start.1) | collective-permute-done | bytes 204832 | tf_op jit(solution)/shard_map/ppermute | solution.py:468
  14.8 0.0 copy-done.1
  14.8 0.0 copy-start.5
  14.8 1.7 %shard_map.94 = (bf16[16,208,128]{2,1,0:T(8,128)(2,1)S(1)}, bf16[2,4,80,640]{3,2,1,0:T(8,128)(2,1)S(1)}) custom-call(bf16[2,2,320,640]{3,2,1,0:T(8,128)(2,1)S(1)} %copy-done.1, bf16[4,80,640]{2,1,0:T(8,128)(2,1)S(1)} %get-tuple-element.23.kept, bf16[2,80,640]{2,1,0:T(8,128)(2,1)S(1)} %collective-permute-done.got, ...), custom_call_target="tpu_custom_call" | custom-call | tf_op jit(solution)/shard_map/pallas_call | solution.py:479
  16.5 27.4 %all_to_all.20.spectrum = bf16[16,208,128]{2,1,0:T(8,128)(2,1)S(1)} all-to-all(bf16[16,208,128]{2,1,0:T(8,128)(2,1)S(1)} %get-tuple-element.26), channel_id=1, replica_groups=mesh['subj'=2,'band'=4,'lon'=2,'pop'=2] {'band','lon','pop'}, dimensions={0} | all-to-all | bytes 1703936 | tf_op jit(solution)/shard_map/all_to_all | solution.py:488
  43.8 1.0 collective-permute-start.2
  44.8 0.0 copy-done.5
  44.8 10.4 %shard_map.95 = bf16[16,208,128]{2,1,0:T(8,128)(2,1)S(1)} custom-call(bf16[16,208,128]{2,1,0:T(8,128)(2,1)S(1)} %all_to_all.20.spectrum, f32[4,640]{1,0:T(4,128)S(1)} %copy-done.5, f32[8,8,640]{2,1,0:T(8,128)S(1)} %fusion.mixing, bf16[80,320,640]{2,1,0:T(8,128)(2,1)} %basis.3), custom_call_target="tpu_custom_call" | custom-call | flops 5000000000 | bytes 20000000 | tf_op jit(solution)/shard_map/pallas_call | solution.py:493
  55.2 0.8 collective-permute-done.2.got
  56.0 24.9 %all_to_all.21.spectrum = bf16[16,208,128]{2,1,0:T(8,128)(2,1)S(1)} all-to-all(bf16[16,208,128]{2,1,0:T(8,128)(2,1)S(1)} %shard_map.95), channel_id=1, replica_groups=mesh['subj'=2,'band'=4,'lon'=2,'pop'=2] {'band','lon','pop'}, dimensions={0} | all-to-all | bytes 1703936 | tf_op jit(solution)/shard_map/all_to_all | solution.py:508
  80.9 4.6 %shard_map.96 = (bf16[16,208,128]{2,1,0:T(8,128)(2,1)S(1)}, bf16[2,4,80,640]{3,2,1,0:T(8,128)(2,1)S(1)}, f32[4,80,1280]{2,1,0:T(8,128)S(1)}) custom-call(f32[4,8]{1,0:T(4,128)S(1)} %copy-done.4, bf16[2,2,320,640]{3,2,1,0:T(8,128)(2,1)S(1)} %copy-done.1, bf16[16,208,128]{2,1,0:T(8,128)(2,1)S(1)} %all_to_all.21.spectrum, ...), custom_call_target="tpu_custom_call" | custom-call | tf_op jit(solution)/shard_map/pallas_call | solution.py:513
  85.5 25.4 %all_to_all.22.spectrum = bf16[16,208,128]{2,1,0:T(8,128)(2,1)S(1)} all-to-all(bf16[16,208,128]{2,1,0:T(8,128)(2,1)S(1)} %get-tuple-element.35), channel_id=1, replica_groups=mesh['subj'=2,'band'=4,'lon'=2,'pop'=2] {'band','lon','pop'}, dimensions={0} | all-to-all | bytes 1703936 | tf_op jit(solution)/shard_map/all_to_all | solution.py:488
  110.9 10.4 %shard_map.97 = bf16[16,208,128]{2,1,0:T(8,128)(2,1)S(1)} custom-call(bf16[16,208,128]{2,1,0:T(8,128)(2,1)S(1)} %all_to_all.22.spectrum, f32[4,640]{1,0:T(4,128)S(1)} %copy-done.5, f32[8,8,640]{2,1,0:T(8,128)S(1)} %fusion.mixing, bf16[80,320,640]{2,1,0:T(8,128)(2,1)} %basis.3), custom_call_target="tpu_custom_call" | custom-call | flops 5000000000 | bytes 20000000 | tf_op jit(solution)/shard_map/pallas_call | solution.py:493
  121.3 25.4 %all_to_all.23.spectrum = bf16[16,208,128]{2,1,0:T(8,128)(2,1)S(1)} all-to-all(bf16[16,208,128]{2,1,0:T(8,128)(2,1)S(1)} %shard_map.97), channel_id=1, replica_groups=mesh['subj'=2,'band'=4,'lon'=2,'pop'=2] {'band','lon','pop'}, dimensions={0} | all-to-all | bytes 1703936 | tf_op jit(solution)/shard_map/all_to_all | solution.py:508
  146.7 1.5 shard_map.98
  148.2 1.1 collective-permute-start.4
  149.3 1.4 shard_map.99
  150.6 1.1 collective-permute-start.3
  151.7 2.0 %shard_map.100.inner = bf16[4,80,640]{2,1,0:T(8,128)(2,1)S(1)} custom-call(f32[4,8]{1,0:T(4,128)S(1)} %copy-done.4, bf16[2,2,320,640]{3,2,1,0:T(8,128)(2,1)S(1)} %copy-done.1, bf16[640,640]{1,0:T(8,128)(2,1)S(1)} %get-tuple-element.38.both, bf16[2,4,80,640]{3,2,1,0:T(8,128)(2,1)S(1)} %get-tuple-element.36.rates, ...), custom_call_target="tpu_custom_call" | custom-call | flops 1000000000 | bytes 5000000 | tf_op jit(solution)/shard_map/pallas_call | solution.py:531
  153.8 2.5 %shard_map.101.refs_0_ = f32[4,160,640]{2,1,0:T(8,128)} custom-call(f32[4,8]{1,0:T(4,128)S(1)} %copy-done.4, f32[4,160,640]{2,1,0:T(8,128)S(1)} %copy-done.2, bf16[4,160,640]{2,1,0:T(8,128)(2,1)S(1)} %copy-done.3, bf16[4,80,640]{2,1,0:T(8,128)(2,1)S(1)} %shard_map.100.inner), custom_call_target="tpu_custom_call" | custom-call | flops 10000000 | bytes 4000000 | tf_op jit(solution)/shard_map/pallas_call | solution.py:547
  156.3 0.0 collective-permute-done.4.inner
  156.3 1.6 shard_map.102.refs_0_
  157.9 2.5 %collective-permute-done.3.inner = bf16[2,80,640]{2,1,0:T(8,128)(2,1)S(1)} collective-permute-done((bf16[2,80,640]{2,1,0:T(8,128)(2,1)S(1)}, bf16[2,80,640]{2,1,0:T(8,128)(2,1)S(1)}, u32[]{:S(2)}, u32[]{:S(2)}) %collective-permute-start.3) | collective-permute-done | bytes 204832 | tf_op jit(solution)/shard_map/ppermute | solution.py:561
  160.4 1.6 shard_map.103
  (1 shorter events, 0.0 us)
Async XLA Ops:
  0.0 7.2 %copy-start = (f32[4,640]{1,0:T(4,128)S(1)}, f32[4,640]{1,0:T(4,128)}, u32[]{:S(2)}) copy-start(f32[4,640]{1,0:T(4,128)} %param.12) | copy-start | bytes 30724
  0.0 7.5 %copy-start.4 = (f32[4,8]{1,0:T(4,128)S(1)}, f32[4,8]{1,0:T(4,128)}, u32[]{:S(2)}) copy-start(f32[4,8]{1,0:T(4,128)} %params.19) | copy-start | bytes 388
  0.0 7.5 %copy-start.2 = (f32[4,160,640]{2,1,0:T(8,128)S(1)}, f32[4,160,640]{2,1,0:T(8,128)}, u32[]{:S(2)}) copy-start(f32[4,160,640]{2,1,0:T(8,128)} %act.11) | copy-start | bytes 4915204
  0.0 7.0 %copy-start.6 = (s32[8,8]{1,0:T(8,128)S(1)}, s32[8,8]{1,0:T(8,128)}, u32[]{:S(2)}) copy-start(s32[8,8]{1,0:T(8,128)} %param.13) | copy-start | bytes 772
  0.0 7.1 %copy-start.7 = (f32[8,8]{1,0:T(8,128)S(1)}, f32[8,8]{1,0:T(8,128)}, u32[]{:S(2)}) copy-start(f32[8,8]{1,0:T(8,128)} %param.14) | copy-start | bytes 772
  0.0 7.5 %copy-start.3 = (bf16[4,160,640]{2,1,0:T(8,128)(2,1)S(1)}, bf16[4,160,640]{2,1,0:T(8,128)(2,1)}, u32[]{:S(2)}) copy-start(bf16[4,160,640]{2,1,0:T(8,128)(2,1)} %drive.7) | copy-start | bytes 2457604
  2.1 9.1 %collective-permute-start = (bf16[2,80,640]{2,1,0:T(8,128)(2,1)}, bf16[2,80,640]{2,1,0:T(8,128)(2,1)S(1)}, u32[]{:S(2)}, u32[]{:S(2)}) collective-permute-start(bf16[2,80,640]{2,1,0:T(8,128)(2,1)} %shard_map.92), channel_id=1, source_target_pairs={{0,2},{2,0},{1,3},{3,1},{4,6},{6,4},{5,7},{7,5},{8,10},{10,8},{9,1... | collective-permute-start | bytes 614408 | tf_op jit(solution)/shard_map/ppermute | solution.py:468
  7.0 7.7 %collective-permute-start.1 = (bf16[2,80,640]{2,1,0:T(8,128)(2,1)}, bf16[2,80,640]{2,1,0:T(8,128)(2,1)S(1)}, u32[]{:S(2)}, u32[]{:S(2)}) collective-permute-start(bf16[2,80,640]{2,1,0:T(8,128)(2,1)} %shard_map.93), channel_id=1, source_target_pairs={{0,2},{2,0},{1,3},{3,1},{4,6},{6,4},{5,7},{7,5},{8,10},{10,8},{9,1... | collective-permute-start | bytes 614408 | tf_op jit(solution)/shard_map/ppermute | solution.py:468
  7.5 7.2 %copy-start.1 = (bf16[2,2,320,640]{3,2,1,0:T(8,128)(2,1)S(1)}, bf16[2,2,320,640]{3,2,1,0:T(8,128)(2,1)}, u32[]{:S(2)}) copy-start(bf16[2,2,320,640]{3,2,1,0:T(8,128)(2,1)} %constant.4.clone.table) | copy-start | bytes 4915204
  14.8 30.1 %copy-start.5 = (f32[4,640]{1,0:T(4,128)S(1)}, f32[4,640]{1,0:T(4,128)}, u32[]{:S(2)}) copy-start(f32[4,640]{1,0:T(4,128)} %constant.5.clone.weight) | copy-start | bytes 30724
  43.8 12.1 %collective-permute-start.2 = (bf16[4,80,640]{2,1,0:T(8,128)(2,1)S(1)}, bf16[4,80,640]{2,1,0:T(8,128)(2,1)S(1)}, u32[]{:S(2)}, u32[]{:S(2)}) collective-permute-start(bf16[4,80,640]{2,1,0:T(8,128)(2,1)S(1)} %get-tuple-element.30), channel_id=1, source_target_pairs={{0,2},{2,0},{1,3},{3,1},{4,6},{6,4},{5,7},{7,5},{8,10},{10,8},{9,1... | collective-permute-start | bytes 1228808 | tf_op jit(solution)/shard_map/ppermute | solution.py:490
  148.2 8.1 %collective-permute-start.4 = (bf16[2,80,640]{2,1,0:T(8,128)(2,1)S(1)}, bf16[2,80,640]{2,1,0:T(8,128)(2,1)S(1)}, u32[]{:S(2)}, u32[]{:S(2)}) collective-permute-start(bf16[2,80,640]{2,1,0:T(8,128)(2,1)S(1)} %get-tuple-element.40), channel_id=1, source_target_pairs={{0,2},{2,0},{1,3},{3,1},{4,6},{6,4},{5,7},{7,5},{8,10},{10,8},{9,1... | collective-permute-start | bytes 614408 | tf_op jit(solution)/shard_map/ppermute | solution.py:560
  150.6 9.8 %collective-permute-start.3 = (bf16[2,80,640]{2,1,0:T(8,128)(2,1)S(1)}, bf16[2,80,640]{2,1,0:T(8,128)(2,1)S(1)}, u32[]{:S(2)}, u32[]{:S(2)}) collective-permute-start(bf16[2,80,640]{2,1,0:T(8,128)(2,1)S(1)} %shard_map.99), channel_id=1, source_target_pairs={{0,2},{2,0},{1,3},{3,1},{4,6},{6,4},{5,7},{7,5},{8,10},{10,8},{9,1... | collective-permute-start | bytes 614408 | tf_op jit(solution)/shard_map/ppermute | solution.py:561

commit v7 on v6

--- a/solution.py
+++ b/solution.py
@@ -147,24 +147,18 @@
     nothing = [jnp.zeros((1, 128), F32)] * (slots * groups - len(polar))
     polar, inner = polar + nothing, inner + nothing
     one, two = rates[0].astype(F32), rates[1].astype(F32)
-    pack = groups // 4
-    block = pack * count
     for p, mix in enumerate((one + two - 1.0, one - two)):
         flat = mix.astype(BF16).reshape(pops * rows, cols)
-        for b in range(waves // block):
-            parts = []
-            for c in range(2):
-                t = table[c, p, b * block : (b + 1) * block]
-                sums = nt_dot(t, flat)
-                if p == 0:
-                    sums = sums + jnp.sum(t.astype(F32), axis=1, keepdims=True)
-                parts.append(sums)
-            joined = jnp.concatenate(parts, axis=1)
-            for k in range(pack):
-                to = (b * pack + k) * 2 + p
-                at = slice(to * slots, (to + 1) * slots)
-                sums = joined[k * count : (k + 1) * count]
-                fourier[to] = packed(sums, polar[at] + inner[at], total)
+        t = jnp.concatenate([table[0, p], table[1, p]], axis=0)
+        sums = nt_dot(t, flat)
+        if p == 0:
+            sums = sums + jnp.sum(t.astype(F32), axis=1, keepdims=True)
+        for k in range(groups // 2):
+            own = slice(k * count, (k + 1) * count)
+            joined = jnp.concatenate([sums[:waves][own], sums[waves:][own]], axis=1)
+            to = k * 2 + p
+            at = slice(to * slots, (to + 1) * slots)
+            fourier[to] = packed(joined, polar[at] + inner[at], total)
 
 
 def first_fourier_body(table, kept, got, got_more, fourier, rates):

time: 162 us -> 161 us (level)
  no operation moved by 1% of the time
where the time goes in v7:
time: 161 us
  blocking collectives  103 us (64%)
  Pallas kernels  42 us (26%)
  waiting for transfers between devices  9.29 us (6%)
  starting transfers between devices  6.12 us (4%)
    all_to_all x2, blocking collectives, coupled(): spectrum = lax.all_to_all(fourier, EVERYONE, 0, 0, tiled=True)  52.8 us
    all_to_all x2, blocking collectives, coupled(): back = lax.all_to_all(synthesis, EVERYONE, 0, 0, tiled=True)  50.4 us
    pallas_call x2, Pallas kernels, coupled(): call(functools.partial(legendre_body, nlon), wire, 40, 5 * 10 ** 9, 2 * 1...  20.8 us
    ppermute x2, waiting for transfers between devices, by_parts(): got.append(lax.ppermute(sent, 'lon', swap))  6.04 us
    pallas_call x3, Pallas kernels, update(): call(functools.partial(grid_update_body, begin, pops_here), shape(*activi...  5.76 us
    pallas_call x1, Pallas kernels, by_parts(): call(middle_body, (wire, both_halves, state), 32, in_specs=[scalars()] +...  4.09 us
    pallas_call x2, Pallas kernels, by_parts(): call(functools.partial(sent_rates_body, pair[0]), shape(some, rows, cols)...  4.03 us
    pallas_call x2, Pallas kernels, inner_of(): call(functools.partial(body, which), shape(len(which), rows, cols), 16, 1...  3.4 us
  transfers between devices with their start and end apart: 5, of which 4 were waited for; matrix products, arithmetic and copies ran while one was open for 0% of the time, Pallas kernels for 13%

profile of v7, /device:TPU:0, one launch (start us, length us, event | category | flops | bytes accessed | tf_op | source)
XLA Modules:
  0.0 161.2 jit_solution(16953512703964757788)
XLA Ops:
  0.0 0.0 copy-start
  0.0 0.0 copy-start.4
  0.0 0.0 copy-start.2
  0.0 0.0 copy-start.6
  0.0 0.0 copy-start.7
  0.0 0.0 copy-start.3
  0.0 2.1 %shard_map.92 = bf16[2,80,640]{2,1,0:T(8,128)(2,1)} custom-call(f32[4,8]{1,0:T(4,128)} %params.19, f32[4,160,640]{2,1,0:T(8,128)} %act.11), custom_call_target="tpu_custom_call" | custom-call | tf_op jit(solution)/shard_map/pallas_call | solution.py:451
  2.1 3.0 %collective-permute-start = (bf16[2,80,640]{2,1,0:T(8,128)(2,1)}, bf16[2,80,640]{2,1,0:T(8,128)(2,1)S(1)}, u32[]{:S(2)}, u32[]{:S(2)}) collective-permute-start(bf16[2,80,640]{2,1,0:T(8,128)(2,1)} %shard_map.92), channel_id=1, source_target_pairs={{0,2},{2,0},{1,3},{3,1},{4,6},{6,4},{5,7},{7,5},{8,10},{10,8},{9,1... | collective-permute-start | bytes 614408 | tf_op jit(solution)/shard_map/ppermute | solution.py:462
  5.1 1.9 %shard_map.93 = bf16[2,80,640]{2,1,0:T(8,128)(2,1)} custom-call(f32[4,8]{1,0:T(4,128)} %params.19, f32[4,160,640]{2,1,0:T(8,128)} %act.11), custom_call_target="tpu_custom_call" | custom-call | tf_op jit(solution)/shard_map/pallas_call | solution.py:451
  7.0 0.0 collective-permute-start.1
  7.0 0.0 copy-done.6
  7.0 0.1 copy.14
  7.1 0.0 copy-done.7
  7.1 0.1 copy.12
  7.2 0.0 copy-done
  7.2 0.3 fusion.mixing
  7.5 0.0 copy-done.4
  7.5 0.0 copy-done.2
  7.5 0.0 copy-done.3
  7.5 0.0 copy-start.1
  7.5 1.2 shard_map.91
  8.7 2.5 %collective-permute-done.got = bf16[2,80,640]{2,1,0:T(8,128)(2,1)S(1)} collective-permute-done((bf16[2,80,640]{2,1,0:T(8,128)(2,1)}, bf16[2,80,640]{2,1,0:T(8,128)(2,1)S(1)}, u32[]{:S(2)}, u32[]{:S(2)}) %collective-permute-start) | collective-permute-done | bytes 204832 | tf_op jit(solution)/shard_map/ppermute | solution.py:462
  11.2 3.6 %collective-permute-done.1.got_more = bf16[2,80,640]{2,1,0:T(8,128)(2,1)S(1)} collective-permute-done((bf16[2,80,640]{2,1,0:T(8,128)(2,1)}, bf16[2,80,640]{2,1,0:T(8,128)(2,1)S(1)}, u32[]{:S(2)}, u32[]{:S(2)}) %collective-permute-start.1) | collective-permute-done | bytes 204832 | tf_op jit(solution)/shard_map/ppermute | solution.py:462
  14.8 0.0 copy-done.1
  14.8 0.0 copy-start.5
  14.8 1.3 shard_map.94
  16.1 27.4 %all_to_all.20.spectrum = bf16[16,208,128]{2,1,0:T(8,128)(2,1)S(1)} all-to-all(bf16[16,208,128]{2,1,0:T(8,128)(2,1)S(1)} %get-tuple-element.26), channel_id=1, replica_groups=mesh['subj'=2,'band'=4,'lon'=2,'pop'=2] {'band','lon','pop'}, dimensions={0} | all-to-all | bytes 1703936 | tf_op jit(solution)/shard_map/all_to_all | solution.py:482
  43.5 1.0 collective-permute-start.2
  44.5 0.0 copy-done.5
  44.5 10.4 %shard_map.95 = bf16[16,208,128]{2,1,0:T(8,128)(2,1)S(1)} custom-call(bf16[16,208,128]{2,1,0:T(8,128)(2,1)S(1)} %all_to_all.20.spectrum, f32[4,640]{1,0:T(4,128)S(1)} %copy-done.5, f32[8,8,640]{2,1,0:T(8,128)S(1)} %fusion.mixing, bf16[80,320,640]{2,1,0:T(8,128)(2,1)} %basis.3), custom_call_target="tpu_custom_call" | custom-call | flops 5000000000 | bytes 20000000 | tf_op jit(solution)/shard_map/pallas_call | solution.py:487
  54.9 0.8 collective-permute-done.2.got
  55.6 24.9 %all_to_all.21.spectrum = bf16[16,208,128]{2,1,0:T(8,128)(2,1)S(1)} all-to-all(bf16[16,208,128]{2,1,0:T(8,128)(2,1)S(1)} %shard_map.95), channel_id=1, replica_groups=mesh['subj'=2,'band'=4,'lon'=2,'pop'=2] {'band','lon','pop'}, dimensions={0} | all-to-all | bytes 1703936 | tf_op jit(solution)/shard_map/all_to_all | solution.py:502
  80.6 4.1 %shard_map.96 = (bf16[16,208,128]{2,1,0:T(8,128)(2,1)S(1)}, bf16[2,4,80,640]{3,2,1,0:T(8,128)(2,1)S(1)}, f32[4,80,1280]{2,1,0:T(8,128)S(1)}) custom-call(f32[4,8]{1,0:T(4,128)S(1)} %copy-done.4, bf16[2,2,320,640]{3,2,1,0:T(8,128)(2,1)S(1)} %copy-done.1, bf16[16,208,128]{2,1,0:T(8,128)(2,1)S(1)} %all_to_all.21.spectrum, ...), custom_call_target="tpu_custom_call" | custom-call | tf_op jit(solution)/shard_map/pallas_call | solution.py:507
  84.7 25.4 %all_to_all.22.spectrum = bf16[16,208,128]{2,1,0:T(8,128)(2,1)S(1)} all-to-all(bf16[16,208,128]{2,1,0:T(8,128)(2,1)S(1)} %get-tuple-element.35), channel_id=1, replica_groups=mesh['subj'=2,'band'=4,'lon'=2,'pop'=2] {'band','lon','pop'}, dimensions={0} | all-to-all | bytes 1703936 | tf_op jit(solution)/shard_map/all_to_all | solution.py:482
  110.1 10.4 %shard_map.97 = bf16[16,208,128]{2,1,0:T(8,128)(2,1)S(1)} custom-call(bf16[16,208,128]{2,1,0:T(8,128)(2,1)S(1)} %all_to_all.22.spectrum, f32[4,640]{1,0:T(4,128)S(1)} %copy-done.5, f32[8,8,640]{2,1,0:T(8,128)S(1)} %fusion.mixing, bf16[80,320,640]{2,1,0:T(8,128)(2,1)} %basis.3), custom_call_target="tpu_custom_call" | custom-call | flops 5000000000 | bytes 20000000 | tf_op jit(solution)/shard_map/pallas_call | solution.py:487
  120.5 25.4 %all_to_all.23.spectrum = bf16[16,208,128]{2,1,0:T(8,128)(2,1)S(1)} all-to-all(bf16[16,208,128]{2,1,0:T(8,128)(2,1)S(1)} %shard_map.97), channel_id=1, replica_groups=mesh['subj'=2,'band'=4,'lon'=2,'pop'=2] {'band','lon','pop'}, dimensions={0} | all-to-all | bytes 1703936 | tf_op jit(solution)/shard_map/all_to_all | solution.py:502
  145.9 1.5 shard_map.98
  147.4 1.1 collective-permute-start.4
  148.5 1.4 shard_map.99
  149.8 1.1 collective-permute-start.3
  150.9 2.0 %shard_map.100.inner = bf16[4,80,640]{2,1,0:T(8,128)(2,1)S(1)} custom-call(f32[4,8]{1,0:T(4,128)S(1)} %copy-done.4, bf16[2,2,320,640]{3,2,1,0:T(8,128)(2,1)S(1)} %copy-done.1, bf16[640,640]{1,0:T(8,128)(2,1)S(1)} %get-tuple-element.38.both, bf16[2,4,80,640]{3,2,1,0:T(8,128)(2,1)S(1)} %get-tuple-element.36.rates, ...), custom_call_target="tpu_custom_call" | custom-call | flops 1000000000 | bytes 5000000 | tf_op jit(solution)/shard_map/pallas_call | solution.py:525
  152.9 2.5 %shard_map.101.refs_0_ = f32[4,160,640]{2,1,0:T(8,128)} custom-call(f32[4,8]{1,0:T(4,128)S(1)} %copy-done.4, f32[4,160,640]{2,1,0:T(8,128)S(1)} %copy-done.2, bf16[4,160,640]{2,1,0:T(8,128)(2,1)S(1)} %copy-done.3, bf16[4,80,640]{2,1,0:T(8,128)(2,1)S(1)} %shard_map.100.inner), custom_call_target="tpu_custom_call" | custom-call | flops 10000000 | bytes 4000000 | tf_op jit(solution)/shard_map/pallas_call | solution.py:541
  155.5 0.0 collective-permute-done.4.inner
  155.5 1.6 %shard_map.102.refs_0_ = f32[4,160,640]{2,1,0:T(8,128)} custom-call(f32[4,8]{1,0:T(4,128)S(1)} %copy-done.4, f32[4,160,640]{2,1,0:T(8,128)S(1)} %copy-done.2, bf16[4,160,640]{2,1,0:T(8,128)(2,1)S(1)} %copy-done.3, bf16[2,80,640]{2,1,0:T(8,128)(2,1)S(1)} %collective-permute-done.4.inner, ...), custom_call_target="tpu_custom_call", output_to_operand_aliasing={{}: (4, {})} | custom-call | flops 10000000 | bytes 4000000 | tf_op jit(solution)/shard_map/pallas_call | solution.py:541
  157.1 2.5 %collective-permute-done.3.inner = bf16[2,80,640]{2,1,0:T(8,128)(2,1)S(1)} collective-permute-done((bf16[2,80,640]{2,1,0:T(8,128)(2,1)S(1)}, bf16[2,80,640]{2,1,0:T(8,128)(2,1)S(1)}, u32[]{:S(2)}, u32[]{:S(2)}) %collective-permute-start.3) | collective-permute-done | bytes 204832 | tf_op jit(solution)/shard_map/ppermute | solution.py:555
  159.6 1.6 %shard_map.103 = f32[4,160,640]{2,1,0:T(8,128)} custom-call(f32[4,8]{1,0:T(4,128)S(1)} %copy-done.4, f32[4,160,640]{2,1,0:T(8,128)S(1)} %copy-done.2, bf16[4,160,640]{2,1,0:T(8,128)(2,1)S(1)} %copy-done.3, bf16[2,80,640]{2,1,0:T(8,128)(2,1)S(1)} %collective-permute-done.3.inner, f32[4,160,640]{2,1,0:T(8,128)} %shard_map.102.refs_0_), custom_call_target="tpu_custom_call", output_to_operand_aliasing={{}: (4, {})} | custom-call | flops 10000000 | bytes 4000000 | tf_op jit(solution)/shard_map/pallas_call | solution.py:541
  (1 shorter events, 0.0 us)
Async XLA Ops:
  0.0 7.2 %copy-start = (f32[4,640]{1,0:T(4,128)S(1)}, f32[4,640]{1,0:T(4,128)}, u32[]{:S(2)}) copy-start(f32[4,640]{1,0:T(4,128)} %param.12) | copy-start | bytes 30724
  0.0 7.5 %copy-start.4 = (f32[4,8]{1,0:T(4,128)S(1)}, f32[4,8]{1,0:T(4,128)}, u32[]{:S(2)}) copy-start(f32[4,8]{1,0:T(4,128)} %params.19) | copy-start | bytes 388
  0.0 7.5 %copy-start.2 = (f32[4,160,640]{2,1,0:T(8,128)S(1)}, f32[4,160,640]{2,1,0:T(8,128)}, u32[]{:S(2)}) copy-start(f32[4,160,640]{2,1,0:T(8,128)} %act.11) | copy-start | bytes 4915204
  0.0 7.0 %copy-start.6 = (s32[8,8]{1,0:T(8,128)S(1)}, s32[8,8]{1,0:T(8,128)}, u32[]{:S(2)}) copy-start(s32[8,8]{1,0:T(8,128)} %param.13) | copy-start | bytes 772
  0.0 7.1 %copy-start.7 = (f32[8,8]{1,0:T(8,128)S(1)}, f32[8,8]{1,0:T(8,128)}, u32[]{:S(2)}) copy-start(f32[8,8]{1,0:T(8,128)} %param.14) | copy-start | bytes 772
  0.0 7.5 %copy-start.3 = (bf16[4,160,640]{2,1,0:T(8,128)(2,1)S(1)}, bf16[4,160,640]{2,1,0:T(8,128)(2,1)}, u32[]{:S(2)}) copy-start(bf16[4,160,640]{2,1,0:T(8,128)(2,1)} %drive.7) | copy-start | bytes 2457604
  2.1 9.1 %collective-permute-start = (bf16[2,80,640]{2,1,0:T(8,128)(2,1)}, bf16[2,80,640]{2,1,0:T(8,128)(2,1)S(1)}, u32[]{:S(2)}, u32[]{:S(2)}) collective-permute-start(bf16[2,80,640]{2,1,0:T(8,128)(2,1)} %shard_map.92), channel_id=1, source_target_pairs={{0,2},{2,0},{1,3},{3,1},{4,6},{6,4},{5,7},{7,5},{8,10},{10,8},{9,1... | collective-permute-start | bytes 614408 | tf_op jit(solution)/shard_map/ppermute | solution.py:462
  7.0 7.7 %collective-permute-start.1 = (bf16[2,80,640]{2,1,0:T(8,128)(2,1)}, bf16[2,80,640]{2,1,0:T(8,128)(2,1)S(1)}, u32[]{:S(2)}, u32[]{:S(2)}) collective-permute-start(bf16[2,80,640]{2,1,0:T(8,128)(2,1)} %shard_map.93), channel_id=1, source_target_pairs={{0,2},{2,0},{1,3},{3,1},{4,6},{6,4},{5,7},{7,5},{8,10},{10,8},{9,1... | collective-permute-start | bytes 614408 | tf_op jit(solution)/shard_map/ppermute | solution.py:462
  7.5 7.2 %copy-start.1 = (bf16[2,2,320,640]{3,2,1,0:T(8,128)(2,1)S(1)}, bf16[2,2,320,640]{3,2,1,0:T(8,128)(2,1)}, u32[]{:S(2)}) copy-start(bf16[2,2,320,640]{3,2,1,0:T(8,128)(2,1)} %constant.4.clone.table) | copy-start | bytes 4915204
  14.8 29.7 %copy-start.5 = (f32[4,640]{1,0:T(4,128)S(1)}, f32[4,640]{1,0:T(4,128)}, u32[]{:S(2)}) copy-start(f32[4,640]{1,0:T(4,128)} %constant.5.clone.weight) | copy-start | bytes 30724
  43.5 12.1 %collective-permute-start.2 = (bf16[4,80,640]{2,1,0:T(8,128)(2,1)S(1)}, bf16[4,80,640]{2,1,0:T(8,128)(2,1)S(1)}, u32[]{:S(2)}, u32[]{:S(2)}) collective-permute-start(bf16[4,80,640]{2,1,0:T(8,128)(2,1)S(1)} %get-tuple-element.30), channel_id=1, source_target_pairs={{0,2},{2,0},{1,3},{3,1},{4,6},{6,4},{5,7},{7,5},{8,10},{10,8},{9,1... | collective-permute-start | bytes 1228808 | tf_op jit(solution)/shard_map/ppermute | solution.py:484
  147.4 8.1 %collective-permute-start.4 = (bf16[2,80,640]{2,1,0:T(8,128)(2,1)S(1)}, bf16[2,80,640]{2,1,0:T(8,128)(2,1)S(1)}, u32[]{:S(2)}, u32[]{:S(2)}) collective-permute-start(bf16[2,80,640]{2,1,0:T(8,128)(2,1)S(1)} %get-tuple-element.40), channel_id=1, source_target_pairs={{0,2},{2,0},{1,3},{3,1},{4,6},{6,4},{5,7},{7,5},{8,10},{10,8},{9,1... | collective-permute-start | bytes 614408 | tf_op jit(solution)/shard_map/ppermute | solution.py:554
  149.8 9.7 %collective-permute-start.3 = (bf16[2,80,640]{2,1,0:T(8,128)(2,1)S(1)}, bf16[2,80,640]{2,1,0:T(8,128)(2,1)S(1)}, u32[]{:S(2)}, u32[]{:S(2)}) collective-permute-start(bf16[2,80,640]{2,1,0:T(8,128)(2,1)S(1)} %shard_map.99), channel_id=1, source_target_pairs={{0,2},{2,0},{1,3},{3,1},{4,6},{6,4},{5,7},{7,5},{8,10},{10,8},{9,1... | collective-permute-start | bytes 614408 | tf_op jit(solution)/shard_map/ppermute | solution.py:555
